TPU v7x, 512 devices: a whole 4x4x16 slice. The times are simulated.
512 devices in a mesh: ta: 4 (over y), gx: 16 (over z), gy: 8 (over x, core).
Axes of the slice: x: 4, y: 4, z: 16, core: 2. Of those that a mesh axis runs over, the one named last changes fastest.
Arguments:
- links: float32 [3, 2, 3, 3, 128, 128, 512], P(None, None, None, None, 'gx', 'gy', 'ta'), parts along dimension 6, may hold values from -1 to 1, as said below
Outputs:
- gauge: float32 [2, 2, 3, 128, 128, 512], P(None, None, None, 'gx', 'gy', 'ta'), parts along dimension 5
- divergence: float32 [8, 128, 128, 512], P(None, 'gx', 'gy', 'ta'), parts along dimension 3
- theta: float32 [12], P('ta'), parts along dimension 0
There are 4 independent parts, one for each index of `ta`. A program takes and returns all parts, laid end to end along the dimension named above; each array names one. Nothing has to cross between parts.
Inputs may be any that keep to these rules, and one draw needn't show every extreme that they name: `links`: each link matrix is special unitary.
All inputs are finite; a program needn't handle non-finite values.
Results may differ from a plain program's by a relative error of at most 0.0003.
Values sent between devices are 32-bit elements; how exact they have to be, the bound alone decides.
No kernel may reach another device: no remote copies, remote signals or barrier semaphores. Data moves between devices by JAX's collectives and lax.ppermute only.
A program may use at most 128 MiB of HBM per device.

v0:
```python
import math

import jax
import jax.numpy as jnp
from jax import lax
from jax.sharding import PartitionSpec as P

LS = 128
NZ = 128
ITERS = 2


STEP_SIZE = 0.08
PEAK_MOMENTUM = 12.0


def shifted(value, axis, steps):
    count = lax.axis_size(axis)
    pairs = [(source, (source + steps) % count) for source in range(count)]
    return lax.ppermute(value, axis, pairs)


def prod_three(left, right):
    return jnp.sum(left[:, :, None] * right[None, :, :], axis=1)


def complex_product(left, right):
    real = prod_three(left[0], right[0]) - prod_three(left[1], right[1])
    imag = prod_three(left[0], right[1]) + prod_three(left[1], right[0])
    return jnp.stack([real, imag])


def dagger(matrix):
    return jnp.stack([jnp.swapaxes(matrix[0], 0, 1), -jnp.swapaxes(matrix[1], 0, 1)])


def algebra(matrix):
    mreal, mimag = (matrix[0], matrix[1])
    middle = (mimag[0, 0] + mimag[1, 1] + mimag[2, 2]) / 3.0
    return jnp.stack(
        [
            mimag[0, 0] - middle,
            mimag[1, 1] - middle,
            (mreal[0, 1] - mreal[1, 0]) / 2.0,
            (mimag[0, 1] + mimag[1, 0]) / 2.0,
            (mreal[0, 2] - mreal[2, 0]) / 2.0,
            (mimag[0, 2] + mimag[2, 0]) / 2.0,
            (mreal[1, 2] - mreal[2, 1]) / 2.0,
            (mimag[1, 2] + mimag[2, 1]) / 2.0,
        ]
    )


def squares(comps):
    third = comps[0] + comps[1]
    rest = jnp.sum(comps[2:] * comps[2:], axis=0)
    return comps[0] * comps[0] + comps[1] * comps[1] + third * third + 2.0 * rest


def to_matrix(comps):
    zero = jnp.zeros_like(comps[0])
    real = jnp.stack(
        [
            jnp.stack([zero, comps[2], comps[4]]),
            jnp.stack([-comps[2], zero, comps[6]]),
            jnp.stack([-comps[4], -comps[6], zero]),
        ]
    )
    imag = jnp.stack(
        [
            jnp.stack([comps[0], comps[3], comps[5]]),
            jnp.stack([comps[3], comps[1], comps[7]]),
            jnp.stack([comps[5], comps[7], -comps[0] - comps[1]]),
        ]
    )
    return jnp.stack([real, imag])


def identity_like(tail):
    eye = jnp.eye(3, dtype=jnp.float32).reshape((3, 3) + (1,) * len(tail))
    real = jnp.broadcast_to(eye, (3, 3) + tuple(tail))
    return jnp.stack([real, jnp.zeros_like(real)])


def normed(row):
    size = jnp.sqrt(jnp.sum(row[0] * row[0] + row[1] * row[1], axis=0))
    return row / size


def unitarize(matrix):
    first = normed(matrix[:, 0])
    second = matrix[:, 1]
    proj_re = jnp.sum(first[0] * second[0] + first[1] * second[1], axis=0)
    proj_im = jnp.sum(first[0] * second[1] - first[1] * second[0], axis=0)
    second = jnp.stack(
        [
            second[0] - (proj_re * first[0] - proj_im * first[1]),
            second[1] - (proj_re * first[1] + proj_im * first[0]),
        ]
    )
    second = normed(second)
    cross_re = []
    cross_im = []
    for entry in range(3):
        after = (entry + 1) % 3
        later = (entry + 2) % 3
        part_re = first[0, after] * second[0, later] - first[1, after] * second[1, later]
        part_re = part_re - (
            first[0, later] * second[0, after] - first[1, later] * second[1, after]
        )
        part_im = first[0, after] * second[1, later] + first[1, after] * second[0, later]
        part_im = part_im - (
            first[0, later] * second[1, after] + first[1, later] * second[0, after]
        )
        cross_re.append(part_re)
        cross_im.append(-part_im)
    third = jnp.stack([jnp.stack(cross_re), jnp.stack(cross_im)])
    return jnp.stack([first, second, third], axis=1)


def exponent(comps):
    step = to_matrix(comps)
    series = identity_like(comps.shape[1:]) + step + 0.5 * complex_product(step, step)
    return unitarize(series)


def tables(length):
    index = jnp.arange(length, dtype=jnp.int32)
    phase = (index[:, None] * index[None, :] % length).astype(jnp.float32) * (
        2.0 * math.pi / length
    )
    return (jnp.cos(phase), jnp.sin(phase))


def along(field, table, axis):
    shape = field.shape
    if axis == len(shape) - 1:
        return jnp.matmul(field, table, precision=lax.Precision.HIGHEST)
    leading = math.prod(shape[:axis])
    trailing = math.prod(shape[axis + 1 :])
    flat = field.reshape(leading, shape[axis], trailing)
    result = jnp.einsum("anr,nk->akr", flat, table, precision=lax.Precision.HIGHEST)
    return result.reshape(shape)


def transform(real, imag, axis, inverse):
    cosine, sine = tables(real.shape[axis])
    if inverse:
        scale = 1.0 / real.shape[axis]
        new_real = (along(real, cosine, axis) - along(imag, sine, axis)) * scale
        new_imag = (along(imag, cosine, axis) + along(real, sine, axis)) * scale
    else:
        new_real = along(real, cosine, axis) + along(imag, sine, axis)
        new_imag = along(imag, cosine, axis) - along(real, sine, axis)
    return (new_real, new_imag)


def filter_table(depth):
    wide_x = lax.axis_size("gx")
    wide_y = lax.axis_size("gy")
    span_y = LS // (wide_x * wide_y)
    place = lax.axis_index("gx") * wide_y + lax.axis_index("gy")
    kx = jnp.arange(LS, dtype=jnp.int32)
    ky = place * span_y + jnp.arange(span_y, dtype=jnp.int32)
    kz = jnp.arange(depth, dtype=jnp.int32)
    sx = jnp.sin(kx.astype(jnp.float32) * (math.pi / LS))
    sy = jnp.sin(ky.astype(jnp.float32) * (math.pi / LS))
    sz = jnp.sin(kz.astype(jnp.float32) * (math.pi / depth))
    total = (
        4.0 * sx[:, None, None] ** 2 + 4.0 * sy[None, :, None] ** 2 + 4.0 * sz[None, None, :] ** 2
    )
    anchor = (
        (kx[:, None, None] == 0) & (ky[None, :, None] == 0) & (kz[None, None, :] == 0)
    ).astype(jnp.float32)
    return PEAK_MOMENTUM / (total + anchor) * (1.0 - anchor)


def accelerate(comps, weights):
    depth = comps.shape[3]
    cosine, sine = tables(depth)
    real = along(comps, cosine, 3)
    imag = -along(comps, sine, 3)
    parts = (
        lax.all_to_all(real, "gy", split_axis=1, concat_axis=2, tiled=True),
        lax.all_to_all(imag, "gy", split_axis=1, concat_axis=2, tiled=True),
    )
    real, imag = transform(parts[0], parts[1], 2, False)
    parts = (
        lax.all_to_all(real, ("gx", "gy"), split_axis=2, concat_axis=1, tiled=True),
        lax.all_to_all(imag, ("gx", "gy"), split_axis=2, concat_axis=1, tiled=True),
    )
    spec_re, spec_im = transform(parts[0], parts[1], 1, False)
    real, imag = transform(spec_re * weights, spec_im * weights, 1, True)
    parts = (
        lax.all_to_all(real, ("gx", "gy"), split_axis=1, concat_axis=2, tiled=True),
        lax.all_to_all(imag, ("gx", "gy"), split_axis=1, concat_axis=2, tiled=True),
    )
    real, imag = transform(parts[0], parts[1], 2, True)
    parts = (
        lax.all_to_all(real, "gy", split_axis=2, concat_axis=1, tiled=True),
        lax.all_to_all(imag, "gy", split_axis=2, concat_axis=1, tiled=True),
    )
    return (along(parts[0], cosine, 3) - along(parts[1], sine, 3)) * (1.0 / depth)


def divergence_of(links):
    first = links[0]
    face_x = shifted(first[:, :, :, -1:], "gx", 1)
    back_x = jnp.concatenate([face_x, first[:, :, :, :-1]], axis=3)
    second = links[1]
    face_y = shifted(second[:, :, :, :, -1:], "gy", 1)
    back_y = jnp.concatenate([face_y, second[:, :, :, :, :-1]], axis=4)
    back_z = jnp.roll(links[2], 1, axis=5)
    total = back_x + back_y + back_z - links[0] - links[1] - links[2]
    return algebra(total)


def per_device(links):
    depth = links.shape[6]
    weights = filter_table(depth)
    gauge = identity_like(links.shape[4:])
    thetas = []
    comps = divergence_of(links)
    for step in range(ITERS + 1):
        if step > 0:
            comps = divergence_of(links)
        local_sum = jnp.sum(squares(comps))
        thetas.append(lax.psum(local_sum, ("gx", "gy")) / (3.0 * LS * LS * NZ))
        if step == ITERS:
            break
        step_comps = STEP_SIZE * accelerate(comps, weights)
        transform_here = exponent(step_comps)
        ahead_x = shifted(transform_here[:, :, :, :1], "gx", -1)
        ahead_y = shifted(transform_here[:, :, :, :, :1], "gy", -1)
        nexts = [
            jnp.concatenate([transform_here[:, :, :, 1:], ahead_x], axis=3),
            jnp.concatenate([transform_here[:, :, :, :, 1:], ahead_y], axis=4),
            jnp.roll(transform_here, -1, axis=5),
        ]
        moved = []
        for mu in range(3):
            moved.append(
                complex_product(complex_product(transform_here, links[mu]), dagger(nexts[mu]))
            )
        links = jnp.stack(moved)
        gauge = complex_product(transform_here, gauge)
    theta = jnp.stack(thetas)
    return (gauge[:, :2], comps, theta)


def solution(mesh):
    in_specs = (P(None, None, None, None, "gx", "gy", "ta"),)
    out_specs = (P(None, None, None, "gx", "gy", "ta"), P(None, "gx", "gy", "ta"), P("ta"))
    return jax.shard_map(
        per_device, mesh=mesh, in_specs=in_specs, out_specs=out_specs, check_vma=False
    )
```

profile of v0, /device:TPU:1, one launch (start us, length us, event | category | flops | bytes accessed | tf_op | source)
XLA Modules:
  0.0 811.1 jit_solution(10462149664327554753)
XLA Ops:
  0.6 2.2 slice_bitcast_fusion
  2.9 4.4 collective-permute-start
  7.3 2.1 collective-permute-start.1
  9.9 2.7 collective-permute-done.1
  12.5 5.9 collective-permute-done
  23.3 5.5 all-to-all-start
  31.5 6.9 all-to-all-done
  38.4 4.9 all-to-all-start.1
  46.8 6.1 all-to-all-done.1
  56.8 11.8 %all-to-all-start.2 = ((f32[8,1,128,128]{3,0,1,2:T(8,128)}), f32[8,1,128,128]{3,0,1,2:T(8,128)}, u32[]{:S(2)}, u32[]{:S(2)}) async-start(f32[8,1,128,128]{3,0,1,2:T(8,128)} %copy.136), calls=%async_computation.2 | async-start | bytes 1048576 | tf_op jit(solution)/shard_map/all_to_all | solution.py:189
  68.6 2.0 fusion.243
  72.6 26.5 %all-to-all-done.2 = f32[8,1,128,128]{3,0,1,2:T(8,128)} async-done(((f32[8,1,128,128]{3,0,1,2:T(8,128)}), f32[8,1,128,128]{3,0,1,2:T(8,128)}, u32[]{:S(2)}, u32[]{:S(2)}) %all-to-all-start.2) | async-done | bytes 524320 | tf_op jit(solution)/shard_map/all_to_all | solution.py:189
  99.1 10.2 %all-to-all-start.3 = ((f32[8,1,128,128]{3,0,1,2:T(8,128)}), f32[8,1,128,128]{3,0,1,2:T(8,128)}, u32[]{:S(2)}, u32[]{:S(2)}) async-start(f32[8,1,128,128]{3,0,1,2:T(8,128)} %copy.141), calls=%async_computation.3 | async-start | bytes 1048576 | tf_op jit(solution)/shard_map/all_to_all | solution.py:190
  110.2 2.7 fusion.98
  112.9 26.7 %all-to-all-done.3 = f32[8,1,128,128]{3,0,1,2:T(8,128)} async-done(((f32[8,1,128,128]{3,0,1,2:T(8,128)}), f32[8,1,128,128]{3,0,1,2:T(8,128)}, u32[]{:S(2)}, u32[]{:S(2)}) %all-to-all-start.3) | async-done | bytes 524320 | tf_op jit(solution)/shard_map/all_to_all | solution.py:190
  139.6 2.1 fusion.27
  142.6 1.9 fusion.94
  144.5 1.9 fusion.25
  148.5 9.6 %all-to-all-start.4 = ((f32[8,128,1,128]{3,0,2,1:T(8,128)}), f32[8,128,1,128]{3,0,2,1:T(8,128)}, u32[]{:S(2)}, u32[]{:S(2)}) async-start(f32[8,128,1,128]{3,0,2,1:T(8,128)} %copy.148), calls=%async_computation.4 | async-start | bytes 1048576 | tf_op jit(solution)/shard_map/all_to_all | solution.py:195
  158.0 1.9 fusion.240
  162.0 26.5 %all-to-all-done.4 = f32[8,128,1,128]{3,0,2,1:T(8,128)} async-done(((f32[8,128,1,128]{3,0,2,1:T(8,128)}), f32[8,128,1,128]{3,0,2,1:T(8,128)}, u32[]{:S(2)}, u32[]{:S(2)}) %all-to-all-start.4) | async-done | bytes 524320 | tf_op jit(solution)/shard_map/all_to_all | solution.py:195
  188.5 9.9 %all-to-all-start.5 = ((f32[8,128,1,128]{3,0,2,1:T(8,128)}), f32[8,128,1,128]{3,0,2,1:T(8,128)}, u32[]{:S(2)}, u32[]{:S(2)}) async-start(f32[8,128,1,128]{3,0,2,1:T(8,128)} %copy.153), calls=%async_computation.5 | async-start | bytes 1048576 | tf_op jit(solution)/shard_map/all_to_all | solution.py:196
  198.4 2.7 fusion.92
  201.2 27.6 %all-to-all-done.5 = f32[8,128,1,128]{3,0,2,1:T(8,128)} async-done(((f32[8,128,1,128]{3,0,2,1:T(8,128)}), f32[8,128,1,128]{3,0,2,1:T(8,128)}, u32[]{:S(2)}, u32[]{:S(2)}) %all-to-all-start.5) | async-done | bytes 524320 | tf_op jit(solution)/shard_map/all_to_all | solution.py:196
  228.7 2.1 fusion.19
  231.9 6.6 all-to-all-start.6
  238.6 1.9 fusion.88
  240.5 1.9 fusion.17
  243.5 4.6 all-to-all-done.6
  248.1 4.9 all-to-all-start.7
  256.8 5.8 all-to-all-done.7
  269.8 2.8 collective-permute-start.2
  274.6 4.2 multiply_reduce_fusion.29
  282.5 2.7 collective-permute-start.3
  288.1 2.2 collective-permute-done.3
  295.2 5.6 all-to-all-start.8
  303.5 6.9 all-to-all-done.8
  310.4 4.9 all-to-all-start.9
  318.8 6.1 all-to-all-done.9
  328.8 8.7 %all-to-all-start.10 = ((f32[8,1,128,128]{3,0,1,2:T(8,128)}), f32[8,1,128,128]{3,0,1,2:T(8,128)}, u32[]{:S(2)}, u32[]{:S(2)}) async-start(f32[8,1,128,128]{3,0,1,2:T(8,128)} %copy.176), calls=%async_computation.10 | async-start | bytes 1048576 | tf_op jit(solution)/shard_map/all_to_all | solution.py:189
  337.5 1.9 fusion.237
  341.5 26.5 %all-to-all-done.10 = f32[8,1,128,128]{3,0,1,2:T(8,128)} async-done(((f32[8,1,128,128]{3,0,1,2:T(8,128)}), f32[8,1,128,128]{3,0,1,2:T(8,128)}, u32[]{:S(2)}, u32[]{:S(2)}) %all-to-all-start.10) | async-done | bytes 524320 | tf_op jit(solution)/shard_map/all_to_all | solution.py:189
  368.0 9.6 %all-to-all-start.11 = ((f32[8,1,128,128]{3,0,1,2:T(8,128)}), f32[8,1,128,128]{3,0,1,2:T(8,128)}, u32[]{:S(2)}, u32[]{:S(2)}) async-start(f32[8,1,128,128]{3,0,1,2:T(8,128)} %copy.181), calls=%async_computation.11 | async-start | bytes 1048576 | tf_op jit(solution)/shard_map/all_to_all | solution.py:190
  377.6 2.7 fusion.86
  380.3 27.7 %all-to-all-done.11 = f32[8,1,128,128]{3,0,1,2:T(8,128)} async-done(((f32[8,1,128,128]{3,0,1,2:T(8,128)}), f32[8,1,128,128]{3,0,1,2:T(8,128)}, u32[]{:S(2)}, u32[]{:S(2)}) %all-to-all-start.11) | async-done | bytes 524320 | tf_op jit(solution)/shard_map/all_to_all | solution.py:190
  408.0 2.1 fusion.12
  413.0 1.9 fusion.10
  416.9 9.6 %all-to-all-start.12 = ((f32[8,128,1,128]{3,0,2,1:T(8,128)}), f32[8,128,1,128]{3,0,2,1:T(8,128)}, u32[]{:S(2)}, u32[]{:S(2)}) async-start(f32[8,128,1,128]{3,0,2,1:T(8,128)} %copy.188), calls=%async_computation.12 | async-start | bytes 1048576 | tf_op jit(solution)/shard_map/all_to_all | solution.py:195
  426.5 1.9 fusion.234
  430.5 26.5 %all-to-all-done.12 = f32[8,128,1,128]{3,0,2,1:T(8,128)} async-done(((f32[8,128,1,128]{3,0,2,1:T(8,128)}), f32[8,128,1,128]{3,0,2,1:T(8,128)}, u32[]{:S(2)}, u32[]{:S(2)}) %all-to-all-start.12) | async-done | bytes 524320 | tf_op jit(solution)/shard_map/all_to_all | solution.py:195
  457.0 9.6 %all-to-all-start.13 = ((f32[8,128,1,128]{3,0,2,1:T(8,128)}), f32[8,128,1,128]{3,0,2,1:T(8,128)}, u32[]{:S(2)}, u32[]{:S(2)}) async-start(f32[8,128,1,128]{3,0,2,1:T(8,128)} %copy.193), calls=%async_computation.13 | async-start | bytes 1048576 | tf_op jit(solution)/shard_map/all_to_all | solution.py:196
  470.1 1.9 fusion.80
  472.0 25.0 %all-to-all-done.13 = f32[8,128,1,128]{3,0,2,1:T(8,128)} async-done(((f32[8,128,1,128]{3,0,2,1:T(8,128)}), f32[8,128,1,128]{3,0,2,1:T(8,128)}, u32[]{:S(2)}, u32[]{:S(2)}) %all-to-all-start.13) | async-done | bytes 524320 | tf_op jit(solution)/shard_map/all_to_all | solution.py:196
  497.0 1.9 fusion.4
  500.1 6.6 all-to-all-start.14
  510.4 1.9 fusion.2
  513.5 2.8 all-to-all-done.14
  516.3 4.5 all-to-all-start.15
  526.2 4.0 all-to-all-done.15
  537.7 2.6 collective-permute-start.6
  541.7 3.7 multiply_reduce_fusion.19
  549.3 2.7 collective-permute-start.7
  554.9 2.2 collective-permute-done.7
  560.0 248.4 %all-reduce.1 = (f32[]{:T(128)}, f32[]{:T(128)}, f32[]{:T(128)}) all-reduce(f32[]{:T(128)} %add_reduce_fusion, f32[]{:T(128)} %add_reduce_fusion.1, f32[]{:T(128)} %add_reduce_fusion.2), channel_id=1, replica_groups=mesh['ta'=4,'gx'=16,'gy'=8] {'gx','gy'}, use_global_device_ids=true, to_apply=%region_80.81 | all-reduce | flops 3 | bytes 24 | tf_op jit(solution)/shard_map/psum | solution.py:228
  (306 shorter events, 101.4 us)
Async XLA Ops:
  2.9 15.5 %collective-permute-start = (f32[2,3,3,1,16,128]{5,4,3,2,1,0:T(8,128)S(1)}, f32[2,3,3,1,16,128]{5,4,3,2,1,0:T(8,128)S(1)}, u32[]{:S(2)}, u32[]{:S(2)}) collective-permute-start(f32[2,3,3,1,16,128]{5,4,3,2,1,0:T(8,128)S(1)} %slice.845), channel_id=1, source_target_pairs={{0,8},{8,16},{16,24},{24,32},{32,40},{40,48},{48,56},{56,64},{64,7... | collective-permute-start | bytes 442376 | tf_op jit(solution)/shard_map/ppermute | solution.py:20
  7.3 5.2 collective-permute-start.1
  9.4 9.0 %copy-start = (f32[3,2,3,3,8,16,128]{6,5,4,3,2,1,0:T(8,128)S(1)}, f32[3,2,3,3,8,16,128]{6,5,4,3,2,1,0:T(8,128)}, u32[]{:S(2)}) copy-start(f32[3,2,3,3,8,16,128]{6,5,4,3,2,1,0:T(8,128)} %param.1) | copy-start | bytes 10616836
  19.3 0.8 copy-start.5
  20.9 0.8 copy-start.21
  23.3 15.1 %all-to-all-start = ((f32[8,8,16,128]{3,2,0,1:T(8,128)}), f32[8,8,16,128]{3,2,0,1:T(8,128)}, u32[]{:S(2)}, u32[]{:S(2)}) async-start(f32[8,8,16,128]{3,2,0,1:T(8,128)} %fusion.102), calls=%async_computation | async-start | bytes 1048576 | tf_op jit(solution)/shard_map/all_to_all | solution.py:184
  38.4 14.5 %all-to-all-start.1 = ((f32[8,8,16,128]{3,2,0,1:T(8,128)}), f32[8,8,16,128]{3,2,0,1:T(8,128)}, u32[]{:S(2)}, u32[]{:S(2)}) async-start(f32[8,8,16,128]{3,2,0,1:T(8,128)} %copy.133), calls=%async_computation.1 | async-start | bytes 1048576 | tf_op jit(solution)/shard_map/all_to_all | solution.py:185
  44.4 0.8 copy-start.15
  52.9 1.9 copy-start.33
  54.0 0.8 copy-start.19
  56.8 42.3 %all-to-all-start.2 = ((f32[8,1,128,128]{3,0,1,2:T(8,128)}), f32[8,1,128,128]{3,0,1,2:T(8,128)}, u32[]{:S(2)}, u32[]{:S(2)}) async-start(f32[8,1,128,128]{3,0,1,2:T(8,128)} %copy.136), calls=%async_computation.2 | async-start | bytes 1048576 | tf_op jit(solution)/shard_map/all_to_all | solution.py:189
  68.6 2.0 copy-start.16
  99.1 40.5 %all-to-all-start.3 = ((f32[8,1,128,128]{3,0,1,2:T(8,128)}), f32[8,1,128,128]{3,0,1,2:T(8,128)}, u32[]{:S(2)}, u32[]{:S(2)}) async-start(f32[8,1,128,128]{3,0,1,2:T(8,128)} %copy.141), calls=%async_computation.3 | async-start | bytes 1048576 | tf_op jit(solution)/shard_map/all_to_all | solution.py:190
  141.7 4.8 copy-start.11
  141.7 2.8 copy-start.35
  146.5 0.9 copy-start.14
  148.5 40.0 %all-to-all-start.4 = ((f32[8,128,1,128]{3,0,2,1:T(8,128)}), f32[8,128,1,128]{3,0,2,1:T(8,128)}, u32[]{:S(2)}, u32[]{:S(2)}) async-start(f32[8,128,1,128]{3,0,2,1:T(8,128)} %copy.148), calls=%async_computation.4 | async-start | bytes 1048576 | tf_op jit(solution)/shard_map/all_to_all | solution.py:195
  158.0 2.0 copy-start.12
  188.5 40.2 %all-to-all-start.5 = ((f32[8,128,1,128]{3,0,2,1:T(8,128)}), f32[8,128,1,128]{3,0,2,1:T(8,128)}, u32[]{:S(2)}, u32[]{:S(2)}) async-start(f32[8,128,1,128]{3,0,2,1:T(8,128)} %copy.153), calls=%async_computation.5 | async-start | bytes 1048576 | tf_op jit(solution)/shard_map/all_to_all | solution.py:196
  231.9 16.2 %all-to-all-start.6 = ((f32[8,1,128,128]{3,0,1,2:T(8,128)}), f32[8,1,128,128]{3,0,1,2:T(8,128)}, u32[]{:S(2)}, u32[]{:S(2)}) async-start(f32[8,1,128,128]{3,0,1,2:T(8,128)} %copy.156), calls=%async_computation.6 | async-start | bytes 1048576 | tf_op jit(solution)/shard_map/all_to_all | solution.py:200
  248.1 14.5 %all-to-all-start.7 = ((f32[8,1,128,128]{3,0,1,2:T(8,128)}), f32[8,1,128,128]{3,0,1,2:T(8,128)}, u32[]{:S(2)}, u32[]{:S(2)}) async-start(f32[8,1,128,128]{3,0,1,2:T(8,128)} %copy.160), calls=%async_computation.7 | async-start | bytes 1048576 | tf_op jit(solution)/shard_map/all_to_all | solution.py:201
  266.5 0.8 copy-start.7
  268.9 11.6 %collective-permute-start.4 = (f32[2,3,3,8,1,128]{5,4,3,2,0,1:T(1,128)S(1)}, f32[2,3,3,8,1,128]{5,4,3,2,0,1:T(1,128)S(1)}, u32[]{:S(2)}, u32[]{:S(2)}) collective-permute-start(f32[2,3,3,8,1,128]{5,4,3,2,0,1:T(1,128)S(1)} %pad_maximum_fusion.26), channel_id=1, source_target_pairs={{0,7},{1,0},{2,1},{3,2},{4,3},{5,4},{6,5},{7,6},{8,15},{9,8},{10,9... | collective-permute-start | bytes 221192 | tf_op jit(solution)/shard_map/ppermute | solution.py:20
  269.8 11.7 %collective-permute-start.2 = (f32[2,3,3,1,16,128]{5,4,3,2,0,1:T(8,128)S(1)}, f32[2,3,3,1,16,128]{5,4,3,2,0,1:T(8,128)S(1)}, u32[]{:S(2)}, u32[]{:S(2)}) collective-permute-start(f32[2,3,3,1,16,128]{5,4,3,2,0,1:T(8,128)S(1)} %slice.898), channel_id=1, source_target_pairs={{0,120},{8,0},{16,8},{24,16},{32,24},{40,32},{48,40},{56,48},{64,5... | collective-permute-start | bytes 442376 | tf_op jit(solution)/shard_map/ppermute | solution.py:20
  272.6 1.1 copy-start.23
  272.6 1.2 copy-start.24
  272.7 1.4 copy-start.25
  272.7 1.6 copy-start.26
  272.7 1.7 copy-start.27
  272.7 1.9 copy-start.28
  282.4 8.0 copy-start.1
  282.5 7.9 copy-start.3
  282.5 7.8 collective-permute-start.3
  285.3 2.9 collective-permute-start.5
  291.2 0.8 copy-start.6
  295.2 15.2 %all-to-all-start.8 = ((f32[8,8,16,128]{3,2,0,1:T(8,128)}), f32[8,8,16,128]{3,2,0,1:T(8,128)}, u32[]{:S(2)}, u32[]{:S(2)}) async-start(f32[8,8,16,128]{3,2,0,1:T(8,128)} %fusion.100), calls=%async_computation.8 | async-start | bytes 1048576 | tf_op jit(solution)/shard_map/all_to_all | solution.py:184
  310.4 14.5 %all-to-all-start.9 = ((f32[8,8,16,128]{3,2,0,1:T(8,128)}), f32[8,8,16,128]{3,2,0,1:T(8,128)}, u32[]{:S(2)}, u32[]{:S(2)}) async-start(f32[8,8,16,128]{3,2,0,1:T(8,128)} %copy.173), calls=%async_computation.9 | async-start | bytes 1048576 | tf_op jit(solution)/shard_map/all_to_all | solution.py:185
  316.4 0.8 copy-start.17
  324.9 2.0 copy-start.34
  326.0 0.8 copy-start.20
  328.8 39.2 %all-to-all-start.10 = ((f32[8,1,128,128]{3,0,1,2:T(8,128)}), f32[8,1,128,128]{3,0,1,2:T(8,128)}, u32[]{:S(2)}, u32[]{:S(2)}) async-start(f32[8,1,128,128]{3,0,1,2:T(8,128)} %copy.176), calls=%async_computation.10 | async-start | bytes 1048576 | tf_op jit(solution)/shard_map/all_to_all | solution.py:189
  337.5 2.0 copy-start.18
  368.0 40.0 %all-to-all-start.11 = ((f32[8,1,128,128]{3,0,1,2:T(8,128)}), f32[8,1,128,128]{3,0,1,2:T(8,128)}, u32[]{:S(2)}, u32[]{:S(2)}) async-start(f32[8,1,128,128]{3,0,1,2:T(8,128)} %copy.181), calls=%async_computation.11 | async-start | bytes 1048576 | tf_op jit(solution)/shard_map/all_to_all | solution.py:190
  410.2 4.8 copy-start.9
  410.2 2.8 copy-start.36
  414.9 0.9 copy-start.13
  416.9 40.0 %all-to-all-start.12 = ((f32[8,128,1,128]{3,0,2,1:T(8,128)}), f32[8,128,1,128]{3,0,2,1:T(8,128)}, u32[]{:S(2)}, u32[]{:S(2)}) async-start(f32[8,128,1,128]{3,0,2,1:T(8,128)} %copy.188), calls=%async_computation.12 | async-start | bytes 1048576 | tf_op jit(solution)/shard_map/all_to_all | solution.py:195
  426.5 2.0 copy-start.10
  457.0 40.0 %all-to-all-start.13 = ((f32[8,128,1,128]{3,0,2,1:T(8,128)}), f32[8,128,1,128]{3,0,2,1:T(8,128)}, u32[]{:S(2)}, u32[]{:S(2)}) async-start(f32[8,128,1,128]{3,0,2,1:T(8,128)} %copy.193), calls=%async_computation.13 | async-start | bytes 1048576 | tf_op jit(solution)/shard_map/all_to_all | solution.py:196
  466.5 3.5 copy-start.30
  498.9 7.8 copy-start.29
  500.1 16.2 %all-to-all-start.14 = ((f32[8,1,128,128]{3,0,1,2:T(8,128)}), f32[8,1,128,128]{3,0,1,2:T(8,128)}, u32[]{:S(2)}, u32[]{:S(2)}) async-start(f32[8,1,128,128]{3,0,1,2:T(8,128)} %copy.196), calls=%async_computation.14 | async-start | bytes 1048576 | tf_op jit(solution)/shard_map/all_to_all | solution.py:200
  516.3 14.0 %all-to-all-start.15 = ((f32[8,1,128,128]{3,0,1,2:T(8,128)}), f32[8,1,128,128]{3,0,1,2:T(8,128)S(1)}, u32[]{:S(2)}, u32[]{:S(2)}) async-start(f32[8,1,128,128]{3,0,1,2:T(8,128)} %copy.200), calls=%async_computation.15 | async-start | bytes 1048576 | tf_op jit(solution)/shard_map/all_to_all | solution.py:201
  530.3 1.0 copy-start.32
  532.2 0.8 copy-start.38
  533.8 1.1 copy-start.8
  536.8 10.6 %collective-permute-start.8 = (f32[2,3,3,8,1,128]{5,4,3,2,0,1:T(1,128)S(1)}, f32[2,3,3,8,1,128]{5,4,3,2,0,1:T(1,128)S(1)}, u32[]{:S(2)}, u32[]{:S(2)}) collective-permute-start(f32[2,3,3,8,1,128]{5,4,3,2,0,1:T(1,128)S(1)} %pad_maximum_fusion.25), channel_id=1, source_target_pairs={{0,7},{1,0},{2,1},{3,2},{4,3},{5,4},{6,5},{7,6},{8,15},{9,8},{10,9... | collective-permute-start | bytes 221192 | tf_op jit(solution)/shard_map/ppermute | solution.py:20
  537.7 10.7 %collective-permute-start.6 = (f32[2,3,3,1,16,128]{5,4,3,2,0,1:T(8,128)S(1)}, f32[2,3,3,1,16,128]{5,4,3,2,0,1:T(8,128)S(1)}, u32[]{:S(2)}, u32[]{:S(2)}) collective-permute-start(f32[2,3,3,1,16,128]{5,4,3,2,0,1:T(8,128)S(1)} %slice.967), channel_id=1, source_target_pairs={{0,120},{8,0},{16,8},{24,16},{32,24},{40,32},{48,40},{56,48},{64,5... | collective-permute-start | bytes 442376 | tf_op jit(solution)/shard_map/ppermute | solution.py:20
  540.3 1.1 copy-start.2
  540.3 1.2 copy-start.4
  540.3 1.4 copy-start.31
  549.3 7.8 collective-permute-start.7
  552.1 2.8 collective-permute-start.9
  558.3 1.7 copy-start.41
  (4 other events, 2.9 us)
where the time goes:
time: 822 us; the launch traced here: 811 us
  waiting for transfers between devices  272 us (33%)
  blocking collectives  248 us (30%)
  starting transfers between devices  144 us (18%)
  matrix products  64.5 us (8%)
  local copies, waits for them, and re-layouts  42.9 us (5%)
  other arithmetic  34.5 us (4%)
    psum x1, blocking collectives, per_device(): thetas.append(lax.psum(local_sum, ('gx', 'gy')) / (3.0 * LS * LS * NZ))  248 us
    all_to_all x2, waiting for transfers between devices, accelerate(): lax.all_to_all(imag, ('gx', 'gy'), split_axis=2, concat_axis=1, tiled=True)  54.4 us
    dot_general x32, matrix products, along(): jnp.einsum('anr,nk->akr', flat, table, precision=lax.Precision.HIGHEST)  53.5 us
    all_to_all x2, waiting for transfers between devices, accelerate(): lax.all_to_all(real, ('gx', 'gy'), split_axis=2, concat_axis=1, tiled=True)  53 us
    all_to_all x2, waiting for transfers between devices, accelerate(): lax.all_to_all(real, ('gx', 'gy'), split_axis=1, concat_axis=2, tiled=True)  53 us
    all_to_all x2, waiting for transfers between devices, accelerate(): lax.all_to_all(imag, ('gx', 'gy'), split_axis=1, concat_axis=2, tiled=True)  52.6 us
    ppermute x10, starting transfers between devices, shifted(): return lax.ppermute(value, axis, pairs)  21.8 us
    all_to_all x2, starting transfers between devices, accelerate(): lax.all_to_all(real, ('gx', 'gy'), split_axis=2, concat_axis=1, tiled=True)  20.5 us
  transfers between devices with their start and end apart: 26, of which 22 were waited for; matrix products, arithmetic and copies ran while one was open for 9% of the time, Pallas kernels for 0%

commit v1 on v0

v1 whole, which is shorter than its diff:
```python
import math

import jax
import jax.numpy as jnp
import numpy as np
from jax import lax
from jax.experimental import pallas as pl
from jax.experimental.pallas import tpu as pltpu
from jax.sharding import PartitionSpec as P

LS = 128
NZ = 128
STEP_SIZE = 0.08
PEAK_MOMENTUM = 12.0
NGX = 16
NGY = 8
F32 = jnp.float32
BF16 = jnp.bfloat16
MEGA = 1024 * 1024


def real_basis(length):
    site = np.arange(length)[:, None]
    freq = np.arange(length)
    freq = np.where(freq <= length // 2, freq, freq - length // 2)
    phase = 2.0 * np.pi * ((site * freq[None, :]) % length) / length
    index = np.arange(length)[None, :]
    basis = np.where(index <= length // 2, np.cos(phase), np.sin(phase)) * np.sqrt(2.0 / length)
    basis[:, 0] = 1.0 / np.sqrt(length)
    basis[:, length // 2] = np.cos(np.pi * np.arange(length)) / np.sqrt(length)
    return basis, freq


def halves(table):
    high = table.astype(np.float32).astype(jnp.bfloat16)
    low = (table - high.astype(np.float64)).astype(np.float32).astype(jnp.bfloat16)
    return high, low


def right_table(table):
    high, low = halves(table)
    return np.concatenate([high, high, low], axis=0)


def left_table(table):
    high, low = halves(table)
    return np.concatenate([high, high, low], axis=1)


def ring_table(squares_y, squares_z):
    mass = squares_y[:, None] + squares_z[None, :]
    weight = np.zeros_like(mass)
    product = np.ones_like(mass)
    for _ in range(7):
        weight = 1.0 / (2.0 + mass - weight)
        product = product * weight
    diag = 2.0 + mass - 2.0 * weight
    out = np.zeros((9,) + mass.shape)
    for mode in range(16):
        eigen = diag - 2.0 * product * math.cos(2.0 * math.pi * mode / 16)
        if mode == 0:
            eigen[0, 0] = np.inf
        for dist in range(9):
            out[dist] += math.cos(2.0 * math.pi * mode * dist / 16) / eigen / 16.0
    return out


BASIS, FREQ = real_basis(128)
SQUARES = 4.0 * np.sin(np.pi * FREQ / 128.0) ** 2
Z_FORWARD = right_table(BASIS)
Z_BACK = right_table(BASIS.T)
Y_FORWARD = left_table(BASIS.T * (STEP_SIZE * PEAK_MOMENTUM))
Y_BACK = left_table(BASIS)
RING = ring_table(SQUARES, SQUARES).astype(np.float32)


def three_lanes(value):
    high = value.astype(BF16)
    low = (value - high.astype(F32)).astype(BF16)
    return jnp.concatenate([high, low, high], axis=1)


def three_rows(value):
    high = value.astype(BF16)
    low = (value - high.astype(F32)).astype(BF16)
    return jnp.concatenate([high, low, high], axis=0)


def swap_blocks(tiles):
    tiles = list(tiles)
    group = lax.broadcasted_iota(jnp.int32, tiles[0].shape, 1) // 16
    for bit in (1, 2, 4):
        upper = (group & bit) != 0
        for i in range(8):
            if i & bit:
                continue
            low, high = tiles[i], tiles[i | bit]
            tiles[i] = jnp.where(upper, pltpu.roll(high, 16 * bit, 1), low)
            tiles[i | bit] = jnp.where(upper, high, pltpu.roll(low, 128 - 16 * bit, 1))
    return tiles


def algebra(mreal, mimag):
    i00, i11, i22 = mimag(0, 0), mimag(1, 1), mimag(2, 2)
    middle = (i00 + i11 + i22) * (1.0 / 3.0)
    return [
        i00 - middle,
        i11 - middle,
        (mreal(0, 1) - mreal(1, 0)) * 0.5,
        (mimag(0, 1) + mimag(1, 0)) * 0.5,
        (mreal(0, 2) - mreal(2, 0)) * 0.5,
        (mimag(0, 2) + mimag(2, 0)) * 0.5,
        (mreal(1, 2) - mreal(2, 1)) * 0.5,
        (mimag(1, 2) + mimag(2, 1)) * 0.5,
    ]


def squares(c):
    third = c[0] + c[1]
    rest = c[2] * c[2] + c[3] * c[3] + c[4] * c[4] + c[5] * c[5] + c[6] * c[6] + c[7] * c[7]
    return c[0] * c[0] + c[1] * c[1] + third * third + 2.0 * rest


def entry(row, col):
    return row * 3 + col


def cross_row(first_re, first_im, second_re, second_im):
    out_re, out_im = [], []
    for k in range(3):
        a, b = (k + 1) % 3, (k + 2) % 3
        out_re.append(
            first_re[a] * second_re[b]
            - first_im[a] * second_im[b]
            - first_re[b] * second_re[a]
            + first_im[b] * second_im[a]
        )
        out_im.append(
            first_re[b] * second_im[a]
            + first_im[b] * second_re[a]
            - first_re[a] * second_im[b]
            - first_im[a] * second_re[b]
        )
    return out_re, out_im


def exponent_rows(c):
    c0, c1, c2, c3, c4, c5, c6, c7 = c
    n01 = c2 * c2 + c3 * c3
    n02 = c4 * c4 + c5 * c5
    n12 = c6 * c6 + c7 * c7
    s00 = 1.0 - 0.5 * (c0 * c0 + n01 + n02)
    s11 = 1.0 - 0.5 * (c1 * c1 + n01 + n12)
    d01 = c0 + c1
    p01r = -(d01 * c3) - (c4 * c6 + c5 * c7)
    p01i = d01 * c2 - (c5 * c6 - c4 * c7)
    p02r = c1 * c5 + (c2 * c6 - c3 * c7)
    p02i = -(c1 * c4) + (c2 * c7 + c3 * c6)
    p12r = -(c2 * c4 + c3 * c5) + c0 * c7
    p12i = -(c2 * c5 - c3 * c4) - c0 * c6
    r0 = [s00, c2 + 0.5 * p01r, c4 + 0.5 * p02r]
    i0 = [c0, c3 + 0.5 * p01i, c5 + 0.5 * p02i]
    r1 = [-c2 + 0.5 * p01r, s11, c6 + 0.5 * p12r]
    i1 = [c3 - 0.5 * p01i, c1, c7 + 0.5 * p12i]
    size = sum(r0[k] * r0[k] + i0[k] * i0[k] for k in range(3))
    scale = 1.0 / jnp.sqrt(size)
    r0 = [v * scale for v in r0]
    i0 = [v * scale for v in i0]
    pr = sum(r0[k] * r1[k] + i0[k] * i1[k] for k in range(3))
    pi = sum(r0[k] * i1[k] - i0[k] * r1[k] for k in range(3))
    r1, i1 = (
        [r1[k] - (pr * r0[k] - pi * i0[k]) for k in range(3)],
        [i1[k] - (pr * i0[k] + pi * r0[k]) for k in range(3)],
    )
    size = sum(r1[k] * r1[k] + i1[k] * i1[k] for k in range(3))
    scale = 1.0 / jnp.sqrt(size)
    r1 = [v * scale for v in r1]
    i1 = [v * scale for v in i1]
    return r0 + r1, i0 + i1


def full_matrix(re6, im6):
    re3, im3 = cross_row(re6[:3], im6[:3], re6[3:], im6[3:])
    return list(re6) + re3 + list(im6) + im3


def times_rows(gre, gim, hre, him):
    out_re, out_im = [], []
    for i in range(2):
        for j in range(3):
            acc_re = acc_im = None
            for k in range(3):
                ar, ai = gre[entry(i, k)], gim[entry(i, k)]
                br, bi = hre[entry(k, j)], him[entry(k, j)]
                pr, pi = ar * br - ai * bi, ar * bi + ai * br
                acc_re = pr if acc_re is None else acc_re + pr
                acc_im = pi if acc_im is None else acc_im + pi
            out_re.append(acc_re)
            out_im.append(acc_im)
    return out_re, out_im


def moved_algebra(g, link, ahead):
    gre, gim = g[:9], g[9:]
    are, aim = ahead[:9], ahead[9:]
    vre, vim = [None] * 9, [None] * 9
    for i in range(3):
        ur = [link(0, i, k) for k in range(3)]
        ui = [link(1, i, k) for k in range(3)]
        for j in range(3):
            br = [are[entry(j, k)] for k in range(3)]
            bi = [aim[entry(j, k)] for k in range(3)]
            vre[entry(i, j)] = (ur[0] * br[0] + ui[0] * bi[0]) + (
                (ur[1] * br[1] + ui[1] * bi[1]) + (ur[2] * br[2] + ui[2] * bi[2])
            )
            vim[entry(i, j)] = (ui[0] * br[0] - ur[0] * bi[0]) + (
                (ui[1] * br[1] - ur[1] * bi[1]) + (ui[2] * br[2] - ur[2] * bi[2])
            )

    def mreal(i, j):
        return sum(
            gre[entry(i, k)] * vre[entry(k, j)] - gim[entry(i, k)] * vim[entry(k, j)]
            for k in range(3)
        )

    def mimag(i, j):
        return sum(
            gre[entry(i, k)] * vim[entry(k, j)] + gim[entry(i, k)] * vre[entry(k, j)]
            for k in range(3)
        )

    return algebra(mreal, mimag)


def first_kernel(links, face_x, face_y, table, out, theta, prev, rows_in, spectrum):
    step = pl.program_id(0)

    @pl.when(step == 0)
    def _():
        prev[...] = face_x[...]
        theta[...] = jnp.zeros_like(theta)

    def of(mu):
        return algebra(
            lambda i, j: links[mu, 0, i, j, 0], lambda i, j: links[mu, 1, i, j, 0]
        )

    top = lax.broadcasted_iota(jnp.int32, (16, 128), 0) == 0
    ax, ay, az = of(0), of(1), of(2)
    comps = []
    for c in range(8):
        edge = face_y[c, pl.ds(step, 1), :]
        back_y = jnp.where(top, edge, pltpu.roll(ay[c], 1, 0))
        back_z = pltpu.roll(az[c], 1, 1)
        comps.append((prev[c] + back_y + back_z) - ax[c] - ay[c] - az[c])
        prev[c] = ax[c]
        rows_in[pl.ds(16 * c, 16), :] = comps[c]
    sq = squares(comps)
    theta[...] += sq[:8] + sq[8:]
    spectrum[step] = jnp.dot(
        three_lanes(rows_in[...]), table[...], preferred_element_type=F32
    )

    @pl.when(step == 7)
    def _():
        scatter_blocks(spectrum, out)


def scatter_blocks(spectrum, out):
    for c in range(8):
        tiles = swap_blocks([spectrum[x, pl.ds(16 * c, 16), :] for x in range(8)])
        for d in range(8):
            out[d, c] = tiles[d]


def weights_of(mass):
    base = mass + 2.0
    weights = [None, 1.0 / base]
    for _ in range(6):
        weights.append(1.0 / (base - weights[-1]))
    return weights


def forward_kernel(recv, table, mass, spectrum, moments, work):
    for c in range(8):
        block = recv[:, c].reshape(128, 128)
        work[c] = jnp.dot(table[...], three_rows(block), preferred_element_type=F32)
    for group in range(8):
        rows = pl.ds(16 * group, 16)
        tiles = swap_blocks([work[c, rows, :] for c in range(8)])
        for x in range(8):
            spectrum[x, rows, :] = tiles[x]
        w = weights_of(mass[rows, :])
        low = w[1] * tiles[7]
        for k in range(6, 0, -1):
            low = w[8 - k] * (tiles[k] + low)
        low = low + tiles[0]
        high = w[1] * tiles[1]
        for k in range(2, 8):
            high = w[k] * (tiles[k] + high)
        for half in range(2):
            part = slice(8 * half, 8 * half + 8)
            moments[2 * group + half, 0] = low[part]
            moments[2 * group + half, 1] = high[part]
            moments[2 * group + half, 2] = jnp.zeros((8, 128), F32)
        if group == 0:
            total = 3.5 * (tiles[1] + tiles[7]) + 6.0 * (tiles[2] + tiles[6])
            total = total + 7.5 * (tiles[3] + tiles[5]) + 8.0 * tiles[4]
            moments[0, 2] = total[:8]


def ring_kernel(recv, ring, zero, out):
    rhs = [recv[j, 0] + recv[(j + 15) % 16, 1] for j in range(16)]
    shift = recv[0, 2]
    for j in range(1, 16):
        shift = shift + recv[j, 2]
    shift = shift * zero[...]
    coef = [ring[n] for n in range(9)]
    for j in range(16):
        acc = coef[0] * rhs[j] + coef[8] * rhs[(j + 8) % 16]
        for n in range(1, 8):
            acc = acc + coef[n] * (rhs[(j + n) % 16] + rhs[(j - n) % 16])
        acc = acc + shift
        out[j, 0] = acc
        out[(j + 15) % 16, 1] = acc


def back_kernel(spectrum, faces, table, mass, out, work, edges, done):
    for group in range(8):
        rows = pl.ds(16 * group, 16)
        tiles = [spectrum[x, rows, :] for x in range(8)]
        near = jnp.concatenate([faces[2 * group, 0], faces[2 * group + 1, 0]], axis=0)
        far = jnp.concatenate([faces[2 * group, 1], faces[2 * group + 1, 1]], axis=0)
        m = mass[rows, :]
        w = weights_of(m)
        partial = [near]
        for k in range(1, 8):
            partial.append(w[k] * (tiles[k] + partial[-1]))
        value = [None] * 8
        value[0] = near
        last = far
        for k in range(7, 0, -1):
            last = partial[k] + w[k] * last
            value[k] = last
        edges[0, rows, :] = (m + 2.0) * near - value[1] - tiles[0]
        edges[1, rows, :] = far
        value = swap_blocks(value)
        for c in range(8):
            work[c, rows, :] = value[c]
    for c in range(8):
        res = jnp.dot(table[...], three_rows(work[c]), preferred_element_type=F32)
        done[pl.ds(128 * c, 128), :] = res
        out[:, c] = res.reshape(8, 16, 128)
    for side in range(2):
        res = jnp.dot(table[...], three_rows(edges[side]), preferred_element_type=F32)
        out[:, 8 + side] = res.reshape(8, 16, 128)
    for d in range(8):
        before = (16 * d + 127) % 128
        after = (16 * d + 16) % 128
        out[d, 10, pl.ds(0, 8), :] = done[pl.ds(before, 8, stride=128), :]
        out[d, 10, pl.ds(8, 8), :] = done[pl.ds(after, 8, stride=128), :]


PLANE = 18 * 32


def update_body(last, refs):
    if last:
        (recv, links_hbm, face_x, face_y, table_back, prior, prior_y, div, gauge, theta) = refs[:10]
        table = out = gout = gout_y = spectrum = None
        (links, sem, packed, comps_in, gs, edge_g, ay, prev, rows_in) = refs[10:]
    else:
        (recv, links_hbm, face_x, face_y, table_back, table, out, theta, gout, gout_y) = refs[:10]
        prior = prior_y = div = gauge = None
        (links, sem, packed, comps_in, gs, edge_g, ay, prev, rows_in, spectrum) = refs[10:]
    copy = pltpu.make_async_copy(links_hbm, links, sem)
    copy.start()
    theta[...] = jnp.zeros_like(theta)

    for r in range(11):
        tiles = swap_blocks([recv[s, r] for s in range(8)])
        for x in range(8):
            packed[x, pl.ds(16 * r, 16), :] = tiles[x]
    for x in range(8):
        comps_in[pl.ds(176 * x, 176), :] = jnp.dot(
            three_lanes(packed[x]), table_back[...], preferred_element_type=F32
        )

    def make(c, before):
        re6, im6 = exponent_rows(c)
        if before is not None:
            re6, im6 = times_rows(re6, im6, before[:9], before[9:])
        return full_matrix(re6, im6)

    def plane(index, c_of, rows):
        before = None
        if last:
            before = [prior[index, k, rows, :] for k in range(18)]
        g = make(c_of(rows), before)
        start = rows.start + 8
        for k in range(18):
            gs[pl.ds(index * PLANE + 32 * k + start, 8), :] = g[k]
            if not last:
                gout[index, k, rows, :] = g[k]
        if last and isinstance(index, int) is False:
            for p in range(2):
                for i in range(2):
                    for j in range(3):
                        gauge[p, i, j, index - 1, rows, :] = g[9 * p + entry(i, j)]

    def inner(x, carry):
        for half in range(2):
            rows = pl.ds(8 * half, 8)
            plane(
                x + 1,
                lambda rr: [
                    comps_in[pl.ds(176 * x + 16 * c + rr.start, 8), :] for c in range(8)
                ],
                rows,
            )
        return carry

    lax.fori_loop(0, 8, inner, 0)
    for side in range(2):
        for half in range(2):
            rows = pl.ds(8 * half, 8)
            plane(
                9 * side,
                lambda rr: [
                    comps_in[pl.ds(176 * c + 128 + 16 * side + rr.start, 8), :] for c in range(8)
                ],
                rows,
            )
    for side in range(2):
        c = [comps_in[pl.ds(160 + 8 * side + k, 8, stride=176), :] for k in range(8)]
        before = [prior_y[side, k] for k in range(18)] if last else None
        g = make(c, before)
        for k in range(18):
            if not last:
                gout_y[side, k] = g[k]
            if side == 0:
                edge_g[k] = g[k]
            else:
                gs[pl.ds(PLANE + 32 * k + 24, 8, stride=PLANE), :] = g[k]

    g = [edge_g[k] for k in range(18)]
    ahead = [gs[pl.ds(PLANE + 32 * k + 8, 8, stride=PLANE), :] for k in range(18)]
    edge = moved_algebra(g, lambda p, i, j: face_y[p, i, j], ahead)
    for c in range(8):
        ay[pl.ds(24 * c + 7, 8, stride=192), :] = edge[c]
    for half in range(2):
        rows = pl.ds(8 * half, 8)
        start = 8 * half + 8
        g = [gs[pl.ds(32 * k + start, 8), :] for k in range(18)]
        ahead = [gs[pl.ds(PLANE + 32 * k + start, 8), :] for k in range(18)]
        edge = moved_algebra(g, lambda p, i, j: face_x[p, i, j, rows, :], ahead)
        for c in range(8):
            prev[c, rows, :] = edge[c]

    copy.wait()

    def sites(x, carry):
        base = (x + 1) * PLANE
        for half in range(2):
            rows = pl.ds(8 * half, 8)
            start = 8 * half + 8
            total = [None] * 8

            def load_g():
                return [gs[pl.ds(base + 32 * k + start, 8), :] for k in range(18)]

            def link_of(mu):
                return lambda p, i, j: links[mu, p, i, j, x, rows, :]

            g = load_g()
            ahead = [gs[pl.ds(base + PLANE + 32 * k + start, 8), :] for k in range(18)]
            a = moved_algebra(g, link_of(0), ahead)
            for c in range(8):
                total[c] = prev[c, rows, :] - a[c]
                prev[c, rows, :] = a[c]
            ahead = [gs[pl.ds(base + 32 * k + start + 1, 8), :] for k in range(18)]
            a = moved_algebra(g, link_of(1), ahead)
            for c in range(8):
                ay[pl.ds(x * 192 + 24 * c + start, 8), :] = a[c]
            for c in range(8):
                total[c] = total[c] + (ay[pl.ds(x * 192 + 24 * c + start - 1, 8), :] - a[c])
            ahead = [pltpu.roll(v, 127, 1) for v in g]
            a = moved_algebra(g, link_of(2), ahead)
            for c in range(8):
                total[c] = total[c] + (pltpu.roll(a[c], 1, 1) - a[c])
                if last:
                    div[c, x, rows, :] = total[c]
                else:
                    rows_in[pl.ds(16 * c + 8 * half, 8), :] = total[c]
            theta[...] += squares(total)
        if not last:
            spectrum[x] = jnp.dot(
                three_lanes(rows_in[...]), table[...], preferred_element_type=F32
            )
        return carry

    lax.fori_loop(0, 8, sites, 0)
    if not last:
        scatter_blocks(spectrum, out)


def update_kernel(*refs):
    update_body(False, refs)


def last_kernel(*refs):
    update_body(True, refs)


def struct(*shape):
    return jax.ShapeDtypeStruct(shape, F32)


def vmem(*shape):
    return pltpu.VMEM(shape, F32)


def whole():
    return pl.BlockSpec(memory_space=pltpu.VMEM)


def params(size):
    return pltpu.CompilerParams(vmem_limit_bytes=size * MEGA)


def first_call(links, face_x, face_y):
    spec = pl.BlockSpec((3, 2, 3, 3, 1, 16, 128), lambda i: (0, 0, 0, 0, i, 0, 0))

    def fixed(*shape):
        return pl.BlockSpec(shape, lambda i: (0,) * len(shape))

    return pl.pallas_call(
        first_kernel,
        grid=(8,),
        in_specs=[spec, fixed(8, 16, 128), fixed(8, 8, 128), fixed(384, 128)],
        out_specs=[fixed(8, 8, 16, 128), fixed(8, 128)],
        out_shape=[struct(8, 8, 16, 128), struct(8, 128)],
        scratch_shapes=[vmem(8, 16, 128), vmem(128, 128), vmem(8, 128, 128)],
        compiler_params=params(16),
        name="first_divergence",
    )(links, face_x, face_y, jnp.asarray(Z_FORWARD))


def forward_call(recv, mass):
    return pl.pallas_call(
        forward_kernel,
        in_specs=[whole()] * 3,
        out_specs=[whole()] * 2,
        out_shape=[struct(8, 128, 128), struct(16, 3, 8, 128)],
        scratch_shapes=[vmem(8, 128, 128)],
        compiler_params=params(16),
        name="forward_y",
    )(recv, jnp.asarray(Y_FORWARD), mass)


def ring_call(recv, ring, zero):
    return pl.pallas_call(
        ring_kernel,
        in_specs=[whole()] * 3,
        out_specs=whole(),
        out_shape=struct(16, 2, 8, 128),
        compiler_params=params(8),
        name="ring_solve",
    )(recv, ring, zero)


def back_call(spectrum, faces, mass):
    return pl.pallas_call(
        back_kernel,
        in_specs=[whole()] * 4,
        out_specs=whole(),
        out_shape=struct(8, 11, 16, 128),
        scratch_shapes=[vmem(8, 128, 128), vmem(2, 128, 128), vmem(1024, 128)],
        compiler_params=params(16),
        name="back_y",
    )(spectrum, faces, jnp.asarray(Y_BACK), mass)


def update_call(recv, links, face_x, face_y, prior):
    last = prior is not None
    specs = [whole(), pl.BlockSpec(memory_space=pl.ANY), whole(), whole(), whole()]
    scratch = [
        vmem(3, 2, 3, 3, 8, 16, 128),
        pltpu.SemaphoreType.DMA,
        vmem(8, 176, 128),
        vmem(8 * 176, 128),
        vmem(10 * PLANE, 128),
        vmem(18, 8, 128),
        vmem(8 * 192, 128),
        vmem(8, 16, 128),
        vmem(128, 128),
    ]
    operands = [recv, links, face_x, face_y, jnp.asarray(Z_BACK)]
    if last:
        shapes = [struct(8, 8, 16, 128), struct(2, 2, 3, 8, 16, 128), struct(8, 128)]
        operands += list(prior)
        specs += [whole()] * 2
    else:
        shapes = [
            struct(8, 8, 16, 128),
            struct(8, 128),
            struct(10, 18, 16, 128),
            struct(2, 18, 8, 128),
        ]
        operands += [jnp.asarray(Z_FORWARD)]
        specs += [whole()]
        scratch += [vmem(8, 128, 128)]
    return pl.pallas_call(
        last_kernel if last else update_kernel,
        in_specs=specs,
        out_specs=[whole()] * len(shapes),
        out_shape=shapes,
        scratch_shapes=scratch,
        compiler_params=params(32),
        name="last_update" if last else "update",
    )(*operands)


def shifted(value, axis, steps):
    count = lax.axis_size(axis)
    pairs = [(source, (source + steps) % count) for source in range(count)]
    return lax.ppermute(value, axis, pairs)


def exchange(value, axis):
    return lax.all_to_all(value, axis, split_axis=0, concat_axis=0, tiled=True)


def face_algebra(link):
    return jnp.stack(algebra(lambda i, j: link[0, i, j], lambda i, j: link[1, i, j]))


def per_device(links):
    gx, gy = lax.axis_index("gx"), lax.axis_index("gy")
    own_x = links[0, :, :, :, 7]
    own_y = links[1, :, :, :, :, 15]
    near_x = shifted(face_algebra(own_x), "gx", 1)
    near_y = shifted(face_algebra(own_y), "gy", 1)
    face_x = shifted(own_x, "gx", 1)
    face_y = shifted(own_y, "gy", 1)

    squares_y = jnp.asarray(SQUARES.astype(np.float32))[:, None]
    squares_z = jnp.asarray(np.tile(SQUARES.astype(np.float32).reshape(8, 1, 16), (1, 8, 1)).reshape(8, 128))
    mass = squares_y + lax.dynamic_slice(squares_z, (gy, 0), (1, 128))
    ring = lax.dynamic_slice(jnp.asarray(RING), (0, gx * 8, gy * 16), (9, 8, 16))
    ring = jnp.tile(ring, (1, 1, 8))
    lane = lax.broadcasted_iota(jnp.int32, (8, 128), 1)
    row = lax.broadcasted_iota(jnp.int32, (8, 128), 0)
    zero = jnp.where((row + gx + gy == 0) & (lane % 16 == 0), -1.0 / 128.0, 0.0).astype(F32)

    packed, theta0 = first_call(links, near_x, near_y)
    thetas = [theta0]
    prior = None
    for step in range(2):
        spectrum, moments = forward_call(exchange(packed, "gy"), mass)
        faces = exchange(ring_call(exchange(moments, "gx"), ring, zero), "gx")
        back = exchange(back_call(spectrum, faces, mass), "gy")
        if step == 0:
            packed, theta, gout, gout_y = update_call(back, links, face_x, face_y, None)
            prior = (gout, gout_y)
        else:
            div, gauge, theta = update_call(back, links, face_x, face_y, prior)
        thetas.append(theta)
    sums = jnp.sum(jnp.stack(thetas), axis=(1, 2))
    sums = jnp.pad(sums, (0, 125)).reshape(1, 1, 128)
    sums = exchange(jnp.broadcast_to(sums, (8, 1, 128)), "gy")
    sums = jnp.sum(sums, axis=0, keepdims=True)
    sums = exchange(jnp.broadcast_to(sums, (16, 1, 128)), "gx")
    sums = jnp.sum(sums, axis=(0, 1))[:3] / (3.0 * LS * LS * NZ)
    return (gauge, div, sums)


def solution(mesh):
    in_specs = (P(None, None, None, None, "gx", "gy", "ta"),)
    out_specs = (P(None, None, None, "gx", "gy", "ta"), P(None, "gx", "gy", "ta"), P("ta"))
    return jax.shard_map(
        per_device, mesh=mesh, in_specs=in_specs, out_specs=out_specs, check_vma=False
    )
```

time: 822 us -> 227 us (0.28); the launches traced: 811 us -> 225 us
  waiting for transfers between devices: 272 us -> 28.9 us
  blocking collectives: 248 us -> 112 us
  starting transfers between devices: 144 us -> 34.8 us
  matrix products: 64.5 us -> 0 us
  other arithmetic: 34.5 us -> 1.54 us
  Pallas kernels: 0 us -> 24.9 us
  local copies, waits for them, and re-layouts: 42.9 us -> 22.2 us
    psum x1 -> x0, blocking collectives: 248 us -> none  [per_device(): thetas.append(lax.psum(local_sum, ('gx', 'gy')) / (3.0 * LS * LS * NZ))]
    all_to_all x16 -> x3, waiting for transfers between devices: 256 us -> 18.3 us  [exchange(): return lax.all_to_all(value, axis, split_axis=0, concat_axis=0, tiled=True)]
    all_to_all x0 -> x7, blocking collectives: none -> 112 us  [exchange(): return lax.all_to_all(value, axis, split_axis=0, concat_axis=0, tiled=True)]
    all_to_all x16 -> x3, starting transfers between devices: 122 us -> 23.4 us  [exchange(): return lax.all_to_all(value, axis, split_axis=0, concat_axis=0, tiled=True)]
    dot_general x40 -> x0, matrix products: 64.5 us -> none  [the longest x32 53.5 us: along(): jnp.einsum('anr,nk->akr', flat, table, precision=lax.Precision.HIGHEST)]
    pallas_call x0 -> x9, Pallas kernels: none -> 24.9 us  [the longest x2 16.4 us: update_call(): pl.pallas_call(last_kernel if last else update_kernel, in_specs=specs, ou...]
    reduce_sum x23 -> x3, other arithmetic: 19.5 us -> 0.14 us  [the longest x1 0.11 us: per_device(): sums = jnp.sum(jnp.stack(thetas), axis=(1, 2))]
    mul x11 -> x0, local copies, waits for them, and re-layouts: 10.8 us -> none  [the longest x4 4.42 us: transform(): new_imag = (along(imag, cosine, axis) + along(real, sine, axis)) * scale]
  transfers between devices with their start and end apart: 26 -> 7, of which waited for: 22 -> 6; matrix products, arithmetic and copies ran while one was open for 9% -> 3% of each run, Pallas kernels for 0% -> 0%
where the time goes in v1:
time: 227 us; the launch traced here: 225 us
  blocking collectives  112 us (49%)
  starting transfers between devices  34.8 us (15%)
  waiting for transfers between devices  28.9 us (13%)
  Pallas kernels  24.9 us (11%)
  local copies, waits for them, and re-layouts  22.2 us (10%)
    all_to_all x7, blocking collectives, exchange(): return lax.all_to_all(value, axis, split_axis=0, concat_axis=0, tiled=True)  112 us
    all_to_all x3, starting transfers between devices, exchange(): return lax.all_to_all(value, axis, split_axis=0, concat_axis=0, tiled=True)  23.4 us
    all_to_all x3, waiting for transfers between devices, exchange(): return lax.all_to_all(value, axis, split_axis=0, concat_axis=0, tiled=True)  18.3 us
    pallas_call x2, Pallas kernels, update_call(): pl.pallas_call(last_kernel if last else update_kernel, in_specs=specs, ou...  16.4 us
    unnamed x52, local copies, waits for them, and re-layouts  16.2 us
    ppermute x4, starting transfers between devices, shifted(): return lax.ppermute(value, axis, pairs)  11.4 us
    ppermute x4, waiting for transfers between devices, shifted(): return lax.ppermute(value, axis, pairs)  10.6 us
  transfers between devices with their start and end apart: 7, of which 6 were waited for; matrix products, arithmetic and copies ran while one was open for 3% of the time, Pallas kernels for 0%

profile of v1, /device:TPU:1, one launch (start us, length us, event | category | flops | bytes accessed | tf_op | source)
XLA Modules:
  0.0 225.1 jit_solution(12640800236586483750)
XLA Ops:
  0.6 0.0 copy-start.25
  0.6 0.9 slice_bitcast_fusion
  1.7 4.4 %collective-permute-start = (f32[8,16,128]{2,1,0:T(8,128)S(1)}, f32[8,16,128]{2,1,0:T(8,128)S(1)}, u32[]{:S(2)}, u32[]{:S(2)}) collective-permute-start(f32[8,16,128]{2,1,0:T(8,128)S(1)} %constant_dynamic-update-slice_fusion), channel_id=1, source_target_pairs={{0,8},{8,16},{16,24},{24,32},{32,40},{40,48},{48,56},{56,64},{64,7... | collective-permute-start | bytes 196616 | tf_op jit(solution)/shard_map/ppermute | solution.py:627
  6.1 1.1 slice.115
  7.2 0.0 copy-start.24
  7.3 2.1 collective-permute-start.1
  9.4 3.1 %collective-permute-done.1.face_y = f32[8,8,128]{2,1,0:T(8,128)S(1)} collective-permute-done((f32[8,8,128]{2,1,0:T(8,128)S(1)}, f32[8,8,128]{2,1,0:T(8,128)S(1)}, u32[]{:S(2)}, u32[]{:S(2)}) %collective-permute-start.1) | collective-permute-done | bytes 32800 | tf_op jit(solution)/shard_map/ppermute | solution.py:627
  12.5 0.0 copy-done.24
  12.5 3.1 %collective-permute-done.face_x = f32[8,16,128]{2,1,0:T(8,128)S(1)} collective-permute-done((f32[8,16,128]{2,1,0:T(8,128)S(1)}, f32[8,16,128]{2,1,0:T(8,128)S(1)}, u32[]{:S(2)}, u32[]{:S(2)}) %collective-permute-start) | collective-permute-done | bytes 65568 | tf_op jit(solution)/shard_map/ppermute | solution.py:627
  15.6 2.0 copy-done
  17.6 0.9 copy-done.16
  18.5 3.3 %first_divergence.1 = (f32[8,8,16,128]{3,2,1,0:T(8,128)S(1)}, f32[8,128]{1,0:T(8,128)S(1)}) custom-call(f32[3,2,3,3,8,16,128]{6,5,4,3,2,1,0:T(8,128)S(1)} %copy-done, f32[8,16,128]{2,1,0:T(8,128)S(1)} %collective-permute-done.face_x, f32[8,8,128]{2,1,0:T(8,128)S(1)} %collective-permute-done.1.face_y, bf16[384,128]{1,0:T(8,128)(2,1)S(1)} %copy-done.16), custom_call_target="tpu_custom_call" | custom-call | tf_op jit(solution)/shard_map/first_divergence/pallas_call | solution.py:537
  21.8 0.0 copy-start.10
  21.8 0.8 copy-done.10
  22.6 5.8 %all-to-all-start = ((f32[8,8,16,128]{3,2,1,0:T(8,128)}), f32[8,8,16,128]{3,2,1,0:T(8,128)}, u32[]{:S(2)}, u32[]{:S(2)}) async-start(f32[8,8,16,128]{3,2,1,0:T(8,128)} %copy-done.10), calls=%async_computation | async-start | bytes 1048576 | tf_op jit(solution)/shard_map/all_to_all | solution.py:631
  28.4 0.7 dynamic-slice_bitcast_fusion
  29.1 0.7 broadcast_add_fusion.mass
  29.8 8.2 %all-to-all-done.recv = f32[8,8,16,128]{3,2,1,0:T(8,128)} async-done(((f32[8,8,16,128]{3,2,1,0:T(8,128)}), f32[8,8,16,128]{3,2,1,0:T(8,128)}, u32[]{:S(2)}, u32[]{:S(2)}) %all-to-all-start) | async-done | bytes 524320 | tf_op jit(solution)/shard_map/all_to_all | solution.py:631
  38.0 0.8 copy-done.3
  38.8 0.9 copy-done.13
  39.7 1.7 forward_y.2
  41.5 0.0 copy-start.8
  41.5 0.8 copy-done.8
  42.3 0.7 copy-done.22
  42.9 9.8 %all-to-all-start.1 = ((f32[16,3,8,128]{3,2,1,0:T(8,128)}), f32[16,3,8,128]{3,2,1,0:T(8,128)}, u32[]{:S(2)}, u32[]{:S(2)}) async-start(f32[16,3,8,128]{3,2,1,0:T(8,128)} %copy-done.22), calls=%async_computation.1 | async-start | bytes 393216 | tf_op jit(solution)/shard_map/all_to_all | solution.py:631
  52.8 0.9 constant_dynamic-slice_fusion
  53.6 0.7 tile.4
  54.4 1.7 tile.10.ring
  56.1 0.1 fusion.29.zero
  56.2 9.0 %all-to-all-done.1.recv = f32[16,3,8,128]{3,2,1,0:T(8,128)} async-done(((f32[16,3,8,128]{3,2,1,0:T(8,128)}), f32[16,3,8,128]{3,2,1,0:T(8,128)}, u32[]{:S(2)}, u32[]{:S(2)}) %all-to-all-start.1) | async-done | bytes 196640 | tf_op jit(solution)/shard_map/all_to_all | solution.py:631
  65.2 0.8 copy-done.18
  66.0 1.0 ring_solve.2
  67.0 20.8 %all_to_all.50.faces = f32[16,2,8,128]{3,2,1,0:T(8,128)S(1)} all-to-all(f32[16,2,8,128]{3,2,1,0:T(8,128)S(1)} %ring_solve.2), channel_id=1, replica_groups=mesh['ta'=4,'gx'=16,'gy'=8] {'gx'}, dimensions={0} | all-to-all | bytes 262144 | tf_op jit(solution)/shard_map/all_to_all | solution.py:631
  87.7 0.8 copy-done.4
  88.6 1.0 copy-done.9
  89.6 0.9 copy-done.11
  90.5 0.9 back_y.2
  91.4 0.0 copy-start.2
  91.4 0.8 copy-done.2
  92.3 7.7 %all-to-all-start.3 = ((f32[8,11,16,128]{3,2,1,0:T(8,128)}), f32[8,11,16,128]{3,2,1,0:T(8,128)}, u32[]{:S(2)}, u32[]{:S(2)}) async-start(f32[8,11,16,128]{3,2,1,0:T(8,128)} %copy-done.2), calls=%async_computation.3 | async-start | bytes 1441792 | tf_op jit(solution)/shard_map/all_to_all | solution.py:631
  100.0 3.1 %collective-permute-start.2 = (f32[2,3,3,16,128]{4,3,2,1,0:T(8,128)}, f32[2,3,3,16,128]{4,3,2,1,0:T(8,128)S(1)}, u32[]{:S(2)}, u32[]{:S(2)}) collective-permute-start(f32[2,3,3,16,128]{4,3,2,1,0:T(8,128)} %copy-done.23), channel_id=1, source_target_pairs={{0,8},{8,16},{16,24},{24,32},{32,40},{40,48},{48,56},{56,64},{64,7... | collective-permute-start | bytes 442376 | tf_op jit(solution)/shard_map/ppermute | solution.py:627
  103.1 1.9 collective-permute-start.3
  105.0 4.4 %collective-permute-done.3.refs_3_ = f32[2,3,3,8,128]{4,3,2,1,0:T(8,128)S(1)} collective-permute-done((f32[2,3,3,8,128]{4,3,2,1,0:T(8,128)}, f32[2,3,3,8,128]{4,3,2,1,0:T(8,128)S(1)}, u32[]{:S(2)}, u32[]{:S(2)}) %collective-permute-start.3) | collective-permute-done | bytes 73760 | tf_op jit(solution)/shard_map/ppermute | solution.py:627
  109.4 0.6 copy-done.20
  110.0 0.0 collective-permute-done.2.refs_2_
  110.0 0.7 copy-done.6
  110.7 1.1 all-to-all-done.3.refs_0_
  111.8 0.9 copy-done.7
  112.7 0.9 copy-done.15
  113.6 0.9 copy-done.17
  114.5 0.9 copy-done.21
  115.4 9.2 %update.1 = (f32[8,8,16,128]{3,2,1,0:T(8,128)S(1)}, f32[8,128]{1,0:T(8,128)S(1)}, f32[10,18,16,128]{3,2,1,0:T(8,128)S(1)}, f32[2,18,8,128]{3,2,1,0:T(8,128)S(1)}) custom-call(f32[8,11,16,128]{3,2,1,0:T(8,128)} %all-to-all-done.3.refs_0_, f32[3,2,3,3,8,16,128]{6,5,4,3,2,1,0:T(8,128)S(1)} %copy-done.1, f32[2,3,3,16,128]{4,3,2,1,0:T(8,128)S(1)} %copy-done.7, ...), custom_call_target="tpu_custom_call" | custom-call | tf_op jit(solution)/shard_map/update/pallas_call | solution.py:613
  124.6 14.3 %all_to_all.51.recv = f32[8,8,16,128]{3,2,1,0:T(8,128)S(1)} all-to-all(f32[8,8,16,128]{3,2,1,0:T(8,128)S(1)} %get-tuple-element.19), channel_id=1, replica_groups=mesh['ta'=4,'gx'=16,'gy'=8] {'gy'}, dimensions={0} | all-to-all | bytes 1048576 | tf_op jit(solution)/shard_map/all_to_all | solution.py:631
  138.9 0.7 forward_y.3
  139.6 15.7 %all_to_all.52.recv = f32[16,3,8,128]{3,2,1,0:T(8,128)S(1)} all-to-all(f32[16,3,8,128]{3,2,1,0:T(8,128)S(1)} %get-tuple-element.21), channel_id=1, replica_groups=mesh['ta'=4,'gx'=16,'gy'=8] {'gx'}, dimensions={0} | all-to-all | bytes 393216 | tf_op jit(solution)/shard_map/all_to_all | solution.py:631
  155.3 0.1 ring_solve.3
  155.3 20.8 %all_to_all.53.faces = f32[16,2,8,128]{3,2,1,0:T(8,128)S(1)} all-to-all(f32[16,2,8,128]{3,2,1,0:T(8,128)S(1)} %ring_solve.3), channel_id=1, replica_groups=mesh['ta'=4,'gx'=16,'gy'=8] {'gx'}, dimensions={0} | all-to-all | bytes 262144 | tf_op jit(solution)/shard_map/all_to_all | solution.py:631
  176.2 0.9 back_y.3
  177.0 17.6 %all_to_all.54.refs_0_ = f32[8,11,16,128]{3,2,1,0:T(8,128)S(1)} all-to-all(f32[8,11,16,128]{3,2,1,0:T(8,128)S(1)} %back_y.3), channel_id=1, replica_groups=mesh['ta'=4,'gx'=16,'gy'=8] {'gy'}, dimensions={0} | all-to-all | bytes 1441792 | tf_op jit(solution)/shard_map/all_to_all | solution.py:631
  194.7 7.2 %last_update.1 = (f32[8,8,16,128]{3,2,1,0:T(8,128)}, f32[2,2,3,8,16,128]{5,4,3,2,1,0:T(8,128)}, f32[8,128]{1,0:T(8,128)S(1)}) custom-call(f32[8,11,16,128]{3,2,1,0:T(8,128)S(1)} %all_to_all.54.refs_0_, f32[3,2,3,3,8,16,128]{6,5,4,3,2,1,0:T(8,128)S(1)} %copy-done.1, f32[2,3,3,16,128]{4,3,2,1,0:T(8,128)S(1)} %copy-done.7, f32[2,3,3,8,128]{4,3,2,1,0:T(8,128)S(1)} %copy-done.21, ...), custom_call_target="tpu_custom_call" | custom-call | tf_op jit(solution)/shard_map/last_update/pallas_call | solution.py:613
  201.9 0.1 maximum_reduce_fusion
  202.0 7.9 %all_to_all.55 = f32[8,1,128]{2,1,0:T(1,128)S(1)} all-to-all(f32[8,1,128]{2,1,0:T(1,128)S(1)} %broadcast_in_dim.22), channel_id=1, replica_groups=mesh['ta'=4,'gx'=16,'gy'=8] {'gy'}, dimensions={0} | all-to-all | bytes 8192 | tf_op jit(solution)/shard_map/all_to_all | solution.py:631
  209.9 14.7 %all_to_all.56 = f32[16,1,128]{2,1,0:T(1,128)S(1)} all-to-all(f32[16,1,128]{2,1,0:T(1,128)S(1)} %broadcast_in_dim.23), channel_id=1, replica_groups=mesh['ta'=4,'gx'=16,'gy'=8] {'gx'}, dimensions={0} | all-to-all | bytes 16384 | tf_op jit(solution)/shard_map/all_to_all | solution.py:631
  224.5 0.5 slice_multiply_fusion
  (52 shorter events, 0.2 us)
Async XLA Ops:
  0.6 28.5 %copy-start.25 = (f32[128]{0:T(128)S(1)}, f32[128]{0:T(128)}, u32[]{:S(2)}) copy-start(f32[128]{0:T(128)} %constant.59.clone) | copy-start | bytes 1540
  1.6 10.9 %copy-start.23 = (f32[2,3,3,16,128]{4,3,2,1,0:T(8,128)}, f32[2,3,3,16,128]{4,3,2,1,0:T(8,128)S(1)}, u32[]{:S(2)}) copy-start(f32[2,3,3,16,128]{4,3,2,1,0:T(8,128)S(1)} %slice_bitcast_fusion) | copy-start | bytes 442372
  1.7 13.9 %collective-permute-start = (f32[8,16,128]{2,1,0:T(8,128)S(1)}, f32[8,16,128]{2,1,0:T(8,128)S(1)}, u32[]{:S(2)}, u32[]{:S(2)}) collective-permute-start(f32[8,16,128]{2,1,0:T(8,128)S(1)} %constant_dynamic-update-slice_fusion), channel_id=1, source_target_pairs={{0,8},{8,16},{16,24},{24,32},{32,40},{40,48},{48,56},{56,64},{64,7... | collective-permute-start | bytes 196616 | tf_op jit(solution)/shard_map/ppermute | solution.py:627
  7.2 5.3 %copy-start.24 = (f32[1,2,3,3,8,1,128]{6,5,4,3,2,1,0:T(1,128)}, f32[1,2,3,3,8,1,128]{6,5,4,3,2,1,0:T(1,128)S(1)}, u32[]{:S(2)}) copy-start(f32[1,2,3,3,8,1,128]{6,5,4,3,2,1,0:T(1,128)S(1)} %slice.115) | copy-start | bytes 221188
  7.3 5.1 %collective-permute-start.1 = (f32[8,8,128]{2,1,0:T(8,128)S(1)}, f32[8,8,128]{2,1,0:T(8,128)S(1)}, u32[]{:S(2)}, u32[]{:S(2)}) collective-permute-start(f32[8,8,128]{2,1,0:T(8,128)S(1)} %constant_dynamic-update-slice_fusion.8), channel_id=1, source_target_pairs={{0,1},{1,2},{2,3},{3,4},{4,5},{5,6},{6,7},{7,0},{8,9},{9,10},{10,1... | collective-permute-start | bytes 98312 | tf_op jit(solution)/shard_map/ppermute | solution.py:627
  15.6 2.0 copy-start
  17.6 0.9 copy-start.16
  21.8 0.8 copy-start.10
  22.6 89.2 %copy-start.1 = (f32[3,2,3,3,8,16,128]{6,5,4,3,2,1,0:T(8,128)S(1)}, f32[3,2,3,3,8,16,128]{6,5,4,3,2,1,0:T(8,128)}, u32[]{:S(2)}) copy-start(f32[3,2,3,3,8,16,128]{6,5,4,3,2,1,0:T(8,128)} %refs_1_.3) | copy-start | bytes 10616836
  22.6 15.4 %all-to-all-start = ((f32[8,8,16,128]{3,2,1,0:T(8,128)}), f32[8,8,16,128]{3,2,1,0:T(8,128)}, u32[]{:S(2)}, u32[]{:S(2)}) async-start(f32[8,8,16,128]{3,2,1,0:T(8,128)} %copy-done.10), calls=%async_computation | async-start | bytes 1048576 | tf_op jit(solution)/shard_map/all_to_all | solution.py:631
  38.0 0.8 copy-start.3
  38.8 0.9 copy-start.13
  41.5 0.8 copy-start.8
  42.3 0.7 copy-start.22
  42.9 22.3 %all-to-all-start.1 = ((f32[16,3,8,128]{3,2,1,0:T(8,128)}), f32[16,3,8,128]{3,2,1,0:T(8,128)}, u32[]{:S(2)}, u32[]{:S(2)}) async-start(f32[16,3,8,128]{3,2,1,0:T(8,128)} %copy-done.22), calls=%async_computation.1 | async-start | bytes 393216 | tf_op jit(solution)/shard_map/all_to_all | solution.py:631
  65.2 0.8 copy-start.18
  87.7 0.8 copy-start.4
  88.6 1.0 copy-start.9
  89.6 0.9 copy-start.11
  91.4 0.9 copy-start.2
  92.3 19.5 %all-to-all-start.3 = ((f32[8,11,16,128]{3,2,1,0:T(8,128)}), f32[8,11,16,128]{3,2,1,0:T(8,128)}, u32[]{:S(2)}, u32[]{:S(2)}) async-start(f32[8,11,16,128]{3,2,1,0:T(8,128)} %copy-done.2), calls=%async_computation.3 | async-start | bytes 1441792 | tf_op jit(solution)/shard_map/all_to_all | solution.py:631
  100.0 10.0 %collective-permute-start.2 = (f32[2,3,3,16,128]{4,3,2,1,0:T(8,128)}, f32[2,3,3,16,128]{4,3,2,1,0:T(8,128)S(1)}, u32[]{:S(2)}, u32[]{:S(2)}) collective-permute-start(f32[2,3,3,16,128]{4,3,2,1,0:T(8,128)} %copy-done.23), channel_id=1, source_target_pairs={{0,8},{8,16},{16,24},{24,32},{32,40},{40,48},{48,56},{56,64},{64,7... | collective-permute-start | bytes 442376 | tf_op jit(solution)/shard_map/ppermute | solution.py:627
  103.1 6.3 %collective-permute-start.3 = (f32[2,3,3,8,128]{4,3,2,1,0:T(8,128)}, f32[2,3,3,8,128]{4,3,2,1,0:T(8,128)S(1)}, u32[]{:S(2)}, u32[]{:S(2)}) collective-permute-start(f32[2,3,3,8,128]{4,3,2,1,0:T(8,128)} %bitcast.135), channel_id=1, source_target_pairs={{0,1},{1,2},{2,3},{3,4},{4,5},{5,6},{6,7},{7,0},{8,9},{9,10},{10,1... | collective-permute-start | bytes 221192 | tf_op jit(solution)/shard_map/ppermute | solution.py:627
  109.4 0.6 copy-start.20
  110.0 0.7 copy-start.6
  111.8 0.9 copy-start.7
  112.7 0.9 copy-start.15
  113.6 0.9 copy-start.17
  114.5 0.9 copy-start.21
  115.3 23.5 %copy-start.5 = (f32[128,128]{1,0:T(8,128)S(1)}, f32[128,128]{1,0:T(8,128)}, u32[]{:S(2)}) copy-start(f32[128,128]{1,0:T(8,128)} %broadcast_add_fusion.mass) | copy-start | bytes 196612
  115.3 23.5 %copy-start.14 = (bf16[128,384]{1,0:T(8,128)(2,1)S(1)}, bf16[128,384]{1,0:T(8,128)(2,1)}, u32[]{:S(2)}) copy-start(bf16[128,384]{1,0:T(8,128)(2,1)} %constant.63.clone.table) | copy-start | bytes 294916
  115.3 39.9 %copy-start.19 = (f32[9,8,128]{2,1,0:T(8,128)S(1)}, f32[9,8,128]{2,1,0:T(8,128)}, u32[]{:S(2)}) copy-start(f32[9,8,128]{2,1,0:T(8,128)} %tile.10.ring) | copy-start | bytes 110596
  115.3 60.8 %copy-start.12 = (bf16[128,384]{1,0:T(8,128)(2,1)S(1)}, bf16[128,384]{1,0:T(8,128)(2,1)}, u32[]{:S(2)}) copy-start(bf16[128,384]{1,0:T(8,128)(2,1)} %constant.64.clone.table) | copy-start | bytes 294916

commit v2 on v1

v2 whole, which is shorter than its diff:
```python
import math

import jax
import jax.numpy as jnp
import numpy as np
from jax import lax
from jax.experimental import pallas as pl
from jax.experimental.pallas import tpu as pltpu
from jax.sharding import PartitionSpec as P

LS = 128
NZ = 128
STEP_SIZE = 0.08
PEAK_MOMENTUM = 12.0
F32 = jnp.float32
BF16 = jnp.bfloat16
MEGA = 1024 * 1024


def real_basis(length):
    site = np.arange(length)[:, None]
    freq = np.arange(length)
    freq = np.where(freq <= length // 2, freq, freq - length // 2)
    phase = 2.0 * np.pi * ((site * freq[None, :]) % length) / length
    index = np.arange(length)[None, :]
    basis = np.where(index <= length // 2, np.cos(phase), np.sin(phase)) * np.sqrt(2.0 / length)
    basis[:, 0] = 1.0 / np.sqrt(length)
    basis[:, length // 2] = np.cos(np.pi * np.arange(length)) / np.sqrt(length)
    return basis, freq


def halves(table):
    high = table.astype(np.float32).astype(jnp.bfloat16)
    low = (table - high.astype(np.float64)).astype(np.float32).astype(jnp.bfloat16)
    return high, low


def right_table(table):
    high, low = halves(table)
    return np.concatenate([high, high, low], axis=0)


def left_table(table):
    high, low = halves(table)
    return np.concatenate([high, high, low], axis=1)


def sine_table():
    x, y = np.arange(8), np.arange(16)
    sx = np.sin(np.pi * np.outer(x, x) / 8.0) * np.sqrt(2.0 / 8.0)
    sy = np.sin(np.pi * np.outer(y, y) / 16.0) * np.sqrt(2.0 / 16.0)
    table = np.kron(sx, sy)
    keep = np.kron(x > 0, y > 0)
    table = table * np.outer(keep, keep)
    eigen = (4.0 * np.sin(np.pi * x / 16.0) ** 2)[:, None] + (4.0 * np.sin(np.pi * y / 32.0) ** 2)[None, :]
    return table, eigen.reshape(128), keep


BASIS, FREQ = real_basis(128)
SQUARES = 4.0 * np.sin(np.pi * FREQ / 128.0) ** 2
SINE, EIGEN, INNER = sine_table()


def node(x, y):
    return 16 * x + y


def reduce_table():
    out = np.zeros((48, 256))
    for y in range(16):
        out[y, node(0, y)] = 1.0
        if y > 0:
            out[y, 128:] = SINE[node(1, y)]
            out[16 + y, 128:] = SINE[node(7, y)]
    out[32, 128:] = SINE[INNER].sum(0)
    for x in range(1, 8):
        out[32 + x, node(x, 0)] = 1.0
        out[32 + x, 128:] = SINE[node(x, 1)]
        out[40 + x, 128:] = SINE[node(x, 15)]
    return out


def source_table():
    out = np.zeros((128, 48))
    for y in range(1, 16):
        out[:, y] = SINE[node(1, y)]
        out[:, 16 + y] = SINE[node(7, y)]
    for x in range(1, 8):
        out[:, 32 + x] = SINE[node(x, 1)]
        out[:, 40 + x] = SINE[node(x, 15)]
    return out


def expand_table():
    out = np.zeros((176, 224))
    val, mass = 128, 176

    def line_x(x):
        return 0 if x == 0 else (16 if x == 8 else 32 + x)

    def line_y(y):
        return 40 if y == 16 else y

    for x in range(1, 8):
        for y in range(1, 16):
            out[node(x, y), :128] = SINE[node(x, y)]
    for y in range(16):
        out[node(0, y), val + y] = 1.0
        out[128 + y, val + 16 + y] = 1.0
    for x in range(1, 8):
        out[node(x, 0), val + 32 + x] = 1.0
    for x in range(8):
        out[160 + x, val + 40 + x] = 1.0
    out[144, val + 32] = 1.0
    for y in range(1, 16):
        row = out[144 + y]
        row[val + y] += 4.0
        row[mass + y] += 1.0
        row[:128] -= SINE[node(1, y)]
        row[val + line_y(y - 1)] -= 1.0
        row[val + line_y(y + 1)] -= 1.0
    for x in range(1, 8):
        row = out[168 + x]
        row[val + line_x(x)] += 4.0
        row[mass + line_x(x)] += 1.0
        row[:128] -= SINE[node(x, 1)]
        row[val + line_x(x - 1)] -= 1.0
        row[val + line_x(x + 1)] -= 1.0
    row = out[168]
    row[val] += 4.0
    row[mass] += 1.0
    row[val + 33] -= 1.0
    row[val + 32] -= 1.0
    row[val + 1] -= 1.0
    return out


def lines_in():
    out = np.zeros((128, 128))
    for g in range(8):
        out[16 * g : 16 * g + 16] = BASIS[16 * g]
    return out


def lines_out():
    out = np.zeros((128, 128))
    for g in range(8):
        out[:, 16 * g : 16 * g + 8] = BASIS[16 * g][:, None]
        out[:, 16 * g + 8 : 16 * g + 16] = BASIS[(16 * g + 16) % 128][:, None]
    return out


SCALE = STEP_SIZE * PEAK_MOMENTUM
ORDER = np.array([8 * j + x for x in range(8) for j in range(16)])


def pack_tables():
    out = np.zeros((864, 768), jnp.bfloat16)
    rights = (BASIS * SCALE, BASIS.T, BASIS, lines_in(), lines_out())
    for k, table in enumerate(rights):
        out[:384, 128 * k : 128 * k + 128] = right_table(table)
    out[384:512, :384] = left_table(SINE)
    out[384:512, 384:] = left_table(BASIS[ORDER].T)
    out[512:640, :384] = left_table(BASIS[ORDER])
    out[512:640, 384:528] = left_table(source_table())
    out[640:688, :] = left_table(reduce_table())
    out[688:864, :672] = left_table(expand_table())
    return out


COARSE = pack_tables()
INVERSE = INNER[:, None] / (np.where(INNER, EIGEN, 1.0)[:, None] + SQUARES[None, :])
PLANE_SUM = SQUARES[:, None] + SQUARES[None, :]
FINE = np.concatenate([INVERSE, PLANE_SUM]).astype(np.float32)
Z_IN, Z_OUT, Y_IN, LINES_IN, LINES_OUT = [(slice(0, 384), slice(128 * k, 128 * k + 128)) for k in range(5)]
MODES = (slice(384, 512), slice(0, 384))
X_IN = (slice(384, 512), slice(384, 768))
X_OUT = (slice(512, 640), slice(0, 384))
SOURCE = (slice(512, 640), slice(384, 528))
REDUCE = (slice(640, 688), slice(0, 768))
EXPAND = (slice(688, 864), slice(0, 672))
ZERO_ROW = 128


def three_lanes(value):
    high = value.astype(BF16)
    low = (value - high.astype(F32)).astype(BF16)
    return jnp.concatenate([high, low, high], axis=1)


def three_rows(value):
    high = value.astype(BF16)
    low = (value - high.astype(F32)).astype(BF16)
    return jnp.concatenate([high, low, high], axis=0)


def swap_blocks(tiles):
    tiles = list(tiles)
    group = lax.broadcasted_iota(jnp.int32, tiles[0].shape, 1) // 16
    for bit in (1, 2, 4):
        upper = (group & bit) != 0
        for i in range(8):
            if i & bit:
                continue
            low, high = tiles[i], tiles[i | bit]
            tiles[i] = jnp.where(upper, pltpu.roll(high, 16 * bit, 1), low)
            tiles[i | bit] = jnp.where(upper, high, pltpu.roll(low, 128 - 16 * bit, 1))
    return tiles


def algebra(mreal, mimag):
    i00, i11, i22 = mimag(0, 0), mimag(1, 1), mimag(2, 2)
    middle = (i00 + i11 + i22) * (1.0 / 3.0)
    return [
        i00 - middle,
        i11 - middle,
        (mreal(0, 1) - mreal(1, 0)) * 0.5,
        (mimag(0, 1) + mimag(1, 0)) * 0.5,
        (mreal(0, 2) - mreal(2, 0)) * 0.5,
        (mimag(0, 2) + mimag(2, 0)) * 0.5,
        (mreal(1, 2) - mreal(2, 1)) * 0.5,
        (mimag(1, 2) + mimag(2, 1)) * 0.5,
    ]


def squares(c):
    third = c[0] + c[1]
    rest = c[2] * c[2] + c[3] * c[3] + c[4] * c[4] + c[5] * c[5] + c[6] * c[6] + c[7] * c[7]
    return c[0] * c[0] + c[1] * c[1] + third * third + 2.0 * rest


def entry(row, col):
    return row * 3 + col


def cross_row(first_re, first_im, second_re, second_im):
    out_re, out_im = [], []
    for k in range(3):
        a, b = (k + 1) % 3, (k + 2) % 3
        out_re.append(
            first_re[a] * second_re[b]
            - first_im[a] * second_im[b]
            - first_re[b] * second_re[a]
            + first_im[b] * second_im[a]
        )
        out_im.append(
            first_re[b] * second_im[a]
            + first_im[b] * second_re[a]
            - first_re[a] * second_im[b]
            - first_im[a] * second_re[b]
        )
    return out_re, out_im


def exponent_rows(c):
    c0, c1, c2, c3, c4, c5, c6, c7 = c
    n01 = c2 * c2 + c3 * c3
    n02 = c4 * c4 + c5 * c5
    n12 = c6 * c6 + c7 * c7
    s00 = 1.0 - 0.5 * (c0 * c0 + n01 + n02)
    s11 = 1.0 - 0.5 * (c1 * c1 + n01 + n12)
    d01 = c0 + c1
    p01r = -(d01 * c3) - (c4 * c6 + c5 * c7)
    p01i = d01 * c2 - (c5 * c6 - c4 * c7)
    p02r = c1 * c5 + (c2 * c6 - c3 * c7)
    p02i = -(c1 * c4) + (c2 * c7 + c3 * c6)
    p12r = -(c2 * c4 + c3 * c5) + c0 * c7
    p12i = -(c2 * c5 - c3 * c4) - c0 * c6
    r0 = [s00, c2 + 0.5 * p01r, c4 + 0.5 * p02r]
    i0 = [c0, c3 + 0.5 * p01i, c5 + 0.5 * p02i]
    r1 = [-c2 + 0.5 * p01r, s11, c6 + 0.5 * p12r]
    i1 = [c3 - 0.5 * p01i, c1, c7 + 0.5 * p12i]
    size = sum(r0[k] * r0[k] + i0[k] * i0[k] for k in range(3))
    scale = 1.0 / jnp.sqrt(size)
    r0 = [v * scale for v in r0]
    i0 = [v * scale for v in i0]
    pr = sum(r0[k] * r1[k] + i0[k] * i1[k] for k in range(3))
    pi = sum(r0[k] * i1[k] - i0[k] * r1[k] for k in range(3))
    r1, i1 = (
        [r1[k] - (pr * r0[k] - pi * i0[k]) for k in range(3)],
        [i1[k] - (pr * i0[k] + pi * r0[k]) for k in range(3)],
    )
    size = sum(r1[k] * r1[k] + i1[k] * i1[k] for k in range(3))
    scale = 1.0 / jnp.sqrt(size)
    r1 = [v * scale for v in r1]
    i1 = [v * scale for v in i1]
    return r0 + r1, i0 + i1


def full_matrix(re6, im6):
    re3, im3 = cross_row(re6[:3], im6[:3], re6[3:], im6[3:])
    return list(re6) + re3 + list(im6) + im3


def times_rows(gre, gim, hre, him):
    out_re, out_im = [], []
    for i in range(2):
        for j in range(3):
            acc_re = acc_im = None
            for k in range(3):
                ar, ai = gre[entry(i, k)], gim[entry(i, k)]
                br, bi = hre[entry(k, j)], him[entry(k, j)]
                pr, pi = ar * br - ai * bi, ar * bi + ai * br
                acc_re = pr if acc_re is None else acc_re + pr
                acc_im = pi if acc_im is None else acc_im + pi
            out_re.append(acc_re)
            out_im.append(acc_im)
    return out_re, out_im


def moved_algebra(g, link, ahead):
    gre, gim = g[:9], g[9:]
    are, aim = ahead[:9], ahead[9:]
    vre, vim = [None] * 9, [None] * 9
    for i in range(3):
        ur = [link(0, i, k) for k in range(3)]
        ui = [link(1, i, k) for k in range(3)]
        for j in range(3):
            br = [are[entry(j, k)] for k in range(3)]
            bi = [aim[entry(j, k)] for k in range(3)]
            vre[entry(i, j)] = (ur[0] * br[0] + ui[0] * bi[0]) + (
                (ur[1] * br[1] + ui[1] * bi[1]) + (ur[2] * br[2] + ui[2] * bi[2])
            )
            vim[entry(i, j)] = (ui[0] * br[0] - ur[0] * bi[0]) + (
                (ui[1] * br[1] - ur[1] * bi[1]) + (ui[2] * br[2] - ur[2] * bi[2])
            )

    def mreal(i, j):
        return sum(
            gre[entry(i, k)] * vre[entry(k, j)] - gim[entry(i, k)] * vim[entry(k, j)]
            for k in range(3)
        )

    def mimag(i, j):
        return sum(
            gre[entry(i, k)] * vim[entry(k, j)] + gim[entry(i, k)] * vre[entry(k, j)]
            for k in range(3)
        )

    return algebra(mreal, mimag)


PLANE = 18 * 32


def dot(left, right):
    return jnp.dot(left, right, preferred_element_type=F32)


def wide(pieces):
    return jnp.concatenate([three_rows(piece) for piece in pieces], axis=1)


def tile(value, c):
    return value[:, 128 * c : 128 * c + 128]


def encode(sources, stride, coarse, fine, modes, packed, out):
    spectrum = dot(three_lanes(sources[...]), coarse[Z_IN])
    parts = [spectrum[stride * c : stride * c + stride] for c in range(8)]
    mode = dot(coarse[MODES], wide([part[:128] for part in parts]))
    scaled = []
    for c in range(8):
        scaled.append(fine[pl.ds(0, 128), :] * tile(mode, c))
        modes[c] = scaled[c]
    both = [jnp.concatenate([parts[c][:128], scaled[c]], axis=0) for c in range(8)]
    reduced = dot(coarse[REDUCE], wide(both))
    for c in range(8):
        values = tile(reduced, c)
        groups = [values[0:16], values[16:32], values[32:48]]
        if stride > 128:
            groups[1] = groups[1] + parts[c][128:144]
            groups[2] = jnp.concatenate([groups[2][:8], groups[2][8:] + parts[c][144:152]], axis=0)
        for t in range(3):
            packed[pl.ds(128 * t + 16 * c, 16), :] = groups[t]
    for t in range(3):
        out[:, pl.ds(128 * t, 128)] = packed[pl.ds(128 * t, 128), :].T


def first_kernel(links, coarse, fine, out, modes, edge_x, edge_y, theta, prev, sources, packed):
    prev[...] = jnp.zeros_like(prev)
    theta[...] = jnp.zeros_like(theta)
    row = lax.broadcasted_iota(jnp.int32, (16, 128), 0)

    def planes(x, carry):
        def of(mu):
            return algebra(
                lambda i, j: links[18 * mu + entry(i, j), x],
                lambda i, j: links[18 * mu + 9 + entry(i, j), x],
            )

        ax, ay, az = of(0), of(1), of(2)
        comps = []
        for c in range(8):
            back_y = jnp.where(row == 0, 0.0, pltpu.roll(ay[c], 1, 0))
            value = (prev[c] + back_y + pltpu.roll(az[c], 1, 1)) - ax[c] - ay[c] - az[c]
            prev[c] = ax[c]
            comps.append(value)
            sources[pl.ds(152 * c + 16 * x, 16), :] = value
            sources[pl.ds(152 * c + 144 + x, 1), :] = ay[c][15:16]
        inner = jnp.where((row > 0) & (x > 0), squares(comps), 0.0)
        theta[...] += inner[:8] + inner[8:]
        return carry

    lax.fori_loop(0, 8, planes, 0)
    for c in range(8):
        sources[pl.ds(152 * c + 128, 16), :] = prev[c]
        edge_x[c] = sources[pl.ds(152 * c, 16), :]
        edge_y[c] = sources[pl.ds(152 * c, 8, stride=16), :]
    encode(sources, 152, coarse, fine, modes, packed, out)


def plane_kernel(own, recv, coarse, fine, out, work, lines, packed):
    lane = lax.broadcasted_iota(jnp.int32, (16, 128), 1) % 16
    zero = jnp.where(own[0] == 0, -1.0 / (LS * LS), 0.0)
    total = fine[pl.ds(ZERO_ROW, 128), :] + fine[pl.ds(ZERO_ROW + own[0], 1), :][:, 0:1]
    inverse = jnp.where(total > 0.0, 1.0 / jnp.where(total > 0.0, total, 1.0), 0.0)
    shifts = []
    for t in range(3):
        packed[pl.ds(128 * t, 128), :] = recv[:, pl.ds(128 * t, 128)]
    moved = [
        swap_blocks([packed[pl.ds(128 * t + g, 16, stride=8), :] for g in range(8)])
        for t in range(3)
    ]
    for c in range(8):
        third = moved[2][c]
        rolled = pltpu.roll(third, 8, 1)
        first = moved[0][c] + pltpu.roll(moved[1][c], 1, 0) + jnp.where(lane == 0, rolled, 0.0)
        work[pl.ds(16 * c, 16), :] = first
        both = third + rolled
        for x in range(1, 8):
            work[pl.ds(128 * x + 16 * c, 16), :] = jnp.where(lane == x, both, 0.0)
        extra = jnp.sum(jnp.where(lane == 0, third, 0.0), axis=0, keepdims=True)
        shifts.append(jnp.sum(extra, axis=1, keepdims=True) * zero)
    lines[pl.ds(0, 128), :] = dot(three_lanes(work[pl.ds(0, 128), :]), coarse[Y_IN])
    lines[pl.ds(128, 896), :] = dot(three_lanes(work[pl.ds(128, 896), :]), coarse[LINES_IN])
    blocks = [
        jnp.concatenate([lines[pl.ds(128 * x + 16 * c, 16), :] for x in range(8)], axis=0)
        for c in range(8)
    ]
    spectrum = dot(coarse[X_IN], wide(blocks))
    spectrum = dot(coarse[X_OUT], wide([tile(spectrum, c) * inverse for c in range(8)]))
    spectrum = [tile(spectrum, c) for c in range(8)]
    at_lines = dot(three_lanes(jnp.concatenate(spectrum, axis=0)), coarse[LINES_OUT])
    first = jnp.concatenate([part[:16] for part in spectrum], axis=0)
    first = dot(three_lanes(first), coarse[Z_OUT])
    groups = [[], [], []]
    for c in range(8):
        own_line = first[16 * c : 16 * c + 16] + shifts[c]
        groups[0].append(own_line)
        groups[1].append(pltpu.roll(own_line, 15, 0))
        parts = [at_lines[128 * c + 16 * x : 128 * c + 16 * x + 16] for x in range(8)]
        third = jnp.where(lane == 0, pltpu.roll(parts[7], 1, 0), parts[0])
        for x in range(1, 8):
            third = jnp.where((lane == x) | (lane == 8 + x), parts[x], third)
        groups[2].append(third + shifts[c])
    for t in range(3):
        tiles = swap_blocks(groups[t])
        for g in range(8):
            packed[pl.ds(128 * t + g, 16, stride=8), :] = tiles[g]
        out[:, pl.ds(128 * t, 128)] = packed[pl.ds(128 * t, 128), :]


def decode(recv, modes, coarse, fine, packed, comps_in):
    for t in range(3):
        packed[pl.ds(128 * t, 128), :] = recv[:, pl.ds(128 * t, 128)].T
    mass = fine[pl.ds(ZERO_ROW, 1), :]
    values = [
        jnp.concatenate([packed[pl.ds(128 * t + 16 * c, 16), :] for t in range(3)], axis=0)
        for c in range(8)
    ]
    mode = dot(coarse[SOURCE], wide(values))
    stacks = []
    for c in range(8):
        own = modes[c] + fine[pl.ds(0, 128), :] * tile(mode, c)
        stacks.append(jnp.concatenate([own, values[c], values[c] * mass], axis=0))
    sites = dot(coarse[EXPAND], wide(stacks))
    sites = jnp.concatenate([tile(sites, c) for c in range(8)], axis=0)
    comps_in[...] = dot(three_lanes(sites), coarse[Z_OUT])


def update_body(last, refs):
    recv, modes, edge_x, edge_y, links, face_x, face_y, theta_in, coarse, fine = refs[:10]
    refs = refs[10:]
    if last:
        prior, prior_y, theta_first, div, gauge, theta = refs[:6]
        packed, comps_in, gs, edge_g, ay, prev, acc = refs[6:]
    else:
        out, modes_out, edge_x_out, edge_y_out, theta, gout, gout_y, theta_out = refs[:8]
        packed, comps_in, gs, edge_g, ay, prev, acc, sources = refs[8:]
    decode(recv, modes, coarse, fine, packed, comps_in)

    add_x = add_y = None
    if not last:
        add_x = algebra(lambda i, j: face_x[entry(i, j)], lambda i, j: face_x[9 + entry(i, j)])
        add_y = algebra(lambda i, j: face_y[entry(i, j)], lambda i, j: face_y[9 + entry(i, j)])
    whole_x, whole_y = [], []
    row = lax.broadcasted_iota(jnp.int32, (16, 128), 0)
    for c in range(8):
        line_x, line_y = edge_x[c], edge_y[c]
        if not last:
            top = row == 0
            line_x = line_x + add_x[c] + jnp.where(top, add_y[c][0:1], 0.0)
            line_y = line_y + add_y[c] + jnp.where(top[:8], add_x[c][0:1], 0.0)
        whole_x.append(line_x)
        whole_y.append(line_y)
        behind = pl.ds(176 * c + 144, 16)
        comps_in[behind, :] = comps_in[behind, :] - jnp.where(row == 0, 0.0, SCALE * line_x)
        below = pl.ds(176 * c + 168, 8)
        comps_in[below, :] = comps_in[below, :] - SCALE * line_y
    if not last:
        sq = squares(whole_x)
        theta_out[...] = (
            theta_in[...] + sq[:8] + sq[8:] + jnp.where(row[:8] == 0, 0.0, squares(whole_y))
        )

    def make(c, before):
        re6, im6 = exponent_rows(c)
        if before is not None:
            re6, im6 = times_rows(re6, im6, before[:9], before[9:])
        return full_matrix(re6, im6)

    def plane(index, first_row, inside):
        for half in range(2):
            rows = pl.ds(8 * half, 8)
            before = [prior[index, k, rows, :] for k in range(18)] if last else None
            g = make([comps_in[pl.ds(first_row(c) + 8 * half, 8), :] for c in range(8)], before)
            for k in range(18):
                gs[pl.ds(index * PLANE + 32 * k + 8 * half + 8, 8), :] = g[k]
                if not last:
                    gout[index, k, rows, :] = g[k]
            if last and inside:
                for p in range(2):
                    for i in range(2):
                        for j in range(3):
                            gauge[p, i, j, index - 1, rows, :] = g[9 * p + entry(i, j)]

    def inner(x, carry):
        plane(x + 1, lambda c: 176 * c + 16 * x, True)
        return carry

    lax.fori_loop(0, 8, inner, 0)
    plane(0, lambda c: 176 * c + 144, False)
    plane(9, lambda c: 176 * c + 128, False)
    for side in range(2):
        c = [comps_in[pl.ds(176 * k + 168 - 8 * side, 8), :] for k in range(8)]
        before = [prior_y[side, k] for k in range(18)] if last else None
        g = make(c, before)
        for k in range(18):
            if not last:
                gout_y[side, k] = g[k]
            if side == 0:
                edge_g[k] = g[k]
            else:
                gs[pl.ds(PLANE + 32 * k + 24, 8, stride=PLANE), :] = g[k]

    g = [edge_g[k] for k in range(18)]
    ahead = [gs[pl.ds(PLANE + 32 * k + 8, 8, stride=PLANE), :] for k in range(18)]
    edge = moved_algebra(g, lambda p, i, j: face_y[9 * p + entry(i, j)], ahead)
    for c in range(8):
        ay[pl.ds(24 * c + 7, 8, stride=192), :] = edge[c]
    for half in range(2):
        rows = pl.ds(8 * half, 8)
        start = 8 * half + 8
        g = [gs[pl.ds(32 * k + start, 8), :] for k in range(18)]
        ahead = [gs[pl.ds(PLANE + 32 * k + start, 8), :] for k in range(18)]
        edge = moved_algebra(g, lambda p, i, j: face_x[9 * p + entry(i, j), rows, :], ahead)
        for c in range(8):
            prev[c, rows, :] = edge[c]

    acc[...] = jnp.zeros_like(acc)

    def sites(x, carry):
        base = (x + 1) * PLANE
        for half in range(2):
            rows = pl.ds(8 * half, 8)
            start = 8 * half + 8
            total = [None] * 8

            def link_of(mu):
                return lambda p, i, j: links[18 * mu + 9 * p + entry(i, j), x, rows, :]

            g = [gs[pl.ds(base + 32 * k + start, 8), :] for k in range(18)]
            ahead = [gs[pl.ds(base + PLANE + 32 * k + start, 8), :] for k in range(18)]
            a = moved_algebra(g, link_of(0), ahead)
            for c in range(8):
                total[c] = prev[c, rows, :] - a[c]
                prev[c, rows, :] = a[c]
            ahead = [gs[pl.ds(base + 32 * k + start + 1, 8), :] for k in range(18)]
            a = moved_algebra(g, link_of(1), ahead)
            for c in range(8):
                ay[pl.ds(x * 192 + 24 * c + start, 8), :] = a[c]
            for c in range(8):
                total[c] = total[c] + (ay[pl.ds(x * 192 + 24 * c + start - 1, 8), :] - a[c])
            ahead = [pltpu.roll(v, 127, 1) for v in g]
            a = moved_algebra(g, link_of(2), ahead)
            for c in range(8):
                total[c] = total[c] + (pltpu.roll(a[c], 1, 1) - a[c])
                if last:
                    div[c, x, rows, :] = total[c]
                else:
                    sources[pl.ds(128 * c + 16 * x + 8 * half, 8), :] = total[c]
            acc[...] += squares(total)
        return carry

    lax.fori_loop(0, 8, sites, 0)
    if last:
        lane = lax.broadcasted_iota(jnp.int32, (1, 128), 1)
        sums = jnp.zeros((1, 128), F32)
        for k, part in enumerate((theta_first, theta_in, acc)):
            sums = sums + jnp.where(lane == k, jnp.sum(part[...]), 0.0)
        theta[...] = jnp.broadcast_to(sums, (128, 128))
    else:
        theta[...] = acc[...]
        for c in range(8):
            edge_x_out[c] = sources[pl.ds(128 * c, 16), :]
            edge_y_out[c] = sources[pl.ds(128 * c, 8, stride=16), :]
        encode(sources, 128, coarse, fine, modes_out, packed, out)


def update_kernel(*refs):
    update_body(False, refs)


def last_kernel(*refs):
    update_body(True, refs)


def struct(*shape):
    return jax.ShapeDtypeStruct(shape, F32)


def vmem(*shape):
    return pltpu.VMEM(shape, F32)


def whole():
    return pl.BlockSpec(memory_space=pltpu.VMEM)


def params(size):
    return pltpu.CompilerParams(vmem_limit_bytes=size * MEGA)


EDGES = [(8, 16, 128), (8, 8, 128)]


def first_call(links, tables):
    shapes = [struct(128, 384), struct(8, 128, 128)] + [struct(*e) for e in EDGES] + [struct(8, 128)]
    return pl.pallas_call(
        first_kernel,
        in_specs=[whole()] * 3,
        out_specs=[whole()] * len(shapes),
        out_shape=shapes,
        scratch_shapes=[vmem(8, 16, 128), vmem(8 * 152, 128), vmem(384, 128)],
        compiler_params=params(32),
        name="first_divergence",
    )(links, *tables)


def plane_call(own, recv, tables):
    return pl.pallas_call(
        plane_kernel,
        in_specs=[pl.BlockSpec(memory_space=pltpu.SMEM)] + [whole()] * 3,
        out_specs=whole(),
        out_shape=struct(128, 384),
        scratch_shapes=[vmem(1024, 128), vmem(1024, 128), vmem(384, 128)],
        compiler_params=params(32),
        name="plane_solve",
    )(own, recv, *tables)


def update_call(recv, state, links, face_x, face_y, tables, prior):
    last = prior is not None
    modes, edge_x, edge_y, theta = state
    operands = [recv, modes, edge_x, edge_y, links, face_x, face_y, theta] + list(tables)
    scratch = [
        vmem(384, 128),
        vmem(8 * 176, 128),
        vmem(10 * PLANE, 128),
        vmem(18, 8, 128),
        vmem(8 * 192, 128),
        vmem(8, 16, 128),
        vmem(8, 128),
    ]
    if last:
        shapes = [struct(8, 8, 16, 128), struct(2, 2, 3, 8, 16, 128), struct(128, 128)]
        operands += list(prior)
    else:
        shapes = [struct(128, 384), struct(8, 128, 128)] + [struct(*e) for e in EDGES]
        shapes += [struct(8, 128), struct(10, 18, 16, 128), struct(2, 18, 8, 128), struct(8, 128)]
        scratch += [vmem(8 * 128, 128)]
    return pl.pallas_call(
        last_kernel if last else update_kernel,
        in_specs=[whole()] * len(operands),
        out_specs=[whole()] * len(shapes),
        out_shape=shapes,
        scratch_shapes=scratch,
        compiler_params=params(32),
        name="last_update" if last else "update",
    )(*operands)


def shifted(value, axis, steps):
    count = lax.axis_size(axis)
    pairs = [(source, (source + steps) % count) for source in range(count)]
    return lax.ppermute(value, axis, pairs)


def exchange(value):
    return lax.all_to_all(value, ("gx", "gy"), split_axis=0, concat_axis=0, tiled=True)


def per_device(links):
    face_x = shifted(links[0, :, :, :, 7].reshape(18, 16, 128), "gx", 1)
    face_y = shifted(links[1, :, :, :, :, 15].reshape(18, 8, 128), "gy", 1)
    flat = links.reshape(54, 8, 16, 128)
    own = (lax.axis_index("gx") * 8 + lax.axis_index("gy")).astype(jnp.int32).reshape(1)
    tables = (jnp.asarray(COARSE), jnp.asarray(FINE))
    packed, *state = first_call(flat, tables)
    packed, face_x, face_y, own = lax.optimization_barrier((packed, face_x, face_y, own))
    prior = None
    for step in range(2):
        values = exchange(plane_call(own, exchange(packed), tables))
        results = update_call(values, state, flat, face_x, face_y, tables, prior)
        if step == 0:
            packed, modes, edge_x, edge_y, theta, gout, gout_y, theta_first = results
            state = (modes, edge_x, edge_y, theta)
            prior = (gout, gout_y, theta_first)
    div, gauge, sums = results
    sums = jnp.sum(exchange(sums), axis=0)[:3] / (3.0 * LS * LS * NZ)
    return (gauge, div, sums)


def solution(mesh):
    in_specs = (P(None, None, None, None, "gx", "gy", "ta"),)
    out_specs = (P(None, None, None, "gx", "gy", "ta"), P(None, "gx", "gy", "ta"), P("ta"))
    return jax.shard_map(
        per_device, mesh=mesh, in_specs=in_specs, out_specs=out_specs, check_vma=False
    )
```

time: 227 us -> 171 us (0.75)
  starting transfers between devices: 34.8 us -> 6.44 us
  waiting for transfers between devices: 28.9 us -> 1.93 us
  blocking collectives: 112 us -> 134 us
  local copies, waits for them, and re-layouts: 22.2 us -> 7.17 us
  Pallas kernels: 24.9 us -> 19.1 us
    all_to_all x3 -> x0, starting transfers between devices: 23.4 us -> none  [exchange(): return lax.all_to_all(value, axis, split_axis=0, concat_axis=0, tiled=True)]
    all_to_all x7 -> x5, blocking collectives: 112 us -> 134 us  [exchange(): lax.all_to_all(value, ('gx', 'gy'), split_axis=0, concat_axis=0, tiled=True)]
    all_to_all x3 -> x0, waiting for transfers between devices: 18.3 us -> none  [exchange(): return lax.all_to_all(value, axis, split_axis=0, concat_axis=0, tiled=True)]
    unnamed x52 -> x14, local copies, waits for them, and re-layouts: 16.2 us -> 4.29 us
    ppermute x4 -> x2, waiting for transfers between devices: 10.6 us -> 1.93 us  [shifted(): return lax.ppermute(value, axis, pairs)]
    pallas_call x9 -> x5, Pallas kernels: 24.9 us -> 19.1 us  [the longest x2 13.7 us: update_call(): pl.pallas_call(last_kernel if last else update_kernel, in_specs=[whole()]...]
    ppermute x4 -> x2, starting transfers between devices: 11.4 us -> 6.44 us  [shifted(): return lax.ppermute(value, axis, pairs)]
    another operation x2 -> x0, local copies, waits for them, and re-layouts: 2.45 us -> none  [per_device(): ring = jnp.tile(ring, (1, 1, 8))]
  transfers between devices with their start and end apart: 7 -> 2, of which waited for: 6 -> 1; matrix products, arithmetic and copies ran while one was open for 3% -> 1% of each run, Pallas kernels for 0% -> 1%
where the time goes in v2:
time: 171 us; the launch traced here: 170 us
  blocking collectives  134 us (78%)
  Pallas kernels  19.1 us (11%)
  local copies, waits for them, and re-layouts  7.17 us (4%)
  starting transfers between devices  6.44 us (4%)
  waiting for transfers between devices  1.93 us (1%)
    all_to_all x5, blocking collectives, exchange(): lax.all_to_all(value, ('gx', 'gy'), split_axis=0, concat_axis=0, tiled=True)  134 us
    pallas_call x2, Pallas kernels, update_call(): pl.pallas_call(last_kernel if last else update_kernel, in_specs=[whole()]...  13.7 us
    ppermute x2, starting transfers between devices, shifted(): return lax.ppermute(value, axis, pairs)  6.44 us
    unnamed x14, local copies, waits for them, and re-layouts  4.29 us
    pallas_call x2, Pallas kernels, plane_call(): pl.pallas_call(plane_kernel, in_specs=[pl.BlockSpec(memory_space=pltpu.SM...  3.62 us
  transfers between devices with their start and end apart: 2, of which 1 were waited for; matrix products, arithmetic and copies ran while one was open for 1% of the time, Pallas kernels for 1%

profile of v2, /device:TPU:1, one launch (start us, length us, event | category | flops | bytes accessed | tf_op | source)
XLA Modules:
  0.0 170.1 jit_solution(15592808780494588611)
XLA Ops:
  0.6 0.9 slice.9
  1.6 4.4 %collective-permute-start = (f32[18,16,128]{2,1,0:T(8,128)S(1)}, f32[18,16,128]{2,1,0:T(8,128)S(1)}, u32[]{:S(2)}, u32[]{:S(2)}) collective-permute-start(f32[18,16,128]{2,1,0:T(8,128)S(1)} %bitcast.35), channel_id=1, source_target_pairs={{0,8},{8,16},{16,24},{24,32},{32,40},{40,48},{48,56},{56,64},{64,7... | collective-permute-start | bytes 442376 | tf_op jit(solution)/shard_map/ppermute | solution.py:707
  5.9 1.1 slice.10
  7.1 2.1 %collective-permute-start.1 = (f32[18,8,128]{2,1,0:T(8,128)S(1)}, f32[18,8,128]{2,1,0:T(8,128)S(1)}, u32[]{:S(2)}, u32[]{:S(2)}) collective-permute-start(f32[18,8,128]{2,1,0:T(8,128)S(1)} %bitcast.36), channel_id=1, source_target_pairs={{0,1},{1,2},{2,3},{3,4},{4,5},{5,6},{6,7},{7,0},{8,9},{9,10},{10,1... | collective-permute-start | bytes 221192 | tf_op jit(solution)/shard_map/ppermute | solution.py:707
  9.1 0.0 copy-start
  9.1 2.0 %copy-done = f32[3,2,3,3,8,16,128]{6,5,4,3,2,1,0:T(8,128)S(1)} copy-done((f32[3,2,3,3,8,16,128]{6,5,4,3,2,1,0:T(8,128)S(1)}, f32[3,2,3,3,8,16,128]{6,5,4,3,2,1,0:T(8,128)}, u32[]{:S(2)}) %copy-start) | copy-done | bytes 3538968
  11.1 0.0 copy-start.2
  11.1 1.3 copy-done.2
  12.5 0.0 copy-start.4
  12.5 0.9 copy-done.4
  13.4 0.0 copy-start.3
  13.4 1.8 %first_divergence.1 = (f32[128,384]{1,0:T(8,128)S(1)}, f32[8,128,128]{2,1,0:T(8,128)S(1)}, f32[8,16,128]{2,1,0:T(8,128)S(1)}, f32[8,8,128]{2,1,0:T(8,128)S(1)}, f32[8,128]{1,0:T(8,128)S(1)}) custom-call(f32[54,8,16,128]{3,2,1,0:T(8,128)S(1)} %bitcast.23, bf16[864,768]{1,0:T(8,128)(2,1)S(1)} %copy-done.2, f32[256,128]{1,0:T(8,128)S(1)} %copy-done.4), custom_call_target="tpu_custom_call" | custom-call | tf_op jit(solution)/shard_map/first_divergence/pallas_call | solution.py:650
  15.1 0.0 collective-permute-done.1.refs_6_
  15.2 1.9 %collective-permute-done.refs_5_ = f32[18,16,128]{2,1,0:T(8,128)S(1)} collective-permute-done((f32[18,16,128]{2,1,0:T(8,128)S(1)}, f32[18,16,128]{2,1,0:T(8,128)S(1)}, u32[]{:S(2)}, u32[]{:S(2)}) %collective-permute-start) | collective-permute-done | bytes 147488 | tf_op jit(solution)/shard_map/ppermute | solution.py:707
  17.1 0.2 copy.6
  17.3 0.0 copy-start.1
  17.3 34.0 %all_to_all.53 = f32[128,1,384]{2,1,0:T(1,128)S(1)} all-to-all(f32[128,1,384]{2,1,0:T(1,128)S(1)} %copy.6), channel_id=1, replica_groups=mesh['ta'=4,'gx'=16,'gy'=8] {'gx','gy'}, dimensions={0} | all-to-all | bytes 393216 | tf_op jit(solution)/shard_map/all_to_all | solution.py:711
  51.3 1.8 %plane_solve.2 = f32[128,384]{1,0:T(8,128)S(1)} custom-call(s32[1]{0:T(128)} %bitcast.3.own, f32[128,384]{1,0:T(8,128)S(1)} %bitcast.29, bf16[864,768]{1,0:T(8,128)(2,1)S(1)} %copy-done.2, f32[256,128]{1,0:T(8,128)S(1)} %copy-done.4), custom_call_target="tpu_custom_call" | custom-call | tf_op jit(solution)/shard_map/plane_solve/pallas_call | solution.py:662
  53.1 0.2 copy.7
  53.3 25.8 %all_to_all.54 = f32[128,1,384]{2,1,0:T(1,128)S(1)} all-to-all(f32[128,1,384]{2,1,0:T(1,128)S(1)} %copy.7), channel_id=1, replica_groups=mesh['ta'=4,'gx'=16,'gy'=8] {'gx','gy'}, dimensions={0} | all-to-all | bytes 393216 | tf_op jit(solution)/shard_map/all_to_all | solution.py:711
  79.1 0.0 copy-done.3
  79.2 0.0 copy-done.1
  79.2 6.8 %update.1 = (f32[128,384]{1,0:T(8,128)S(1)}, f32[8,128,128]{2,1,0:T(8,128)S(1)}, f32[8,16,128]{2,1,0:T(8,128)S(1)}, f32[8,8,128]{2,1,0:T(8,128)S(1)}, f32[8,128]...) custom-call(f32[128,384]{1,0:T(8,128)S(1)} %bitcast.26, ...), custom_call_target="tpu_custom_call" | custom-call | tf_op jit(solution)/shard_map/update/pallas_call | solution.py:693
  85.9 0.2 copy.8
  86.1 25.8 %all_to_all.55 = f32[128,1,384]{2,1,0:T(1,128)S(1)} all-to-all(f32[128,1,384]{2,1,0:T(1,128)S(1)} %copy.8), channel_id=1, replica_groups=mesh['ta'=4,'gx'=16,'gy'=8] {'gx','gy'}, dimensions={0} | all-to-all | bytes 393216 | tf_op jit(solution)/shard_map/all_to_all | solution.py:711
  112.0 1.8 %plane_solve.3 = f32[128,384]{1,0:T(8,128)S(1)} custom-call(s32[1]{0:T(128)} %bitcast.3.own, f32[128,384]{1,0:T(8,128)S(1)} %bitcast.27, bf16[864,768]{1,0:T(8,128)(2,1)S(1)} %copy-done.3, f32[256,128]{1,0:T(8,128)S(1)} %copy-done.4), custom_call_target="tpu_custom_call" | custom-call | tf_op jit(solution)/shard_map/plane_solve/pallas_call | solution.py:662
  113.8 0.2 copy.9
  114.0 25.8 %all_to_all.56 = f32[128,1,384]{2,1,0:T(1,128)S(1)} all-to-all(f32[128,1,384]{2,1,0:T(1,128)S(1)} %copy.9), channel_id=1, replica_groups=mesh['ta'=4,'gx'=16,'gy'=8] {'gx','gy'}, dimensions={0} | all-to-all | bytes 393216 | tf_op jit(solution)/shard_map/all_to_all | solution.py:711
  139.8 7.0 %last_update.1 = (f32[8,8,16,128]{3,2,1,0:T(8,128)}, f32[2,2,3,8,16,128]{5,4,3,2,1,0:T(8,128)}, f32[128,128]{1,0:T(8,128)S(1)}) custom-call(f32[128,384]{1,0:T(8,128)S(1)} %bitcast.31, f32[8,128,128]{2,1,0:T(8,128)S(1)} %get-tuple-element.33.refs_1_, f32[8,16,128]{2,1,0:T(8,128)S(1)} %get-tuple-element.34.refs_2_, ...), custom_call_target="tpu_custom_call" | custom-call | tf_op jit(solution)/shard_map/last_update/pallas_call | solution.py:693
  146.7 22.7 %all_to_all.57 = f32[128,1,128]{2,1,0:T(1,128)S(1)} all-to-all(f32[128,1,128]{2,1,0:T(1,128)S(1)} %bitcast.34), channel_id=1, replica_groups=mesh['ta'=4,'gx'=16,'gy'=8] {'gx','gy'}, dimensions={0} | all-to-all | bytes 131072 | tf_op jit(solution)/shard_map/all_to_all | solution.py:711
  169.4 0.2 reduce_sum.9
  169.6 0.5 slice_multiply_fusion
  (4 shorter events, 0.1 us)
Async XLA Ops:
  1.6 15.5 %collective-permute-start = (f32[18,16,128]{2,1,0:T(8,128)S(1)}, f32[18,16,128]{2,1,0:T(8,128)S(1)}, u32[]{:S(2)}, u32[]{:S(2)}) collective-permute-start(f32[18,16,128]{2,1,0:T(8,128)S(1)} %bitcast.35), channel_id=1, source_target_pairs={{0,8},{8,16},{16,24},{24,32},{32,40},{40,48},{48,56},{56,64},{64,7... | collective-permute-start | bytes 442376 | tf_op jit(solution)/shard_map/ppermute | solution.py:707
  7.1 8.1 %collective-permute-start.1 = (f32[18,8,128]{2,1,0:T(8,128)S(1)}, f32[18,8,128]{2,1,0:T(8,128)S(1)}, u32[]{:S(2)}, u32[]{:S(2)}) collective-permute-start(f32[18,8,128]{2,1,0:T(8,128)S(1)} %bitcast.36), channel_id=1, source_target_pairs={{0,1},{1,2},{2,3},{3,4},{4,5},{5,6},{6,7},{7,0},{8,9},{9,10},{10,1... | collective-permute-start | bytes 221192 | tf_op jit(solution)/shard_map/ppermute | solution.py:707
  9.1 2.0 %copy-start = (f32[3,2,3,3,8,16,128]{6,5,4,3,2,1,0:T(8,128)S(1)}, f32[3,2,3,3,8,16,128]{6,5,4,3,2,1,0:T(8,128)}, u32[]{:S(2)}) copy-start(f32[3,2,3,3,8,16,128]{6,5,4,3,2,1,0:T(8,128)} %param.3) | copy-start | bytes 10616836
  11.1 1.3 copy-start.2
  12.5 0.9 copy-start.4
  13.4 65.8 %copy-start.3 = (bf16[864,768]{1,0:T(8,128)(2,1)S(1)}, bf16[864,768]{1,0:T(8,128)(2,1)}, u32[]{:S(2)}) copy-start(bf16[864,768]{1,0:T(8,128)(2,1)} %constant.20.clone.coarse.refs_8_) | copy-start | bytes 3981316
  17.3 61.9 %copy-start.1 = (f32[3,2,3,3,8,16,128]{6,5,4,3,2,1,0:T(8,128)S(1)}, f32[3,2,3,3,8,16,128]{6,5,4,3,2,1,0:T(8,128)}, u32[]{:S(2)}) copy-start(f32[3,2,3,3,8,16,128]{6,5,4,3,2,1,0:T(8,128)} %param.3) | copy-start | bytes 10616836

commit v3 on v2

--- a/solution.py
+++ b/solution.py
@@ -155,7 +155,7 @@
 
 
 def pack_tables():
-    out = np.zeros((864, 768), jnp.bfloat16)
+    out = np.zeros((992, 768), jnp.bfloat16)
     rights = (BASIS * SCALE, BASIS.T, BASIS, lines_in(), lines_out())
     for k, table in enumerate(rights):
         out[:384, 128 * k : 128 * k + 128] = right_table(table)
@@ -165,13 +165,19 @@
     out[512:640, 384:528] = left_table(source_table())
     out[640:688, :] = left_table(reduce_table())
     out[688:864, :672] = left_table(expand_table())
+    for k, table in enumerate((INVERSE, PLANE_SUM)):
+        rest = table.astype(np.float32).astype(np.float64)
+        for part in range(3):
+            piece = rest.astype(np.float32).astype(jnp.bfloat16)
+            lanes = 384 * k + 128 * part
+            out[864:992, lanes : lanes + 128] = piece
+            rest = rest - piece.astype(np.float64)
     return out
 
 
-COARSE = pack_tables()
 INVERSE = INNER[:, None] / (np.where(INNER, EIGEN, 1.0)[:, None] + SQUARES[None, :])
 PLANE_SUM = SQUARES[:, None] + SQUARES[None, :]
-FINE = np.concatenate([INVERSE, PLANE_SUM]).astype(np.float32)
+TABLE = pack_tables()
 Z_IN, Z_OUT, Y_IN, LINES_IN, LINES_OUT = [(slice(0, 384), slice(128 * k, 128 * k + 128)) for k in range(5)]
 MODES = (slice(384, 512), slice(0, 384))
 X_IN = (slice(384, 512), slice(384, 768))
@@ -179,7 +185,14 @@
 SOURCE = (slice(512, 640), slice(384, 528))
 REDUCE = (slice(640, 688), slice(0, 768))
 EXPAND = (slice(688, 864), slice(0, 672))
-ZERO_ROW = 128
+
+
+def float_table(table, which, rows=128):
+    parts = [
+        table[864 : 864 + rows, 384 * which + 128 * k : 384 * which + 128 * k + 128].astype(F32)
+        for k in range(3)
+    ]
+    return (parts[0] + parts[1]) + parts[2]
 
 
 def three_lanes(value):
@@ -271,7 +284,7 @@
     r1 = [-c2 + 0.5 * p01r, s11, c6 + 0.5 * p12r]
     i1 = [c3 - 0.5 * p01i, c1, c7 + 0.5 * p12i]
     size = sum(r0[k] * r0[k] + i0[k] * i0[k] for k in range(3))
-    scale = 1.0 / jnp.sqrt(size)
+    scale = lax.rsqrt(size)
     r0 = [v * scale for v in r0]
     i0 = [v * scale for v in i0]
     pr = sum(r0[k] * r1[k] + i0[k] * i1[k] for k in range(3))
@@ -281,7 +294,7 @@
         [i1[k] - (pr * i0[k] + pi * r0[k]) for k in range(3)],
     )
     size = sum(r1[k] * r1[k] + i1[k] * i1[k] for k in range(3))
-    scale = 1.0 / jnp.sqrt(size)
+    scale = lax.rsqrt(size)
     r1 = [v * scale for v in r1]
     i1 = [v * scale for v in i1]
     return r0 + r1, i0 + i1
@@ -312,7 +325,7 @@
     gre, gim = g[:9], g[9:]
     are, aim = ahead[:9], ahead[9:]
     vre, vim = [None] * 9, [None] * 9
-    for i in range(3):
+    for i in range(2):
         ur = [link(0, i, k) for k in range(3)]
         ui = [link(1, i, k) for k in range(3)]
         for j in range(3):
@@ -325,6 +338,8 @@
                 (ui[1] * br[1] - ur[1] * bi[1]) + (ui[2] * br[2] - ur[2] * bi[2])
             )
 
+    vre[6:], vim[6:] = cross_row(vre[:3], vim[:3], vre[3:6], vim[3:6])
+
     def mreal(i, j):
         return sum(
             gre[entry(i, k)] * vre[entry(k, j)] - gim[entry(i, k)] * vim[entry(k, j)]
@@ -355,16 +370,17 @@
     return value[:, 128 * c : 128 * c + 128]
 
 
-def encode(sources, stride, coarse, fine, modes, packed, out):
-    spectrum = dot(three_lanes(sources[...]), coarse[Z_IN])
+def encode(sources, stride, table, modes, packed, out):
+    spectrum = dot(three_lanes(sources[...]), table[Z_IN])
     parts = [spectrum[stride * c : stride * c + stride] for c in range(8)]
-    mode = dot(coarse[MODES], wide([part[:128] for part in parts]))
+    mode = dot(table[MODES], wide([part[:128] for part in parts]))
+    inverse = float_table(table, 0)
     scaled = []
     for c in range(8):
-        scaled.append(fine[pl.ds(0, 128), :] * tile(mode, c))
+        scaled.append(inverse * tile(mode, c))
         modes[c] = scaled[c]
     both = [jnp.concatenate([parts[c][:128], scaled[c]], axis=0) for c in range(8)]
-    reduced = dot(coarse[REDUCE], wide(both))
+    reduced = dot(table[REDUCE], wide(both))
     for c in range(8):
         values = tile(reduced, c)
         groups = [values[0:16], values[16:32], values[32:48]]
@@ -377,16 +393,28 @@
         out[:, pl.ds(128 * t, 128)] = packed[pl.ds(128 * t, 128), :].T
 
 
-def first_kernel(links, coarse, fine, out, modes, edge_x, edge_y, theta, prev, sources, packed):
+def first_kernel(*refs):
+    links_hbm, table_hbm, out, modes, edge_x, edge_y, theta, table, face_x, face_y = refs[:10]
+    links, prev, sources, packed, sems = refs[10:]
+
+    def plane_copy(x):
+        return pltpu.make_async_copy(links_hbm.at[:, x], links.at[x], sems.at[x])
+
+    for x in range(8):
+        plane_copy(x).start()
+    table_copy = pltpu.make_async_copy(table_hbm, table, sems.at[8])
+    table_copy.start()
     prev[...] = jnp.zeros_like(prev)
     theta[...] = jnp.zeros_like(theta)
     row = lax.broadcasted_iota(jnp.int32, (16, 128), 0)
 
     def planes(x, carry):
+        plane_copy(x).wait()
+
         def of(mu):
             return algebra(
-                lambda i, j: links[18 * mu + entry(i, j), x],
-                lambda i, j: links[18 * mu + 9 + entry(i, j), x],
+                lambda i, j: links[x, 18 * mu + entry(i, j)],
+                lambda i, j: links[x, 18 * mu + 9 + entry(i, j)],
             )
 
         ax, ay, az = of(0), of(1), of(2)
@@ -398,6 +426,8 @@
             comps.append(value)
             sources[pl.ds(152 * c + 16 * x, 16), :] = value
             sources[pl.ds(152 * c + 144 + x, 1), :] = ay[c][15:16]
+        for k in range(12):
+            face_y[k, pl.ds(x, 1), :] = links[x, 18 + k % 6 + 9 * (k // 6), 15:16, :]
         inner = jnp.where((row > 0) & (x > 0), squares(comps), 0.0)
         theta[...] += inner[:8] + inner[8:]
         return carry
@@ -407,13 +437,18 @@
         sources[pl.ds(152 * c + 128, 16), :] = prev[c]
         edge_x[c] = sources[pl.ds(152 * c, 16), :]
         edge_y[c] = sources[pl.ds(152 * c, 8, stride=16), :]
-    encode(sources, 152, coarse, fine, modes, packed, out)
-
-
-def plane_kernel(own, recv, coarse, fine, out, work, lines, packed):
+    for k in range(12):
+        face_x[k] = links[7, k % 6 + 9 * (k // 6)]
+    table_copy.wait()
+    encode(sources, 152, table, modes, packed, out)
+
+
+def plane_kernel(own, recv, table, out, work, lines, packed):
     lane = lax.broadcasted_iota(jnp.int32, (16, 128), 1) % 16
     zero = jnp.where(own[0] == 0, -1.0 / (LS * LS), 0.0)
-    total = fine[pl.ds(ZERO_ROW, 128), :] + fine[pl.ds(ZERO_ROW + own[0], 1), :][:, 0:1]
+    total = float_table(table, 1)
+    work[pl.ds(0, 128), :] = total
+    total = total + work[pl.ds(own[0], 1), :][:, 0:1]
     inverse = jnp.where(total > 0.0, 1.0 / jnp.where(total > 0.0, total, 1.0), 0.0)
     shifts = []
     for t in range(3):
@@ -432,18 +467,18 @@
             work[pl.ds(128 * x + 16 * c, 16), :] = jnp.where(lane == x, both, 0.0)
         extra = jnp.sum(jnp.where(lane == 0, third, 0.0), axis=0, keepdims=True)
         shifts.append(jnp.sum(extra, axis=1, keepdims=True) * zero)
-    lines[pl.ds(0, 128), :] = dot(three_lanes(work[pl.ds(0, 128), :]), coarse[Y_IN])
-    lines[pl.ds(128, 896), :] = dot(three_lanes(work[pl.ds(128, 896), :]), coarse[LINES_IN])
+    lines[pl.ds(0, 128), :] = dot(three_lanes(work[pl.ds(0, 128), :]), table[Y_IN])
+    lines[pl.ds(128, 896), :] = dot(three_lanes(work[pl.ds(128, 896), :]), table[LINES_IN])
     blocks = [
         jnp.concatenate([lines[pl.ds(128 * x + 16 * c, 16), :] for x in range(8)], axis=0)
         for c in range(8)
     ]
-    spectrum = dot(coarse[X_IN], wide(blocks))
-    spectrum = dot(coarse[X_OUT], wide([tile(spectrum, c) * inverse for c in range(8)]))
+    spectrum = dot(table[X_IN], wide(blocks))
+    spectrum = dot(table[X_OUT], wide([tile(spectrum, c) * inverse for c in range(8)]))
     spectrum = [tile(spectrum, c) for c in range(8)]
-    at_lines = dot(three_lanes(jnp.concatenate(spectrum, axis=0)), coarse[LINES_OUT])
+    at_lines = dot(three_lanes(jnp.concatenate(spectrum, axis=0)), table[LINES_OUT])
     first = jnp.concatenate([part[:16] for part in spectrum], axis=0)
-    first = dot(three_lanes(first), coarse[Z_OUT])
+    first = dot(three_lanes(first), table[Z_OUT])
     groups = [[], [], []]
     for c in range(8):
         own_line = first[16 * c : 16 * c + 16] + shifts[c]
@@ -461,39 +496,44 @@
         out[:, pl.ds(128 * t, 128)] = packed[pl.ds(128 * t, 128), :]
 
 
-def decode(recv, modes, coarse, fine, packed, comps_in):
+def decode(recv, modes, table, packed, comps_in):
     for t in range(3):
         packed[pl.ds(128 * t, 128), :] = recv[:, pl.ds(128 * t, 128)].T
-    mass = fine[pl.ds(ZERO_ROW, 1), :]
+    mass = float_table(table, 1, 16)[0:1]
+    inverse = float_table(table, 0)
     values = [
         jnp.concatenate([packed[pl.ds(128 * t + 16 * c, 16), :] for t in range(3)], axis=0)
         for c in range(8)
     ]
-    mode = dot(coarse[SOURCE], wide(values))
+    mode = dot(table[SOURCE], wide(values))
     stacks = []
     for c in range(8):
-        own = modes[c] + fine[pl.ds(0, 128), :] * tile(mode, c)
+        own = modes[c] + inverse * tile(mode, c)
         stacks.append(jnp.concatenate([own, values[c], values[c] * mass], axis=0))
-    sites = dot(coarse[EXPAND], wide(stacks))
+    sites = dot(table[EXPAND], wide(stacks))
     sites = jnp.concatenate([tile(sites, c) for c in range(8)], axis=0)
-    comps_in[...] = dot(three_lanes(sites), coarse[Z_OUT])
+    comps_in[...] = dot(three_lanes(sites), table[Z_OUT])
 
 
 def update_body(last, refs):
-    recv, modes, edge_x, edge_y, links, face_x, face_y, theta_in, coarse, fine = refs[:10]
-    refs = refs[10:]
+    recv, modes, edge_x, edge_y, links_hbm, face_x, face_y, theta_in, table = refs[:9]
+    refs = refs[9:]
     if last:
         prior, prior_y, theta_first, div, gauge, theta = refs[:6]
-        packed, comps_in, gs, edge_g, ay, prev, acc = refs[6:]
+        links, sem, packed, comps_in, gs, edge_g, ay, prev, acc = refs[6:]
     else:
         out, modes_out, edge_x_out, edge_y_out, theta, gout, gout_y, theta_out = refs[:8]
-        packed, comps_in, gs, edge_g, ay, prev, acc, sources = refs[8:]
-    decode(recv, modes, coarse, fine, packed, comps_in)
+        links, sem, packed, comps_in, gs, edge_g, ay, prev, acc, sources = refs[8:]
+    copy = pltpu.make_async_copy(links_hbm, links, sem)
+    copy.start()
+    decode(recv, modes, table, packed, comps_in)
 
     add_x = add_y = None
     if not last:
-        add_x = algebra(lambda i, j: face_x[entry(i, j)], lambda i, j: face_x[9 + entry(i, j)])
-        add_y = algebra(lambda i, j: face_y[entry(i, j)], lambda i, j: face_y[9 + entry(i, j)])
+        whole_face = full_matrix([face_x[k] for k in range(6)], [face_x[6 + k] for k in range(6)])
+        add_x = algebra(lambda i, j: whole_face[entry(i, j)], lambda i, j: whole_face[9 + entry(i, j)])
+        whole_face = full_matrix([face_y[k] for k in range(6)], [face_y[6 + k] for k in range(6)])
+        add_y = algebra(lambda i, j: whole_face[entry(i, j)], lambda i, j: whole_face[9 + entry(i, j)])
     whole_x, whole_y = [], []
     row = lax.broadcasted_iota(jnp.int32, (16, 128), 0)
     for c in range(8):
@@ -556,7 +596,7 @@
 
     g = [edge_g[k] for k in range(18)]
     ahead = [gs[pl.ds(PLANE + 32 * k + 8, 8, stride=PLANE), :] for k in range(18)]
-    edge = moved_algebra(g, lambda p, i, j: face_y[9 * p + entry(i, j)], ahead)
+    edge = moved_algebra(g, lambda p, i, j: face_y[6 * p + entry(i, j)], ahead)
     for c in range(8):
         ay[pl.ds(24 * c + 7, 8, stride=192), :] = edge[c]
     for half in range(2):
@@ -564,10 +604,11 @@
         start = 8 * half + 8
         g = [gs[pl.ds(32 * k + start, 8), :] for k in range(18)]
         ahead = [gs[pl.ds(PLANE + 32 * k + start, 8), :] for k in range(18)]
-        edge = moved_algebra(g, lambda p, i, j: face_x[9 * p + entry(i, j), rows, :], ahead)
+        edge = moved_algebra(g, lambda p, i, j: face_x[6 * p + entry(i, j), rows, :], ahead)
         for c in range(8):
             prev[c, rows, :] = edge[c]
 
+    copy.wait()
     acc[...] = jnp.zeros_like(acc)
 
     def sites(x, carry):
@@ -615,7 +656,7 @@
         for c in range(8):
             edge_x_out[c] = sources[pl.ds(128 * c, 16), :]
             edge_y_out[c] = sources[pl.ds(128 * c, 8, stride=16), :]
-        encode(sources, 128, coarse, fine, modes_out, packed, out)
+        encode(sources, 128, table, modes_out, packed, out)
 
 
 def update_kernel(*refs):
@@ -638,6 +679,10 @@
     return pl.BlockSpec(memory_space=pltpu.VMEM)
 
 
+def in_hbm(value):
+    return pltpu.with_memory_space_constraint(value, pltpu.HBM)
+
+
 def params(size):
     return pltpu.CompilerParams(vmem_limit_bytes=size * MEGA)
 
@@ -645,36 +690,45 @@
 EDGES = [(8, 16, 128), (8, 8, 128)]
 
 
-def first_call(links, tables):
+def first_call(links, table):
     shapes = [struct(128, 384), struct(8, 128, 128)] + [struct(*e) for e in EDGES] + [struct(8, 128)]
+    shapes += [jax.ShapeDtypeStruct(table.shape, table.dtype), struct(12, 16, 128), struct(12, 8, 128)]
     return pl.pallas_call(
         first_kernel,
-        in_specs=[whole()] * 3,
+        in_specs=[pl.BlockSpec(memory_space=pl.ANY)] * 2,
         out_specs=[whole()] * len(shapes),
         out_shape=shapes,
-        scratch_shapes=[vmem(8, 16, 128), vmem(8 * 152, 128), vmem(384, 128)],
+        scratch_shapes=[
+            vmem(8, 54, 16, 128),
+            vmem(8, 16, 128),
+            vmem(8 * 152, 128),
+            vmem(384, 128),
+            pltpu.SemaphoreType.DMA((9,)),
+        ],
         compiler_params=params(32),
         name="first_divergence",
-    )(links, *tables)
-
-
-def plane_call(own, recv, tables):
+    )(in_hbm(links), in_hbm(table))
+
+
+def plane_call(own, recv, table):
     return pl.pallas_call(
         plane_kernel,
-        in_specs=[pl.BlockSpec(memory_space=pltpu.SMEM)] + [whole()] * 3,
+        in_specs=[pl.BlockSpec(memory_space=pltpu.SMEM)] + [whole()] * 2,
         out_specs=whole(),
         out_shape=struct(128, 384),
         scratch_shapes=[vmem(1024, 128), vmem(1024, 128), vmem(384, 128)],
         compiler_params=params(32),
         name="plane_solve",
-    )(own, recv, *tables)
-
-
-def update_call(recv, state, links, face_x, face_y, tables, prior):
+    )(own, recv, table)
+
+
+def update_call(recv, state, links, face_x, face_y, table, prior):
     last = prior is not None
     modes, edge_x, edge_y, theta = state
-    operands = [recv, modes, edge_x, edge_y, links, face_x, face_y, theta] + list(tables)
+    operands = [recv, modes, edge_x, edge_y, in_hbm(links), face_x, face_y, theta, table]
     scratch = [
+        vmem(54, 8, 16, 128),
+        pltpu.SemaphoreType.DMA,
         vmem(384, 128),
         vmem(8 * 176, 128),
         vmem(10 * PLANE, 128),
@@ -692,7 +746,7 @@
         scratch += [vmem(8 * 128, 128)]
     return pl.pallas_call(
         last_kernel if last else update_kernel,
-        in_specs=[whole()] * len(operands),
+        in_specs=[pl.BlockSpec(memory_space=pl.ANY) if k == 4 else whole() for k in range(len(operands))],
         out_specs=[whole()] * len(shapes),
         out_shape=shapes,
         scratch_shapes=scratch,
@@ -712,17 +766,18 @@
 
 
 def per_device(links):
-    face_x = shifted(links[0, :, :, :, 7].reshape(18, 16, 128), "gx", 1)
-    face_y = shifted(links[1, :, :, :, :, 15].reshape(18, 8, 128), "gy", 1)
     flat = links.reshape(54, 8, 16, 128)
     own = (lax.axis_index("gx") * 8 + lax.axis_index("gy")).astype(jnp.int32).reshape(1)
-    tables = (jnp.asarray(COARSE), jnp.asarray(FINE))
-    packed, *state = first_call(flat, tables)
-    packed, face_x, face_y, own = lax.optimization_barrier((packed, face_x, face_y, own))
+    table = jnp.asarray(TABLE)
+    packed, modes, edge_x, edge_y, theta, table, face_x, face_y = first_call(flat, table)
+    face_x = shifted(face_x, "gx", 1)
+    face_y = shifted(face_y, "gy", 1)
+    state = (modes, edge_x, edge_y, theta)
+    packed, own = lax.optimization_barrier((packed, own))
     prior = None
     for step in range(2):
-        values = exchange(plane_call(own, exchange(packed), tables))
-        results = update_call(values, state, flat, face_x, face_y, tables, prior)
+        values = exchange(plane_call(own, exchange(packed), table))
+        results = update_call(values, state, flat, face_x, face_y, table, prior)
         if step == 0:
             packed, modes, edge_x, edge_y, theta, gout, gout_y, theta_first = results
             state = (modes, edge_x, edge_y, theta)

time: 171 us -> 164 us (0.959)
  blocking collectives: 134 us -> 112 us
  waiting for transfers between devices: 1.93 us -> 14.4 us
  starting transfers between devices: 6.44 us -> 13 us
  local copies, waits for them, and re-layouts: 7.17 us -> 1.55 us
  Pallas kernels: 19.1 us -> 21 us
    all_to_all x5 -> x4, blocking collectives: 134 us -> 112 us  [exchange(): lax.all_to_all(value, ('gx', 'gy'), split_axis=0, concat_axis=0, tiled=True)]
    all_to_all x0 -> x1, waiting for transfers between devices: none -> 14.4 us  [exchange(): lax.all_to_all(value, ('gx', 'gy'), split_axis=0, concat_axis=0, tiled=True)]
    all_to_all x0 -> x1, starting transfers between devices: none -> 7.96 us  [exchange(): lax.all_to_all(value, ('gx', 'gy'), split_axis=0, concat_axis=0, tiled=True)]
    unnamed x14 -> x4, local copies, waits for them, and re-layouts: 4.29 us -> 0.05 us
    slice x2 -> x0, local copies, waits for them, and re-layouts: 2.06 us -> none  [the longest x1 1.13 us: per_device(): face_y = shifted(links[1, :, :, :, :, 15].reshape(18, 8, 128), 'gy', 1)]
    pallas_call x3, Pallas kernels: 15.5 us -> 17.4 us  [the longest x2 13.9 us: update_call(): pl.pallas_call(last_kernel if last else update_kernel, in_specs=[pl.Block...]
    ppermute x2, waiting for transfers between devices: 1.93 us -> 0.01 us  [shifted(): return lax.ppermute(value, axis, pairs)]
  transfers between devices with their start and end apart: 2 -> 3, of which waited for: 1 -> 1; matrix products, arithmetic and copies ran while one was open for 1% -> 0% of each run, Pallas kernels for 1% -> 0%
where the time goes in v3:
time: 164 us
  blocking collectives  112 us (68%)
  Pallas kernels  21 us (13%)
  waiting for transfers between devices  14.4 us (9%)
  starting transfers between devices  13 us (8%)
    all_to_all x4, blocking collectives, exchange(): lax.all_to_all(value, ('gx', 'gy'), split_axis=0, concat_axis=0, tiled=True)  112 us
    all_to_all x1, waiting for transfers between devices, exchange(): lax.all_to_all(value, ('gx', 'gy'), split_axis=0, concat_axis=0, tiled=True)  14.4 us
    pallas_call x2, Pallas kernels, update_call(): pl.pallas_call(last_kernel if last else update_kernel, in_specs=[pl.Block...  13.9 us
    all_to_all x1, starting transfers between devices, exchange(): lax.all_to_all(value, ('gx', 'gy'), split_axis=0, concat_axis=0, tiled=True)  7.96 us
    ppermute x2, starting transfers between devices, shifted(): return lax.ppermute(value, axis, pairs)  5.02 us
    pallas_call x2, Pallas kernels, plane_call(): pl.pallas_call(plane_kernel, in_specs=[pl.BlockSpec(memory_space=pltpu.SM...  3.63 us
    pallas_call x1, Pallas kernels, first_call(): pl.pallas_call(first_kernel, in_specs=[pl.BlockSpec(memory_space=pl.ANY)]...  3.53 us
  transfers between devices with their start and end apart: 3, of which 1 were waited for; matrix products, arithmetic and copies ran while one was open for 0% of the time, Pallas kernels for 0%

profile of v3, /device:TPU:1, one launch (start us, length us, event | category | flops | bytes accessed | tf_op | source)
XLA Modules:
  0.0 163.8 jit_solution(8769991788677539048)
XLA Ops:
  0.6 3.5 %first_divergence.1 = (f32[128,384]{1,0:T(8,128)S(1)}, f32[8,128,128]{2,1,0:T(8,128)S(1)}, f32[8,16,128]{2,1,0:T(8,128)S(1)}, f32[8,8,128]{2,1,0:T(8,128)S(1)}, ...) custom-call(f32[54,8,16,128]{3,2,1,0:T(8,128)} %bitcast.30, ...), custom_call_target="tpu_custom_call" | custom-call | tf_op jit(solution)/shard_map/first_divergence/pallas_call | solution.py:696
  4.2 0.2 copy.5
  4.4 38.2 %all_to_all.53 = f32[128,1,384]{2,1,0:T(1,128)S(1)} all-to-all(f32[128,1,384]{2,1,0:T(1,128)S(1)} %copy.5), channel_id=1, replica_groups=mesh['ta'=4,'gx'=16,'gy'=8] {'gx','gy'}, dimensions={0} | all-to-all | bytes 393216 | tf_op jit(solution)/shard_map/all_to_all | solution.py:765
  42.6 1.8 %plane_solve.2 = f32[128,384]{1,0:T(8,128)S(1)} custom-call(s32[1]{0:T(128)} %bitcast.1.own, f32[128,384]{1,0:T(8,128)S(1)} %bitcast.24, bf16[992,768]{1,0:T(8,128)(2,1)S(1)} %get-tuple-element.27.table.refs_8_), custom_call_target="tpu_custom_call" | custom-call | tf_op jit(solution)/shard_map/plane_solve/pallas_call | solution.py:714
  44.4 0.9 copy.6
  45.3 8.0 %all-to-all-start.1 = ((f32[128,1,384]{2,1,0:T(1,128)}), f32[128,1,384]{2,1,0:T(1,128)S(1)}, u32[]{:S(2)}, u32[]{:S(2)}) async-start(f32[128,1,384]{2,1,0:T(1,128)} %copy.6), calls=%async_computation.1 | async-start | bytes 393216 | tf_op jit(solution)/shard_map/all_to_all | solution.py:765
  53.3 3.3 %collective-permute-start = (f32[12,16,128]{2,1,0:T(8,128)S(1)}, f32[12,16,128]{2,1,0:T(8,128)S(1)}, u32[]{:S(2)}, u32[]{:S(2)}) collective-permute-start(f32[12,16,128]{2,1,0:T(8,128)S(1)} %get-tuple-element.31), channel_id=1, source_target_pairs={{0,8},{8,16},{16,24},{24,32},{32,40},{40,48},{48,56},{56,64},{64,7... | collective-permute-start | bytes 294920 | tf_op jit(solution)/shard_map/ppermute | solution.py:761
  56.6 1.7 %collective-permute-start.1 = (f32[12,8,128]{2,1,0:T(8,128)S(1)}, f32[12,8,128]{2,1,0:T(8,128)S(1)}, u32[]{:S(2)}, u32[]{:S(2)}) collective-permute-start(f32[12,8,128]{2,1,0:T(8,128)S(1)} %get-tuple-element.32), channel_id=1, source_target_pairs={{0,1},{1,2},{2,3},{3,4},{4,5},{5,6},{6,7},{7,0},{8,9},{9,10},{10,1... | collective-permute-start | bytes 147464 | tf_op jit(solution)/shard_map/ppermute | solution.py:761
  58.3 14.4 %all-to-all-done.1 = f32[128,1,384]{2,1,0:T(1,128)S(1)} async-done(((f32[128,1,384]{2,1,0:T(1,128)}), f32[128,1,384]{2,1,0:T(1,128)S(1)}, u32[]{:S(2)}, u32[]{:S(2)}) %all-to-all-start.1) | async-done | bytes 196640 | tf_op jit(solution)/shard_map/all_to_all | solution.py:765
  72.7 0.0 collective-permute-done.1.refs_6_
  72.7 0.0 collective-permute-done.refs_5_
  72.7 7.3 %update.1 = (f32[128,384]{1,0:T(8,128)S(1)}, f32[8,128,128]{2,1,0:T(8,128)S(1)}, f32[8,16,128]{2,1,0:T(8,128)S(1)}, f32[8,8,128]{2,1,0:T(8,128)S(1)}, f32[8,128]...) custom-call(f32[128,384]{1,0:T(8,128)S(1)} %bitcast.21, ...), custom_call_target="tpu_custom_call" | custom-call | tf_op jit(solution)/shard_map/update/pallas_call | solution.py:747
  80.1 0.2 copy.7
  80.3 25.7 %all_to_all.54 = f32[128,1,384]{2,1,0:T(1,128)S(1)} all-to-all(f32[128,1,384]{2,1,0:T(1,128)S(1)} %copy.7), channel_id=1, replica_groups=mesh['ta'=4,'gx'=16,'gy'=8] {'gx','gy'}, dimensions={0} | all-to-all | bytes 393216 | tf_op jit(solution)/shard_map/all_to_all | solution.py:765
  106.0 1.8 %plane_solve.3 = f32[128,384]{1,0:T(8,128)S(1)} custom-call(s32[1]{0:T(128)} %bitcast.1.own, f32[128,384]{1,0:T(8,128)S(1)} %bitcast.22, bf16[992,768]{1,0:T(8,128)(2,1)S(1)} %get-tuple-element.27.table.refs_8_), custom_call_target="tpu_custom_call" | custom-call | tf_op jit(solution)/shard_map/plane_solve/pallas_call | solution.py:714
  107.9 0.2 copy.8
  108.1 25.8 %all_to_all.55 = f32[128,1,384]{2,1,0:T(1,128)S(1)} all-to-all(f32[128,1,384]{2,1,0:T(1,128)S(1)} %copy.8), channel_id=1, replica_groups=mesh['ta'=4,'gx'=16,'gy'=8] {'gx','gy'}, dimensions={0} | all-to-all | bytes 393216 | tf_op jit(solution)/shard_map/all_to_all | solution.py:765
  133.9 6.6 %last_update.1 = (f32[8,8,16,128]{3,2,1,0:T(8,128)}, f32[2,2,3,8,16,128]{5,4,3,2,1,0:T(8,128)}, f32[128,128]{1,0:T(8,128)S(1)}) custom-call(f32[128,384]{1,0:T(8,128)S(1)} %bitcast.26, f32[8,128,128]{2,1,0:T(8,128)S(1)} %get-tuple-element.35.refs_1_, f32[8,16,128]{2,1,0:T(8,128)S(1)} %get-tuple-element.36.refs_2_, ...), custom_call_target="tpu_custom_call" | custom-call | tf_op jit(solution)/shard_map/last_update/pallas_call | solution.py:747
  140.4 22.7 %all_to_all.56 = f32[128,1,128]{2,1,0:T(1,128)S(1)} all-to-all(f32[128,1,128]{2,1,0:T(1,128)S(1)} %bitcast.29), channel_id=1, replica_groups=mesh['ta'=4,'gx'=16,'gy'=8] {'gx','gy'}, dimensions={0} | all-to-all | bytes 131072 | tf_op jit(solution)/shard_map/all_to_all | solution.py:765
  163.1 0.2 reduce_sum.9
  163.2 0.5 slice_multiply_fusion
  (4 shorter events, 0.1 us)
Async XLA Ops:
  45.3 27.4 %all-to-all-start.1 = ((f32[128,1,384]{2,1,0:T(1,128)}), f32[128,1,384]{2,1,0:T(1,128)S(1)}, u32[]{:S(2)}, u32[]{:S(2)}) async-start(f32[128,1,384]{2,1,0:T(1,128)} %copy.6), calls=%async_computation.1 | async-start | bytes 393216 | tf_op jit(solution)/shard_map/all_to_all | solution.py:765
  53.3 19.4 %collective-permute-start = (f32[12,16,128]{2,1,0:T(8,128)S(1)}, f32[12,16,128]{2,1,0:T(8,128)S(1)}, u32[]{:S(2)}, u32[]{:S(2)}) collective-permute-start(f32[12,16,128]{2,1,0:T(8,128)S(1)} %get-tuple-element.31), channel_id=1, source_target_pairs={{0,8},{8,16},{16,24},{24,32},{32,40},{40,48},{48,56},{56,64},{64,7... | collective-permute-start | bytes 294920 | tf_op jit(solution)/shard_map/ppermute | solution.py:761
  56.6 16.1 %collective-permute-start.1 = (f32[12,8,128]{2,1,0:T(8,128)S(1)}, f32[12,8,128]{2,1,0:T(8,128)S(1)}, u32[]{:S(2)}, u32[]{:S(2)}) collective-permute-start(f32[12,8,128]{2,1,0:T(8,128)S(1)} %get-tuple-element.32), channel_id=1, source_target_pairs={{0,1},{1,2},{2,3},{3,4},{4,5},{5,6},{6,7},{7,0},{8,9},{9,10},{10,1... | collective-permute-start | bytes 147464 | tf_op jit(solution)/shard_map/ppermute | solution.py:761

commit v4 on v3

--- a/solution.py
+++ b/solution.py
@@ -66,17 +66,14 @@
 
 
 def reduce_table():
-    out = np.zeros((48, 256))
-    for y in range(16):
-        out[y, node(0, y)] = 1.0
-        if y > 0:
-            out[y, 128:] = SINE[node(1, y)]
-            out[16 + y, 128:] = SINE[node(7, y)]
-    out[32, 128:] = SINE[INNER].sum(0)
+    out = np.zeros((48, 128))
+    for y in range(1, 16):
+        out[y] = SINE[node(1, y)]
+        out[16 + y] = SINE[node(7, y)]
+    out[32] = SINE[INNER].sum(0)
     for x in range(1, 8):
-        out[32 + x, node(x, 0)] = 1.0
-        out[32 + x, 128:] = SINE[node(x, 1)]
-        out[40 + x, 128:] = SINE[node(x, 15)]
+        out[32 + x] = SINE[node(x, 1)]
+        out[40 + x] = SINE[node(x, 15)]
     return out
 
 
@@ -92,8 +89,8 @@
 
 
 def expand_table():
-    out = np.zeros((176, 224))
-    val, mass = 128, 176
+    out = np.zeros((176, 176))
+    val = 128
 
     def line_x(x):
         return 0 if x == 0 else (16 if x == 8 else 32 + x)
@@ -115,24 +112,23 @@
     for y in range(1, 16):
         row = out[144 + y]
         row[val + y] += 4.0
-        row[mass + y] += 1.0
         row[:128] -= SINE[node(1, y)]
         row[val + line_y(y - 1)] -= 1.0
         row[val + line_y(y + 1)] -= 1.0
     for x in range(1, 8):
         row = out[168 + x]
         row[val + line_x(x)] += 4.0
-        row[mass + line_x(x)] += 1.0
         row[:128] -= SINE[node(x, 1)]
         row[val + line_x(x - 1)] -= 1.0
         row[val + line_x(x + 1)] -= 1.0
     row = out[168]
     row[val] += 4.0
-    row[mass] += 1.0
     row[val + 33] -= 1.0
     row[val + 32] -= 1.0
     row[val + 1] -= 1.0
-    return out
+    high, low = halves(out)
+    assert not np.any(low[:, 128:].astype(np.float32))
+    return np.concatenate([high, high, low[:, :128]], axis=1)
 
 
 def lines_in():
@@ -163,8 +159,8 @@
     out[384:512, 384:] = left_table(BASIS[ORDER].T)
     out[512:640, :384] = left_table(BASIS[ORDER])
     out[512:640, 384:528] = left_table(source_table())
-    out[640:688, :] = left_table(reduce_table())
-    out[688:864, :672] = left_table(expand_table())
+    out[640:688, :384] = left_table(reduce_table())
+    out[688:864, :480] = expand_table()
     for k, table in enumerate((INVERSE, PLANE_SUM)):
         rest = table.astype(np.float32).astype(np.float64)
         for part in range(3):
@@ -183,8 +179,8 @@
 X_IN = (slice(384, 512), slice(384, 768))
 X_OUT = (slice(512, 640), slice(0, 384))
 SOURCE = (slice(512, 640), slice(384, 528))
-REDUCE = (slice(640, 688), slice(0, 768))
-EXPAND = (slice(688, 864), slice(0, 672))
+REDUCE = (slice(640, 688), slice(0, 384))
+EXPAND = (slice(688, 864), slice(0, 480))
 
 
 def float_table(table, which, rows=128):
@@ -370,27 +366,29 @@
     return value[:, 128 * c : 128 * c + 128]
 
 
-def encode(sources, stride, table, modes, packed, out):
-    spectrum = dot(three_lanes(sources[...]), table[Z_IN])
-    parts = [spectrum[stride * c : stride * c + stride] for c in range(8)]
-    mode = dot(table[MODES], wide([part[:128] for part in parts]))
+def encode(spectrum, stride, table, modes, packed, out):
+    mode = dot(table[MODES], wide([spectrum[pl.ds(stride * c, 128), :] for c in range(8)]))
     inverse = float_table(table, 0)
     scaled = []
     for c in range(8):
         scaled.append(inverse * tile(mode, c))
         modes[c] = scaled[c]
-    both = [jnp.concatenate([parts[c][:128], scaled[c]], axis=0) for c in range(8)]
-    reduced = dot(table[REDUCE], wide(both))
-    for c in range(8):
+    reduced = dot(table[REDUCE], wide(scaled))
+    corner = lax.broadcasted_iota(jnp.int32, (8, 128), 0) == 0
+    for c in range(8):
+        start = stride * c
         values = tile(reduced, c)
-        groups = [values[0:16], values[16:32], values[32:48]]
+        line_x = values[0:16] + spectrum[pl.ds(start, 16), :]
+        line_y = jnp.where(corner, 0.0, spectrum[pl.ds(start, 8, stride=16), :])
+        next_x, next_y = values[16:32], values[40:48]
         if stride > 128:
-            groups[1] = groups[1] + parts[c][128:144]
-            groups[2] = jnp.concatenate([groups[2][:8], groups[2][8:] + parts[c][144:152]], axis=0)
+            next_x = next_x + spectrum[pl.ds(start + 128, 16), :]
+            next_y = next_y + spectrum[pl.ds(start + 144, 8), :]
+        groups = [line_x, next_x, jnp.concatenate([values[32:40] + line_y, next_y], axis=0)]
         for t in range(3):
             packed[pl.ds(128 * t + 16 * c, 16), :] = groups[t]
     for t in range(3):
-        out[:, pl.ds(128 * t, 128)] = packed[pl.ds(128 * t, 128), :].T
+        out[pl.ds(t, 128, stride=3), :] = packed[pl.ds(128 * t, 128), :].T
 
 
 def first_kernel(*refs):
@@ -398,7 +396,7 @@
     links, prev, sources, packed, sems = refs[10:]
 
     def plane_copy(x):
-        return pltpu.make_async_copy(links_hbm.at[:, x], links.at[x], sems.at[x])
+        return pltpu.make_async_copy(links_hbm.at[:, x], links.at[:, x], sems.at[x])
 
     for x in range(8):
         plane_copy(x).start()
@@ -413,8 +411,8 @@
 
         def of(mu):
             return algebra(
-                lambda i, j: links[x, 18 * mu + entry(i, j)],
-                lambda i, j: links[x, 18 * mu + 9 + entry(i, j)],
+                lambda i, j: links[18 * mu + entry(i, j), x],
+                lambda i, j: links[18 * mu + 9 + entry(i, j), x],
             )
 
         ax, ay, az = of(0), of(1), of(2)
@@ -427,7 +425,7 @@
             sources[pl.ds(152 * c + 16 * x, 16), :] = value
             sources[pl.ds(152 * c + 144 + x, 1), :] = ay[c][15:16]
         for k in range(12):
-            face_y[k, pl.ds(x, 1), :] = links[x, 18 + k % 6 + 9 * (k // 6), 15:16, :]
+            face_y[k, pl.ds(x, 1), :] = links[18 + k % 6 + 9 * (k // 6), x, 15:16, :]
         inner = jnp.where((row > 0) & (x > 0), squares(comps), 0.0)
         theta[...] += inner[:8] + inner[8:]
         return carry
@@ -438,12 +436,13 @@
         edge_x[c] = sources[pl.ds(152 * c, 16), :]
         edge_y[c] = sources[pl.ds(152 * c, 8, stride=16), :]
     for k in range(12):
-        face_x[k] = links[7, k % 6 + 9 * (k // 6)]
+        face_x[k] = links[k % 6 + 9 * (k // 6), 7]
     table_copy.wait()
+    sources[...] = dot(three_lanes(sources[...]), table[Z_IN])
     encode(sources, 152, table, modes, packed, out)
 
 
-def plane_kernel(own, recv, table, out, work, lines, packed):
+def plane_kernel(own, recv, table, out, work, lines):
     lane = lax.broadcasted_iota(jnp.int32, (16, 128), 1) % 16
     zero = jnp.where(own[0] == 0, -1.0 / (LS * LS), 0.0)
     total = float_table(table, 1)
@@ -451,10 +450,8 @@
     total = total + work[pl.ds(own[0], 1), :][:, 0:1]
     inverse = jnp.where(total > 0.0, 1.0 / jnp.where(total > 0.0, total, 1.0), 0.0)
     shifts = []
-    for t in range(3):
-        packed[pl.ds(128 * t, 128), :] = recv[:, pl.ds(128 * t, 128)]
     moved = [
-        swap_blocks([packed[pl.ds(128 * t + g, 16, stride=8), :] for g in range(8)])
+        swap_blocks([recv[pl.ds(3 * g + t, 16, stride=24), :] for g in range(8)])
         for t in range(3)
     ]
     for c in range(8):
@@ -492,13 +489,12 @@
     for t in range(3):
         tiles = swap_blocks(groups[t])
         for g in range(8):
-            packed[pl.ds(128 * t + g, 16, stride=8), :] = tiles[g]
-        out[:, pl.ds(128 * t, 128)] = packed[pl.ds(128 * t, 128), :]
+            out[pl.ds(3 * g + t, 16, stride=24), :] = tiles[g]
 
 
 def decode(recv, modes, table, packed, comps_in):
     for t in range(3):
-        packed[pl.ds(128 * t, 128), :] = recv[:, pl.ds(128 * t, 128)].T
+        packed[pl.ds(128 * t, 128), :] = recv[pl.ds(t, 128, stride=3), :].T
     mass = float_table(table, 1, 16)[0:1]
     inverse = float_table(table, 0)
     values = [
@@ -509,109 +505,40 @@
     stacks = []
     for c in range(8):
         own = modes[c] + inverse * tile(mode, c)
-        stacks.append(jnp.concatenate([own, values[c], values[c] * mass], axis=0))
-    sites = dot(table[EXPAND], wide(stacks))
-    sites = jnp.concatenate([tile(sites, c) for c in range(8)], axis=0)
-    comps_in[...] = dot(three_lanes(sites), table[Z_OUT])
-
-
-def update_body(last, refs):
-    recv, modes, edge_x, edge_y, links_hbm, face_x, face_y, theta_in, table = refs[:9]
-    refs = refs[9:]
-    if last:
-        prior, prior_y, theta_first, div, gauge, theta = refs[:6]
-        links, sem, packed, comps_in, gs, edge_g, ay, prev, acc = refs[6:]
-    else:
-        out, modes_out, edge_x_out, edge_y_out, theta, gout, gout_y, theta_out = refs[:8]
-        links, sem, packed, comps_in, gs, edge_g, ay, prev, acc, sources = refs[8:]
-    copy = pltpu.make_async_copy(links_hbm, links, sem)
-    copy.start()
-    decode(recv, modes, table, packed, comps_in)
-
-    add_x = add_y = None
-    if not last:
-        whole_face = full_matrix([face_x[k] for k in range(6)], [face_x[6 + k] for k in range(6)])
-        add_x = algebra(lambda i, j: whole_face[entry(i, j)], lambda i, j: whole_face[9 + entry(i, j)])
-        whole_face = full_matrix([face_y[k] for k in range(6)], [face_y[6 + k] for k in range(6)])
-        add_y = algebra(lambda i, j: whole_face[entry(i, j)], lambda i, j: whole_face[9 + entry(i, j)])
-    whole_x, whole_y = [], []
+        value = jnp.concatenate([own, values[c]], axis=0)
+        high = value.astype(BF16)
+        low = (value - high.astype(F32)).astype(BF16)
+        stacks.append(jnp.concatenate([high, low, high[:128]], axis=0))
+    sites = dot(table[EXPAND], jnp.concatenate(stacks, axis=1))
     row = lax.broadcasted_iota(jnp.int32, (16, 128), 0)
-    for c in range(8):
-        line_x, line_y = edge_x[c], edge_y[c]
-        if not last:
-            top = row == 0
-            line_x = line_x + add_x[c] + jnp.where(top, add_y[c][0:1], 0.0)
-            line_y = line_y + add_y[c] + jnp.where(top[:8], add_x[c][0:1], 0.0)
-        whole_x.append(line_x)
-        whole_y.append(line_y)
-        behind = pl.ds(176 * c + 144, 16)
-        comps_in[behind, :] = comps_in[behind, :] - jnp.where(row == 0, 0.0, SCALE * line_x)
-        below = pl.ds(176 * c + 168, 8)
-        comps_in[below, :] = comps_in[below, :] - SCALE * line_y
-    if not last:
-        sq = squares(whole_x)
-        theta_out[...] = (
-            theta_in[...] + sq[:8] + sq[8:] + jnp.where(row[:8] == 0, 0.0, squares(whole_y))
-        )
-
-    def make(c, before):
-        re6, im6 = exponent_rows(c)
-        if before is not None:
-            re6, im6 = times_rows(re6, im6, before[:9], before[9:])
-        return full_matrix(re6, im6)
-
-    def plane(index, first_row, inside):
-        for half in range(2):
-            rows = pl.ds(8 * half, 8)
-            before = [prior[index, k, rows, :] for k in range(18)] if last else None
-            g = make([comps_in[pl.ds(first_row(c) + 8 * half, 8), :] for c in range(8)], before)
-            for k in range(18):
-                gs[pl.ds(index * PLANE + 32 * k + 8 * half + 8, 8), :] = g[k]
-                if not last:
-                    gout[index, k, rows, :] = g[k]
-            if last and inside:
-                for p in range(2):
-                    for i in range(2):
-                        for j in range(3):
-                            gauge[p, i, j, index - 1, rows, :] = g[9 * p + entry(i, j)]
-
-    def inner(x, carry):
-        plane(x + 1, lambda c: 176 * c + 16 * x, True)
-        return carry
-
-    lax.fori_loop(0, 8, inner, 0)
-    plane(0, lambda c: 176 * c + 144, False)
-    plane(9, lambda c: 176 * c + 128, False)
-    for side in range(2):
-        c = [comps_in[pl.ds(176 * k + 168 - 8 * side, 8), :] for k in range(8)]
-        before = [prior_y[side, k] for k in range(18)] if last else None
-        g = make(c, before)
-        for k in range(18):
-            if not last:
-                gout_y[side, k] = g[k]
-            if side == 0:
-                edge_g[k] = g[k]
-            else:
-                gs[pl.ds(PLANE + 32 * k + 24, 8, stride=PLANE), :] = g[k]
-
-    g = [edge_g[k] for k in range(18)]
-    ahead = [gs[pl.ds(PLANE + 32 * k + 8, 8, stride=PLANE), :] for k in range(18)]
-    edge = moved_algebra(g, lambda p, i, j: face_y[6 * p + entry(i, j)], ahead)
-    for c in range(8):
-        ay[pl.ds(24 * c + 7, 8, stride=192), :] = edge[c]
-    for half in range(2):
-        rows = pl.ds(8 * half, 8)
-        start = 8 * half + 8
-        g = [gs[pl.ds(32 * k + start, 8), :] for k in range(18)]
-        ahead = [gs[pl.ds(PLANE + 32 * k + start, 8), :] for k in range(18)]
-        edge = moved_algebra(g, lambda p, i, j: face_x[6 * p + entry(i, j), rows, :], ahead)
-        for c in range(8):
-            prev[c, rows, :] = edge[c]
-
-    copy.wait()
-    acc[...] = jnp.zeros_like(acc)
-
+    parts = []
+    for c in range(8):
+        part, value = tile(sites, c), values[c]
+        behind = part[144:160] + mass * jnp.where(row == 0, 0.0, value[0:16])
+        below = part[168:176] + mass * jnp.where(row[:8] == 0, value[0:8], value[32:40])
+        parts.append(jnp.concatenate([part[:144], behind, part[160:168], below], axis=0))
+    comps_in[...] = dot(three_lanes(jnp.concatenate(parts, axis=0)), table[Z_OUT])
+
+
+def make(c, before=None):
+    re6, im6 = exponent_rows(c)
+    if before is not None:
+        re6, im6 = times_rows(re6, im6, before[:9], before[9:])
+    return full_matrix(re6, im6)
+
+
+def start_links(links_hbm, links, sems):
+    def plane_copy(x):
+        return pltpu.make_async_copy(links_hbm.at[:, x], links.at[:, x], sems.at[x])
+
+    for x in range(8):
+        plane_copy(x).start()
+    return plane_copy
+
+
+def moved_divergence(links, plane_copy, gs, ay, prev, emit):
     def sites(x, carry):
+        plane_copy(x).wait()
         base = (x + 1) * PLANE
         for half in range(2):
             rows = pl.ds(8 * half, 8)
@@ -633,38 +560,175 @@
                 ay[pl.ds(x * 192 + 24 * c + start, 8), :] = a[c]
             for c in range(8):
                 total[c] = total[c] + (ay[pl.ds(x * 192 + 24 * c + start - 1, 8), :] - a[c])
+            top = [v[7:8] for v in a]
             ahead = [pltpu.roll(v, 127, 1) for v in g]
             a = moved_algebra(g, link_of(2), ahead)
             for c in range(8):
                 total[c] = total[c] + (pltpu.roll(a[c], 1, 1) - a[c])
-                if last:
-                    div[c, x, rows, :] = total[c]
-                else:
-                    sources[pl.ds(128 * c + 16 * x + 8 * half, 8), :] = total[c]
-            acc[...] += squares(total)
+            emit(x, half, total, top)
         return carry
 
     lax.fori_loop(0, 8, sites, 0)
-    if last:
-        lane = lax.broadcasted_iota(jnp.int32, (1, 128), 1)
-        sums = jnp.zeros((1, 128), F32)
-        for k, part in enumerate((theta_first, theta_in, acc)):
-            sums = sums + jnp.where(lane == k, jnp.sum(part[...]), 0.0)
-        theta[...] = jnp.broadcast_to(sums, (128, 128))
-    else:
-        theta[...] = acc[...]
+
+
+def update_kernel(*refs):
+    recv, modes, links_hbm, table = refs[:4]
+    out, modes_out, edge_x, edge_y, theta, gout, gout_y, raw_x, raw_y = refs[4:13]
+    links, sems, packed, comps_in, gs, ay, prev, sources = refs[13:]
+    plane_copy = start_links(links_hbm, links, sems)
+    decode(recv, modes, table, packed, comps_in)
+    for c in range(8):
+        raw_x[c] = comps_in[pl.ds(176 * c + 144, 16), :]
+        raw_y[c] = comps_in[pl.ds(176 * c + 168, 8), :]
+
+    def plane(index, first_row):
+        for half in range(2):
+            g = make([comps_in[pl.ds(first_row(c) + 8 * half, 8), :] for c in range(8)])
+            for k in range(18):
+                gs[pl.ds(index * PLANE + 32 * k + 8 * half + 8, 8), :] = g[k]
+                gout[pl.ds((index - 1) * 288 + 16 * k + 8 * half, 8), :] = g[k]
+
+    def inner(x, carry):
+        plane(x + 1, lambda c: 176 * c + 16 * x)
+        return carry
+
+    lax.fori_loop(0, 8, inner, 0)
+    plane(9, lambda c: 176 * c + 128)
+    g = make([comps_in[pl.ds(176 * c + 160, 8), :] for c in range(8)])
+    for k in range(18):
+        gout_y[k] = g[k]
+        gs[pl.ds(PLANE + 32 * k + 24, 8, stride=PLANE), :] = g[k]
+
+    prev[...] = jnp.zeros_like(prev)
+    theta[...] = jnp.zeros_like(theta)
+    for c in range(8):
+        ay[pl.ds(24 * c + 7, 8, stride=192), :] = jnp.zeros((8, 128), F32)
+    row = lax.broadcasted_iota(jnp.int32, (8, 128), 0)
+
+    def emit(x, half, total, top):
         for c in range(8):
-            edge_x_out[c] = sources[pl.ds(128 * c, 16), :]
-            edge_y_out[c] = sources[pl.ds(128 * c, 8, stride=16), :]
-        encode(sources, 128, table, modes_out, packed, out)
-
-
-def update_kernel(*refs):
-    update_body(False, refs)
+            sources[pl.ds(152 * c + 16 * x + 8 * half, 8), :] = total[c]
+            if half == 1:
+                sources[pl.ds(152 * c + 144 + x, 1), :] = top[c]
+        theta[...] += jnp.where((x > 0) & (row + half > 0), squares(total), 0.0)
+
+    moved_divergence(links, plane_copy, gs, ay, prev, emit)
+    for c in range(8):
+        sources[pl.ds(152 * c + 128, 16), :] = prev[c]
+        edge_x[c] = sources[pl.ds(152 * c, 16), :]
+        edge_y[c] = sources[pl.ds(152 * c, 8, stride=16), :]
+    sources[...] = dot(three_lanes(sources[...]), table[Z_IN])
+    encode(sources, 152, table, modes_out, packed, out)
+
+
+def whole_lines(line_x, line_y, add_x, add_y):
+    top = lax.broadcasted_iota(jnp.int32, (16, 128), 0) == 0
+    out_x, out_y = [], []
+    for c in range(8):
+        out_x.append(line_x[c] + add_x[c] + jnp.where(top, add_y[c][0:1], 0.0))
+        out_y.append(line_y[c] + add_y[c] + jnp.where(top[:8], add_x[c][0:1], 0.0))
+    sq = squares(out_x)
+    return out_x, out_y, sq[:8] + sq[8:] + jnp.where(top[:8], 0.0, squares(out_y))
 
 
 def last_kernel(*refs):
-    update_body(True, refs)
+    recv, modes, links_hbm, table, line0_x, line0_y, line1_x, line1_y, raw_x, raw_y = refs[:10]
+    face_x, face_y, theta0, theta1, prior, prior_y, div, gauge, theta = refs[10:19]
+    links, sems, packed, comps_in, gs, behind, below, ay, prev, acc = refs[19:]
+    plane_copy = start_links(links_hbm, links, sems)
+    decode(recv, modes, table, packed, comps_in)
+    row = lax.broadcasted_iota(jnp.int32, (16, 128), 0)
+
+    face = full_matrix([face_x[k] for k in range(6)], [face_x[6 + k] for k in range(6)])
+    add_x = algebra(lambda i, j: face[entry(i, j)], lambda i, j: face[9 + entry(i, j)])
+    face = full_matrix([face_y[k] for k in range(6)], [face_y[6 + k] for k in range(6)])
+    add_y = algebra(lambda i, j: face[entry(i, j)], lambda i, j: face[9 + entry(i, j)])
+    whole_x, whole_y, extra0 = whole_lines(line0_x, line0_y, add_x, add_y)
+    for half in range(2):
+        rows = pl.ds(8 * half, 8)
+        part = slice(8 * half, 8 * half + 8)
+        taken = [jnp.where(row == 0, 0.0, SCALE * whole_x[c])[part] for c in range(8)]
+        g = make([raw_x[c, rows, :] - taken[c] for c in range(8)])
+        for k in range(18):
+            behind[k, rows, :] = g[k]
+        ahead = [prior[pl.ds(16 * k + 8 * half, 8), :] for k in range(18)]
+        edge = moved_algebra(g, lambda p, i, j: face_x[6 * p + entry(i, j), rows, :], ahead)
+        for c in range(8):
+            prev[c, rows, :] = edge[c]
+    g = make([raw_y[c] - SCALE * whole_y[c] for c in range(8)])
+    for k in range(18):
+        below[k] = g[k]
+    ahead = [prior[pl.ds(16 * k, 8, stride=288), :] for k in range(18)]
+    edge = moved_algebra(g, lambda p, i, j: face_y[6 * p + entry(i, j)], ahead)
+    whole_x, whole_y, extra1 = whole_lines(line1_x, line1_y, prev, edge)
+
+    for c in range(8):
+        rows = pl.ds(176 * c + 144, 16)
+        comps_in[rows, :] = comps_in[rows, :] - jnp.where(row == 0, 0.0, SCALE * whole_x[c])
+        rows = pl.ds(176 * c + 168, 8)
+        comps_in[rows, :] = comps_in[rows, :] - SCALE * whole_y[c]
+
+    def plane(index, first_row, before):
+        for half in range(2):
+            rows = pl.ds(8 * half, 8)
+            g = make([comps_in[pl.ds(first_row(c) + 8 * half, 8), :] for c in range(8)], before(half))
+            for k in range(18):
+                gs[pl.ds(index * PLANE + 32 * k + 8 * half + 8, 8), :] = g[k]
+            if not isinstance(index, int):
+                for p in range(2):
+                    for i in range(2):
+                        for j in range(3):
+                            gauge[p, i, j, index - 1, rows, :] = g[9 * p + entry(i, j)]
+
+    def before_at(index):
+        return lambda half: [
+            prior[pl.ds((index - 1) * 288 + 16 * k + 8 * half, 8), :] for k in range(18)
+        ]
+
+    def inner(x, carry):
+        plane(x + 1, lambda c: 176 * c + 16 * x, before_at(x + 1))
+        return carry
+
+    lax.fori_loop(0, 8, inner, 0)
+    plane(
+        0,
+        lambda c: 176 * c + 144,
+        lambda half: [behind[k, pl.ds(8 * half, 8), :] for k in range(18)],
+    )
+    plane(9, lambda c: 176 * c + 128, before_at(9))
+    g = make(
+        [comps_in[pl.ds(176 * c + 160, 8), :] for c in range(8)], [prior_y[k] for k in range(18)]
+    )
+    for k in range(18):
+        gs[pl.ds(PLANE + 32 * k + 24, 8, stride=PLANE), :] = g[k]
+
+    g = make([comps_in[pl.ds(176 * c + 168, 8), :] for c in range(8)], [below[k] for k in range(18)])
+    ahead = [gs[pl.ds(PLANE + 32 * k + 8, 8, stride=PLANE), :] for k in range(18)]
+    edge = moved_algebra(g, lambda p, i, j: face_y[6 * p + entry(i, j)], ahead)
+    for c in range(8):
+        ay[pl.ds(24 * c + 7, 8, stride=192), :] = edge[c]
+    for half in range(2):
+        rows = pl.ds(8 * half, 8)
+        start = 8 * half + 8
+        g = [gs[pl.ds(32 * k + start, 8), :] for k in range(18)]
+        ahead = [gs[pl.ds(PLANE + 32 * k + start, 8), :] for k in range(18)]
+        edge = moved_algebra(g, lambda p, i, j: face_x[6 * p + entry(i, j), rows, :], ahead)
+        for c in range(8):
+            prev[c, rows, :] = edge[c]
+
+    acc[...] = jnp.zeros_like(acc)
+
+    def emit(x, half, total, top):
+        for c in range(8):
+            div[c, x, pl.ds(8 * half, 8), :] = total[c]
+        acc[...] += squares(total)
+
+    moved_divergence(links, plane_copy, gs, ay, prev, emit)
+    lane = lax.broadcasted_iota(jnp.int32, (1, 128), 1)
+    sums = jnp.zeros((1, 128), F32)
+    for k, part in enumerate((theta0[...] + extra0, theta1[...] + extra1, acc[...])):
+        sums = sums + jnp.where(lane == k, jnp.sum(part), 0.0)
+    theta[...] = jnp.broadcast_to(sums * (1.0 / (3.0 * LS * LS * NZ)), (128, 128))
 
 
 def struct(*shape):
@@ -691,7 +755,7 @@
 
 
 def first_call(links, table):
-    shapes = [struct(128, 384), struct(8, 128, 128)] + [struct(*e) for e in EDGES] + [struct(8, 128)]
+    shapes = [struct(384, 128), struct(8, 128, 128)] + [struct(*e) for e in EDGES] + [struct(8, 128)]
     shapes += [jax.ShapeDtypeStruct(table.shape, table.dtype), struct(12, 16, 128), struct(12, 8, 128)]
     return pl.pallas_call(
         first_kernel,
@@ -699,7 +763,7 @@
         out_specs=[whole()] * len(shapes),
         out_shape=shapes,
         scratch_shapes=[
-            vmem(8, 54, 16, 128),
+            vmem(54, 8, 16, 128),
             vmem(8, 16, 128),
             vmem(8 * 152, 128),
             vmem(384, 128),
@@ -715,43 +779,29 @@
         plane_kernel,
         in_specs=[pl.BlockSpec(memory_space=pltpu.SMEM)] + [whole()] * 2,
         out_specs=whole(),
-        out_shape=struct(128, 384),
-        scratch_shapes=[vmem(1024, 128), vmem(1024, 128), vmem(384, 128)],
+        out_shape=struct(384, 128),
+        scratch_shapes=[vmem(1024, 128), vmem(1024, 128)],
         compiler_params=params(32),
         name="plane_solve",
     )(own, recv, table)
 
 
-def update_call(recv, state, links, face_x, face_y, table, prior):
-    last = prior is not None
-    modes, edge_x, edge_y, theta = state
-    operands = [recv, modes, edge_x, edge_y, in_hbm(links), face_x, face_y, theta, table]
+def update_call(kernel, operands, shapes, extra, name):
     scratch = [
         vmem(54, 8, 16, 128),
-        pltpu.SemaphoreType.DMA,
+        pltpu.SemaphoreType.DMA((8,)),
         vmem(384, 128),
         vmem(8 * 176, 128),
         vmem(10 * PLANE, 128),
-        vmem(18, 8, 128),
-        vmem(8 * 192, 128),
-        vmem(8, 16, 128),
-        vmem(8, 128),
     ]
-    if last:
-        shapes = [struct(8, 8, 16, 128), struct(2, 2, 3, 8, 16, 128), struct(128, 128)]
-        operands += list(prior)
-    else:
-        shapes = [struct(128, 384), struct(8, 128, 128)] + [struct(*e) for e in EDGES]
-        shapes += [struct(8, 128), struct(10, 18, 16, 128), struct(2, 18, 8, 128), struct(8, 128)]
-        scratch += [vmem(8 * 128, 128)]
     return pl.pallas_call(
-        last_kernel if last else update_kernel,
-        in_specs=[pl.BlockSpec(memory_space=pl.ANY) if k == 4 else whole() for k in range(len(operands))],
+        kernel,
+        in_specs=[pl.BlockSpec(memory_space=pl.ANY) if k == 2 else whole() for k in range(len(operands))],
         out_specs=[whole()] * len(shapes),
         out_shape=shapes,
-        scratch_shapes=scratch,
+        scratch_shapes=scratch + extra,
         compiler_params=params(32),
-        name="last_update" if last else "update",
+        name=name,
     )(*operands)
 
 
@@ -762,7 +812,9 @@
 
 
 def exchange(value):
-    return lax.all_to_all(value, ("gx", "gy"), split_axis=0, concat_axis=0, tiled=True)
+    rows = value.reshape(128, 1, value.size // 128)
+    rows = lax.all_to_all(rows, ("gx", "gy"), split_axis=0, concat_axis=0, tiled=True)
+    return rows.reshape(value.shape)
 
 
 def per_device(links):
@@ -772,19 +824,30 @@
     packed, modes, edge_x, edge_y, theta, table, face_x, face_y = first_call(flat, table)
     face_x = shifted(face_x, "gx", 1)
     face_y = shifted(face_y, "gy", 1)
-    state = (modes, edge_x, edge_y, theta)
     packed, own = lax.optimization_barrier((packed, own))
-    prior = None
-    for step in range(2):
-        values = exchange(plane_call(own, exchange(packed), table))
-        results = update_call(values, state, flat, face_x, face_y, table, prior)
-        if step == 0:
-            packed, modes, edge_x, edge_y, theta, gout, gout_y, theta_first = results
-            state = (modes, edge_x, edge_y, theta)
-            prior = (gout, gout_y, theta_first)
-    div, gauge, sums = results
-    sums = jnp.sum(exchange(sums), axis=0)[:3] / (3.0 * LS * LS * NZ)
-    return (gauge, div, sums)
+    values = exchange(plane_call(own, exchange(packed), table))
+    edges = [struct(*e) for e in EDGES]
+    shapes = [struct(384, 128), struct(8, 128, 128)] + edges + [struct(8, 128)]
+    shapes += [struct(9 * 288, 128), struct(18, 8, 128)] + edges
+    packed, modes, edge1_x, edge1_y, theta1, prior, prior_y, raw_x, raw_y = update_call(
+        update_kernel,
+        [values, modes, in_hbm(flat), table],
+        shapes,
+        [vmem(8 * 192, 128), vmem(8, 16, 128), vmem(8 * 152, 128)],
+        "update",
+    )
+    packed, face_x, face_y = lax.optimization_barrier((packed, face_x, face_y))
+    values = exchange(plane_call(own, exchange(packed), table))
+    operands = [values, modes, in_hbm(flat), table, edge_x, edge_y, edge1_x, edge1_y, raw_x, raw_y]
+    operands += [face_x, face_y, theta, theta1, prior, prior_y]
+    div, gauge, sums = update_call(
+        last_kernel,
+        operands,
+        [struct(8, 8, 16, 128), struct(2, 2, 3, 8, 16, 128), struct(128, 128)],
+        [vmem(18, 16, 128), vmem(18, 8, 128), vmem(8 * 192, 128), vmem(8, 16, 128), vmem(8, 128)],
+        "last_update",
+    )
+    return (gauge, div, jnp.sum(exchange(sums)[:, :3], axis=0))
 
 
 def solution(mesh):

time: 164 us -> 161 us (0.982)
  transfers between devices with their start and end apart: 3 -> 3, of which waited for: 1 -> 1; matrix products, arithmetic and copies ran while one was open for 0% -> 0% of each run, Pallas kernels for 0% -> 4%
where the time goes in v4:
time: 161 us
  blocking collectives  111 us (69%)
  Pallas kernels  20.6 us (13%)
  waiting for transfers between devices  14.4 us (9%)
  starting transfers between devices  13 us (8%)
    all_to_all x4, blocking collectives, exchange(): lax.all_to_all(rows, ('gx', 'gy'), split_axis=0, concat_axis=0, tiled=True)  111 us
    all_to_all x1, waiting for transfers between devices, exchange(): lax.all_to_all(rows, ('gx', 'gy'), split_axis=0, concat_axis=0, tiled=True)  14.4 us
    pallas_call x2, Pallas kernels, update_call(): pl.pallas_call(kernel, in_specs=[pl.BlockSpec(memory_space=pl.ANY) if k =...  12.8 us
    all_to_all x1, starting transfers between devices, exchange(): lax.all_to_all(rows, ('gx', 'gy'), split_axis=0, concat_axis=0, tiled=True)  7.96 us
    ppermute x2, starting transfers between devices, shifted(): return lax.ppermute(value, axis, pairs)  5.02 us
    pallas_call x2, Pallas kernels, plane_call(): pl.pallas_call(plane_kernel, in_specs=[pl.BlockSpec(memory_space=pltpu.SM...  4.25 us
    pallas_call x1, Pallas kernels, first_call(): pl.pallas_call(first_kernel, in_specs=[pl.BlockSpec(memory_space=pl.ANY)]...  3.52 us
  transfers between devices with their start and end apart: 3, of which 1 were waited for; matrix products, arithmetic and copies ran while one was open for 0% of the time, Pallas kernels for 4%

profile of v4, /device:TPU:1, one launch (start us, length us, event | category | flops | bytes accessed | tf_op | source)
XLA Modules:
  0.0 160.5 jit_solution(316997729035843743)
XLA Ops:
  0.6 3.5 %first_divergence.1 = (f32[384,128]{1,0:T(8,128)S(1)}, f32[8,128,128]{2,1,0:T(8,128)S(1)}, f32[8,16,128]{2,1,0:T(8,128)S(1)}, f32[8,8,128]{2,1,0:T(8,128)S(1)}, ...) custom-call(f32[54,8,16,128]{3,2,1,0:T(8,128)} %bitcast.22, ...), custom_call_target="tpu_custom_call" | custom-call | tf_op jit(solution)/shard_map/first_divergence/pallas_call | solution.py:760
  4.2 38.2 %all_to_all.25 = f32[128,1,384]{2,1,0:T(1,128)S(1)} all-to-all(f32[128,1,384]{2,1,0:T(1,128)S(1)} %bitcast.20), channel_id=1, replica_groups=mesh['ta'=4,'gx'=16,'gy'=8] {'gx','gy'}, dimensions={0} | all-to-all | bytes 393216 | tf_op jit(solution)/shard_map/all_to_all | solution.py:816
  42.4 2.5 %plane_solve.2 = f32[384,128]{1,0:T(8,128)} custom-call(s32[1]{0:T(128)} %bitcast.1.own, f32[384,128]{1,0:T(8,128)S(1)} %bitcast.17, bf16[992,768]{1,0:T(8,128)(2,1)S(1)} %get-tuple-element.31.table.refs_3_), custom_call_target="tpu_custom_call" | custom-call | tf_op jit(solution)/shard_map/plane_solve/pallas_call | solution.py:778
  44.9 8.0 %all-to-all-start.1 = ((f32[128,1,384]{2,1,0:T(1,128)}), f32[128,1,384]{2,1,0:T(1,128)S(1)}, u32[]{:S(2)}, u32[]{:S(2)}) async-start(f32[128,1,384]{2,1,0:T(1,128)} %bitcast.4), calls=%async_computation.1 | async-start | bytes 393216 | tf_op jit(solution)/shard_map/all_to_all | solution.py:816
  52.8 3.3 %collective-permute-start = (f32[12,16,128]{2,1,0:T(8,128)S(1)}, f32[12,16,128]{2,1,0:T(8,128)S(1)}, u32[]{:S(2)}, u32[]{:S(2)}) collective-permute-start(f32[12,16,128]{2,1,0:T(8,128)S(1)} %get-tuple-element.34), channel_id=1, source_target_pairs={{0,8},{8,16},{16,24},{24,32},{32,40},{40,48},{48,56},{56,64},{64,7... | collective-permute-start | bytes 294920 | tf_op jit(solution)/shard_map/ppermute | solution.py:811
  56.1 1.7 %collective-permute-start.1 = (f32[12,8,128]{2,1,0:T(8,128)S(1)}, f32[12,8,128]{2,1,0:T(8,128)S(1)}, u32[]{:S(2)}, u32[]{:S(2)}) collective-permute-start(f32[12,8,128]{2,1,0:T(8,128)S(1)} %get-tuple-element.35), channel_id=1, source_target_pairs={{0,1},{1,2},{2,3},{3,4},{4,5},{5,6},{6,7},{7,0},{8,9},{9,10},{10,1... | collective-permute-start | bytes 147464 | tf_op jit(solution)/shard_map/ppermute | solution.py:811
  57.8 14.4 %all-to-all-done.1 = f32[128,1,384]{2,1,0:T(1,128)S(1)} async-done(((f32[128,1,384]{2,1,0:T(1,128)}), f32[128,1,384]{2,1,0:T(1,128)S(1)}, u32[]{:S(2)}, u32[]{:S(2)}) %all-to-all-start.1) | async-done | bytes 196640 | tf_op jit(solution)/shard_map/all_to_all | solution.py:816
  72.2 6.1 %update.1 = (f32[384,128]{1,0:T(8,128)S(1)}, f32[8,128,128]{2,1,0:T(8,128)S(1)}, f32[8,16,128]{2,1,0:T(8,128)S(1)}, f32[8,8,128]{2,1,0:T(8,128)S(1)}, f32[8,128]...) custom-call(f32[384,128]{1,0:T(8,128)S(1)} %bitcast.14, ...), custom_call_target="tpu_custom_call" | custom-call | tf_op jit(solution)/shard_map/update/pallas_call | solution.py:797
  78.4 0.0 collective-permute-done.1.refs_11_
  78.4 0.0 collective-permute-done.refs_10_
  78.4 24.5 %all_to_all.26 = f32[128,1,384]{2,1,0:T(1,128)S(1)} all-to-all(f32[128,1,384]{2,1,0:T(1,128)S(1)} %bitcast.19), channel_id=1, replica_groups=mesh['ta'=4,'gx'=16,'gy'=8] {'gx','gy'}, dimensions={0} | all-to-all | bytes 393216 | tf_op jit(solution)/shard_map/all_to_all | solution.py:816
  102.9 1.8 %plane_solve.3 = f32[384,128]{1,0:T(8,128)S(1)} custom-call(s32[1]{0:T(128)} %bitcast.1.own, f32[384,128]{1,0:T(8,128)S(1)} %bitcast.15, bf16[992,768]{1,0:T(8,128)(2,1)S(1)} %get-tuple-element.31.table.refs_3_), custom_call_target="tpu_custom_call" | custom-call | tf_op jit(solution)/shard_map/plane_solve/pallas_call | solution.py:778
  104.7 26.0 %all_to_all.27 = f32[128,1,384]{2,1,0:T(1,128)S(1)} all-to-all(f32[128,1,384]{2,1,0:T(1,128)S(1)} %bitcast.16), channel_id=1, replica_groups=mesh['ta'=4,'gx'=16,'gy'=8] {'gx','gy'}, dimensions={0} | all-to-all | bytes 393216 | tf_op jit(solution)/shard_map/all_to_all | solution.py:816
  130.7 6.7 %last_update.1 = (f32[8,8,16,128]{3,2,1,0:T(8,128)}, f32[2,2,3,8,16,128]{5,4,3,2,1,0:T(8,128)}, f32[128,128]{1,0:T(8,128)S(1)}) custom-call(f32[384,128]{1,0:T(8,128)S(1)} %bitcast.18, f32[8,128,128]{2,1,0:T(8,128)S(1)} %get-tuple-element.37.refs_1_, f32[54,8,16,128]{3,2,1,0:T(8,128)} %bitcast.24, bf16[992,768]{1,0:T(8,128)(2,1)S(1)} %get-tuple-element.31.table.refs_3_, ...), custom_call_target="tpu_custom_call" | custom-call | tf_op jit(solution)/shard_map/last_update/pallas_call | solution.py:797
  137.3 22.6 %all_to_all.28 = f32[128,1,128]{2,1,0:T(1,128)S(1)} all-to-all(f32[128,1,128]{2,1,0:T(1,128)S(1)} %bitcast.21), channel_id=1, replica_groups=mesh['ta'=4,'gx'=16,'gy'=8] {'gx','gy'}, dimensions={0} | all-to-all | bytes 131072 | tf_op jit(solution)/shard_map/all_to_all | solution.py:816
  160.0 0.5 slice_reduce_fusion
Async XLA Ops:
  44.9 27.4 %all-to-all-start.1 = ((f32[128,1,384]{2,1,0:T(1,128)}), f32[128,1,384]{2,1,0:T(1,128)S(1)}, u32[]{:S(2)}, u32[]{:S(2)}) async-start(f32[128,1,384]{2,1,0:T(1,128)} %bitcast.4), calls=%async_computation.1 | async-start | bytes 393216 | tf_op jit(solution)/shard_map/all_to_all | solution.py:816
  52.8 25.6 %collective-permute-start = (f32[12,16,128]{2,1,0:T(8,128)S(1)}, f32[12,16,128]{2,1,0:T(8,128)S(1)}, u32[]{:S(2)}, u32[]{:S(2)}) collective-permute-start(f32[12,16,128]{2,1,0:T(8,128)S(1)} %get-tuple-element.34), channel_id=1, source_target_pairs={{0,8},{8,16},{16,24},{24,32},{32,40},{40,48},{48,56},{56,64},{64,7... | collective-permute-start | bytes 294920 | tf_op jit(solution)/shard_map/ppermute | solution.py:811
  56.1 22.2 %collective-permute-start.1 = (f32[12,8,128]{2,1,0:T(8,128)S(1)}, f32[12,8,128]{2,1,0:T(8,128)S(1)}, u32[]{:S(2)}, u32[]{:S(2)}) collective-permute-start(f32[12,8,128]{2,1,0:T(8,128)S(1)} %get-tuple-element.35), channel_id=1, source_target_pairs={{0,1},{1,2},{2,3},{3,4},{4,5},{5,6},{6,7},{7,0},{8,9},{9,10},{10,1... | collective-permute-start | bytes 147464 | tf_op jit(solution)/shard_map/ppermute | solution.py:811

commit v5 on v4

--- a/solution.py
+++ b/solution.py
@@ -29,20 +29,21 @@
     return basis, freq
 
 
-def halves(table):
-    high = table.astype(np.float32).astype(jnp.bfloat16)
-    low = (table - high.astype(np.float64)).astype(np.float32).astype(jnp.bfloat16)
-    return high, low
+def thirds(table):
+    rest, out = table.astype(np.float32).astype(np.float64), []
+    for _ in range(3):
+        piece = rest.astype(np.float32).astype(jnp.bfloat16)
+        out.append(piece)
+        rest = rest - piece.astype(np.float64)
+    return out
 
 
 def right_table(table):
-    high, low = halves(table)
-    return np.concatenate([high, high, low], axis=0)
+    return np.concatenate(thirds(table), axis=0)
 
 
 def left_table(table):
-    high, low = halves(table)
-    return np.concatenate([high, high, low], axis=1)
+    return np.concatenate(thirds(table), axis=1)
 
 
 def sine_table():
@@ -126,9 +127,8 @@
     row[val + 33] -= 1.0
     row[val + 32] -= 1.0
     row[val + 1] -= 1.0
-    high, low = halves(out)
-    assert not np.any(low[:, 128:].astype(np.float32))
-    return np.concatenate([high, high, low[:, :128]], axis=1)
+    values = thirds(out[:, 128:])[0]
+    return np.concatenate([left_table(out[:, :128]), values, values, values], axis=1)
 
 
 def lines_in():
@@ -158,16 +158,12 @@
     out[384:512, :384] = left_table(SINE)
     out[384:512, 384:] = left_table(BASIS[ORDER].T)
     out[512:640, :384] = left_table(BASIS[ORDER])
-    out[512:640, 384:528] = left_table(source_table())
+    high, middle, low = thirds(source_table())
+    out[512:640, 384:672] = np.concatenate([high, high, high, middle, middle, low], axis=1)
     out[640:688, :384] = left_table(reduce_table())
-    out[688:864, :480] = expand_table()
+    out[688:864, :528] = expand_table()
     for k, table in enumerate((INVERSE, PLANE_SUM)):
-        rest = table.astype(np.float32).astype(np.float64)
-        for part in range(3):
-            piece = rest.astype(np.float32).astype(jnp.bfloat16)
-            lanes = 384 * k + 128 * part
-            out[864:992, lanes : lanes + 128] = piece
-            rest = rest - piece.astype(np.float64)
+        out[864:992, 384 * k : 384 * k + 384] = left_table(table)
     return out
 
 
@@ -178,9 +174,10 @@
 MODES = (slice(384, 512), slice(0, 384))
 X_IN = (slice(384, 512), slice(384, 768))
 X_OUT = (slice(512, 640), slice(0, 384))
-SOURCE = (slice(512, 640), slice(384, 528))
+SOURCE = (slice(512, 640), slice(384, 672))
 REDUCE = (slice(640, 688), slice(0, 384))
-EXPAND = (slice(688, 864), slice(0, 480))
+EXPAND = (slice(688, 864), slice(0, 384))
+EXPAND_LINES = (slice(688, 864), slice(384, 528))
 
 
 def float_table(table, which, rows=128):
@@ -191,16 +188,34 @@
     return (parts[0] + parts[1]) + parts[2]
 
 
-def three_lanes(value):
+def parts_of(value):
     high = value.astype(BF16)
-    low = (value - high.astype(F32)).astype(BF16)
-    return jnp.concatenate([high, low, high], axis=1)
-
-
-def three_rows(value):
-    high = value.astype(BF16)
-    low = (value - high.astype(F32)).astype(BF16)
-    return jnp.concatenate([high, low, high], axis=0)
+    rest = value - high.astype(F32)
+    middle = rest.astype(BF16)
+    return high, middle, (rest - middle.astype(F32)).astype(BF16)
+
+
+def products(value, axis, fine):
+    high, middle, low = parts_of(value)
+    parts = [high, middle, low, high, middle, high] if fine else [high, middle, high]
+    return jnp.concatenate(parts, axis=axis)
+
+
+def chosen(fine):
+    return (0, 0, 0, 1, 1, 2) if fine else (0, 0, 1)
+
+
+def right_dot(value, table, place, fine):
+    rows, lanes = place
+    parts = [table[rows.start + 128 * k : rows.start + 128 * k + 128, lanes] for k in chosen(fine)]
+    return dot(products(value, 1, fine), jnp.concatenate(parts, axis=0))
+
+
+def left_dot(table, place, pieces, fine):
+    rows, lanes = place
+    parts = [table[rows, lanes.start + 128 * k : lanes.start + 128 * k + 128] for k in chosen(fine)]
+    pieces = [products(piece, 0, fine) for piece in pieces]
+    return dot(jnp.concatenate(parts, axis=1), jnp.concatenate(pieces, axis=1))
 
 
 def swap_blocks(tiles):
@@ -358,22 +373,18 @@
     return jnp.dot(left, right, preferred_element_type=F32)
 
 
-def wide(pieces):
-    return jnp.concatenate([three_rows(piece) for piece in pieces], axis=1)
-
-
 def tile(value, c):
     return value[:, 128 * c : 128 * c + 128]
 
 
 def encode(spectrum, stride, table, modes, packed, out):
-    mode = dot(table[MODES], wide([spectrum[pl.ds(stride * c, 128), :] for c in range(8)]))
+    mode = left_dot(table, MODES, [spectrum[pl.ds(stride * c, 128), :] for c in range(8)], False)
     inverse = float_table(table, 0)
     scaled = []
     for c in range(8):
         scaled.append(inverse * tile(mode, c))
         modes[c] = scaled[c]
-    reduced = dot(table[REDUCE], wide(scaled))
+    reduced = left_dot(table, REDUCE, scaled, False)
     corner = lax.broadcasted_iota(jnp.int32, (8, 128), 0) == 0
     for c in range(8):
         start = stride * c
@@ -438,7 +449,7 @@
     for k in range(12):
         face_x[k] = links[k % 6 + 9 * (k // 6), 7]
     table_copy.wait()
-    sources[...] = dot(three_lanes(sources[...]), table[Z_IN])
+    sources[...] = right_dot(sources[...], table, Z_IN, False)
     encode(sources, 152, table, modes, packed, out)
 
 
@@ -464,18 +475,18 @@
             work[pl.ds(128 * x + 16 * c, 16), :] = jnp.where(lane == x, both, 0.0)
         extra = jnp.sum(jnp.where(lane == 0, third, 0.0), axis=0, keepdims=True)
         shifts.append(jnp.sum(extra, axis=1, keepdims=True) * zero)
-    lines[pl.ds(0, 128), :] = dot(three_lanes(work[pl.ds(0, 128), :]), table[Y_IN])
-    lines[pl.ds(128, 896), :] = dot(three_lanes(work[pl.ds(128, 896), :]), table[LINES_IN])
+    lines[pl.ds(0, 128), :] = right_dot(work[pl.ds(0, 128), :], table, Y_IN, False)
+    lines[pl.ds(128, 896), :] = right_dot(work[pl.ds(128, 896), :], table, LINES_IN, False)
     blocks = [
         jnp.concatenate([lines[pl.ds(128 * x + 16 * c, 16), :] for x in range(8)], axis=0)
         for c in range(8)
     ]
-    spectrum = dot(table[X_IN], wide(blocks))
-    spectrum = dot(table[X_OUT], wide([tile(spectrum, c) * inverse for c in range(8)]))
+    spectrum = left_dot(table, X_IN, blocks, False)
+    spectrum = left_dot(table, X_OUT, [tile(spectrum, c) * inverse for c in range(8)], True)
     spectrum = [tile(spectrum, c) for c in range(8)]
-    at_lines = dot(three_lanes(jnp.concatenate(spectrum, axis=0)), table[LINES_OUT])
+    at_lines = right_dot(jnp.concatenate(spectrum, axis=0), table, LINES_OUT, True)
     first = jnp.concatenate([part[:16] for part in spectrum], axis=0)
-    first = dot(three_lanes(first), table[Z_OUT])
+    first = right_dot(first, table, Z_OUT, True)
     groups = [[], [], []]
     for c in range(8):
         own_line = first[16 * c : 16 * c + 16] + shifts[c]
@@ -501,15 +512,14 @@
         jnp.concatenate([packed[pl.ds(128 * t + 16 * c, 16), :] for t in range(3)], axis=0)
         for c in range(8)
     ]
-    mode = dot(table[SOURCE], wide(values))
+    mode = dot(table[SOURCE], jnp.concatenate([products(value, 0, True) for value in values], axis=1))
     stacks = []
     for c in range(8):
         own = modes[c] + inverse * tile(mode, c)
-        value = jnp.concatenate([own, values[c]], axis=0)
-        high = value.astype(BF16)
-        low = (value - high.astype(F32)).astype(BF16)
-        stacks.append(jnp.concatenate([high, low, high[:128]], axis=0))
-    sites = dot(table[EXPAND], jnp.concatenate(stacks, axis=1))
+        stacks.append(own)
+    sites = left_dot(table, EXPAND, stacks, True)
+    exact = [jnp.concatenate(parts_of(value), axis=0) for value in values]
+    sites = sites + dot(table[EXPAND_LINES], jnp.concatenate(exact, axis=1))
     row = lax.broadcasted_iota(jnp.int32, (16, 128), 0)
     parts = []
     for c in range(8):
@@ -517,7 +527,7 @@
         behind = part[144:160] + mass * jnp.where(row == 0, 0.0, value[0:16])
         below = part[168:176] + mass * jnp.where(row[:8] == 0, value[0:8], value[32:40])
         parts.append(jnp.concatenate([part[:144], behind, part[160:168], below], axis=0))
-    comps_in[...] = dot(three_lanes(jnp.concatenate(parts, axis=0)), table[Z_OUT])
+    comps_in[...] = right_dot(jnp.concatenate(parts, axis=0), table, Z_OUT, True)
 
 
 def make(c, before=None):
@@ -617,7 +627,7 @@
         sources[pl.ds(152 * c + 128, 16), :] = prev[c]
         edge_x[c] = sources[pl.ds(152 * c, 16), :]
         edge_y[c] = sources[pl.ds(152 * c, 8, stride=16), :]
-    sources[...] = dot(three_lanes(sources[...]), table[Z_IN])
+    sources[...] = right_dot(sources[...], table, Z_IN, False)
     encode(sources, 152, table, modes_out, packed, out)
 
 
@@ -633,8 +643,8 @@
 
 def last_kernel(*refs):
     recv, modes, links_hbm, table, line0_x, line0_y, line1_x, line1_y, raw_x, raw_y = refs[:10]
-    face_x, face_y, theta0, theta1, prior, prior_y, div, gauge, theta = refs[10:19]
-    links, sems, packed, comps_in, gs, behind, below, ay, prev, acc = refs[19:]
+    face_x, face_y, theta0, theta1, prior, prior_y, div_hbm, gauge_hbm, theta = refs[10:19]
+    links, sems, packed, comps_in, gs, behind, below, ay, prev, acc, div, gauge, out_sems = refs[19:]
     plane_copy = start_links(links_hbm, links, sems)
     decode(recv, modes, table, packed, comps_in)
     row = lax.broadcasted_iota(jnp.int32, (16, 128), 0)
@@ -690,6 +700,12 @@
         return carry
 
     lax.fori_loop(0, 8, inner, 0)
+    gauge_copy = pltpu.make_async_copy(gauge, gauge_hbm, out_sems.at[8])
+    gauge_copy.start()
+
+    def div_copy(x):
+        return pltpu.make_async_copy(div.at[:, x], div_hbm.at[:, x], out_sems.at[x])
+
     plane(
         0,
         lambda c: 176 * c + 144,
@@ -722,6 +738,8 @@
         for c in range(8):
             div[c, x, pl.ds(8 * half, 8), :] = total[c]
         acc[...] += squares(total)
+        if half == 1:
+            div_copy(x).start()
 
     moved_divergence(links, plane_copy, gs, ay, prev, emit)
     lane = lax.broadcasted_iota(jnp.int32, (1, 128), 1)
@@ -729,6 +747,9 @@
     for k, part in enumerate((theta0[...] + extra0, theta1[...] + extra1, acc[...])):
         sums = sums + jnp.where(lane == k, jnp.sum(part), 0.0)
     theta[...] = jnp.broadcast_to(sums * (1.0 / (3.0 * LS * LS * NZ)), (128, 128))
+    gauge_copy.wait()
+    for x in range(8):
+        div_copy(x).wait()
 
 
 def struct(*shape):
@@ -786,7 +807,7 @@
     )(own, recv, table)
 
 
-def update_call(kernel, operands, shapes, extra, name):
+def update_call(kernel, operands, shapes, extra, name, copied=0):
     scratch = [
         vmem(54, 8, 16, 128),
         pltpu.SemaphoreType.DMA((8,)),
@@ -797,7 +818,7 @@
     return pl.pallas_call(
         kernel,
         in_specs=[pl.BlockSpec(memory_space=pl.ANY) if k == 2 else whole() for k in range(len(operands))],
-        out_specs=[whole()] * len(shapes),
+        out_specs=[pl.BlockSpec(memory_space=pl.ANY)] * copied + [whole()] * (len(shapes) - copied),
         out_shape=shapes,
         scratch_shapes=scratch + extra,
         compiler_params=params(32),
@@ -844,8 +865,10 @@
         last_kernel,
         operands,
         [struct(8, 8, 16, 128), struct(2, 2, 3, 8, 16, 128), struct(128, 128)],
-        [vmem(18, 16, 128), vmem(18, 8, 128), vmem(8 * 192, 128), vmem(8, 16, 128), vmem(8, 128)],
+        [vmem(18, 16, 128), vmem(18, 8, 128), vmem(8 * 192, 128), vmem(8, 16, 128), vmem(8, 128)]
+        + [vmem(8, 8, 16, 128), vmem(2, 2, 3, 8, 16, 128), pltpu.SemaphoreType.DMA((9,))],
         "last_update",
+        2,
     )
     return (gauge, div, jnp.sum(exchange(sums)[:, :3], axis=0))
 

time: 161 us -> 162 us (level)
  Pallas kernels: 20.6 us -> 22.3 us
where the time goes in v5:
time: 162 us
  blocking collectives  111 us (69%)
  Pallas kernels  22.3 us (14%)
  waiting for transfers between devices  14.4 us (9%)
  starting transfers between devices  13 us (8%)
    all_to_all x4, blocking collectives, exchange(): lax.all_to_all(rows, ('gx', 'gy'), split_axis=0, concat_axis=0, tiled=True)  111 us
    all_to_all x1, waiting for transfers between devices, exchange(): lax.all_to_all(rows, ('gx', 'gy'), split_axis=0, concat_axis=0, tiled=True)  14.4 us
    pallas_call x2, Pallas kernels, update_call(): pl.pallas_call(kernel, in_specs=[pl.BlockSpec(memory_space=pl.ANY) if k =...  14.2 us
    all_to_all x1, starting transfers between devices, exchange(): lax.all_to_all(rows, ('gx', 'gy'), split_axis=0, concat_axis=0, tiled=True)  7.96 us
    ppermute x2, starting transfers between devices, shifted(): return lax.ppermute(value, axis, pairs)  5.02 us
    pallas_call x2, Pallas kernels, plane_call(): pl.pallas_call(plane_kernel, in_specs=[pl.BlockSpec(memory_space=pltpu.SM...  4.6 us
    pallas_call x1, Pallas kernels, first_call(): pl.pallas_call(first_kernel, in_specs=[pl.BlockSpec(memory_space=pl.ANY)]...  3.52 us
  transfers between devices with their start and end apart: 3, of which 1 were waited for; matrix products, arithmetic and copies ran while one was open for 0% of the time, Pallas kernels for 4%

profile of v5, /device:TPU:1, one launch (start us, length us, event | category | flops | bytes accessed | tf_op | source)
XLA Modules:
  0.0 162.1 jit_solution(9799862735354960949)
XLA Ops:
  0.6 3.5 %first_divergence.1 = (f32[384,128]{1,0:T(8,128)S(1)}, f32[8,128,128]{2,1,0:T(8,128)S(1)}, f32[8,16,128]{2,1,0:T(8,128)S(1)}, f32[8,8,128]{2,1,0:T(8,128)S(1)}, ...) custom-call(f32[54,8,16,128]{3,2,1,0:T(8,128)} %bitcast.22, ...), custom_call_target="tpu_custom_call" | custom-call | tf_op jit(solution)/shard_map/first_divergence/pallas_call | solution.py:781
  4.2 38.2 %all_to_all.25 = f32[128,1,384]{2,1,0:T(1,128)S(1)} all-to-all(f32[128,1,384]{2,1,0:T(1,128)S(1)} %bitcast.20), channel_id=1, replica_groups=mesh['ta'=4,'gx'=16,'gy'=8] {'gx','gy'}, dimensions={0} | all-to-all | bytes 393216 | tf_op jit(solution)/shard_map/all_to_all | solution.py:837
  42.4 2.6 %plane_solve.2 = f32[384,128]{1,0:T(8,128)} custom-call(s32[1]{0:T(128)} %bitcast.1.own, f32[384,128]{1,0:T(8,128)S(1)} %bitcast.17, bf16[992,768]{1,0:T(8,128)(2,1)S(1)} %get-tuple-element.31.table.refs_3_), custom_call_target="tpu_custom_call" | custom-call | tf_op jit(solution)/shard_map/plane_solve/pallas_call | solution.py:799
  45.0 8.0 %all-to-all-start.1 = ((f32[128,1,384]{2,1,0:T(1,128)}), f32[128,1,384]{2,1,0:T(1,128)S(1)}, u32[]{:S(2)}, u32[]{:S(2)}) async-start(f32[128,1,384]{2,1,0:T(1,128)} %bitcast.4), calls=%async_computation.1 | async-start | bytes 393216 | tf_op jit(solution)/shard_map/all_to_all | solution.py:837
  53.0 3.3 %collective-permute-start = (f32[12,16,128]{2,1,0:T(8,128)S(1)}, f32[12,16,128]{2,1,0:T(8,128)S(1)}, u32[]{:S(2)}, u32[]{:S(2)}) collective-permute-start(f32[12,16,128]{2,1,0:T(8,128)S(1)} %get-tuple-element.34), channel_id=1, source_target_pairs={{0,8},{8,16},{16,24},{24,32},{32,40},{40,48},{48,56},{56,64},{64,7... | collective-permute-start | bytes 294920 | tf_op jit(solution)/shard_map/ppermute | solution.py:832
  56.3 1.7 %collective-permute-start.1 = (f32[12,8,128]{2,1,0:T(8,128)S(1)}, f32[12,8,128]{2,1,0:T(8,128)S(1)}, u32[]{:S(2)}, u32[]{:S(2)}) collective-permute-start(f32[12,8,128]{2,1,0:T(8,128)S(1)} %get-tuple-element.35), channel_id=1, source_target_pairs={{0,1},{1,2},{2,3},{3,4},{4,5},{5,6},{6,7},{7,0},{8,9},{9,10},{10,1... | collective-permute-start | bytes 147464 | tf_op jit(solution)/shard_map/ppermute | solution.py:832
  58.0 14.4 %all-to-all-done.1 = f32[128,1,384]{2,1,0:T(1,128)S(1)} async-done(((f32[128,1,384]{2,1,0:T(1,128)}), f32[128,1,384]{2,1,0:T(1,128)S(1)}, u32[]{:S(2)}, u32[]{:S(2)}) %all-to-all-start.1) | async-done | bytes 196640 | tf_op jit(solution)/shard_map/all_to_all | solution.py:837
  72.4 7.2 %update.1 = (f32[384,128]{1,0:T(8,128)S(1)}, f32[8,128,128]{2,1,0:T(8,128)S(1)}, f32[8,16,128]{2,1,0:T(8,128)S(1)}, f32[8,8,128]{2,1,0:T(8,128)S(1)}, f32[8,128]...) custom-call(f32[384,128]{1,0:T(8,128)S(1)} %bitcast.14, ...), custom_call_target="tpu_custom_call" | custom-call | tf_op jit(solution)/shard_map/update/pallas_call | solution.py:818
  79.6 0.0 collective-permute-done.1.refs_11_
  79.6 0.0 collective-permute-done.refs_10_
  79.6 24.5 %all_to_all.26 = f32[128,1,384]{2,1,0:T(1,128)S(1)} all-to-all(f32[128,1,384]{2,1,0:T(1,128)S(1)} %bitcast.19), channel_id=1, replica_groups=mesh['ta'=4,'gx'=16,'gy'=8] {'gx','gy'}, dimensions={0} | all-to-all | bytes 393216 | tf_op jit(solution)/shard_map/all_to_all | solution.py:837
  104.2 2.0 %plane_solve.3 = f32[384,128]{1,0:T(8,128)S(1)} custom-call(s32[1]{0:T(128)} %bitcast.1.own, f32[384,128]{1,0:T(8,128)S(1)} %bitcast.15, bf16[992,768]{1,0:T(8,128)(2,1)S(1)} %get-tuple-element.31.table.refs_3_), custom_call_target="tpu_custom_call" | custom-call | tf_op jit(solution)/shard_map/plane_solve/pallas_call | solution.py:799
  106.1 25.8 %all_to_all.27 = f32[128,1,384]{2,1,0:T(1,128)S(1)} all-to-all(f32[128,1,384]{2,1,0:T(1,128)S(1)} %bitcast.16), channel_id=1, replica_groups=mesh['ta'=4,'gx'=16,'gy'=8] {'gx','gy'}, dimensions={0} | all-to-all | bytes 393216 | tf_op jit(solution)/shard_map/all_to_all | solution.py:837
  131.9 7.0 %last_update.1 = (f32[8,8,16,128]{3,2,1,0:T(8,128)}, f32[2,2,3,8,16,128]{5,4,3,2,1,0:T(8,128)}, f32[128,128]{1,0:T(8,128)S(1)}) custom-call(f32[384,128]{1,0:T(8,128)S(1)} %bitcast.18, f32[8,128,128]{2,1,0:T(8,128)S(1)} %get-tuple-element.37.refs_1_, f32[54,8,16,128]{3,2,1,0:T(8,128)} %bitcast.24, bf16[992,768]{1,0:T(8,128)(2,1)S(1)} %get-tuple-element.31.table.refs_3_, ...), custom_call_target="tpu_custom_call" | custom-call | tf_op jit(solution)/shard_map/last_update/pallas_call | solution.py:818
  138.9 22.7 %all_to_all.28 = f32[128,1,128]{2,1,0:T(1,128)S(1)} all-to-all(f32[128,1,128]{2,1,0:T(1,128)S(1)} %bitcast.21), channel_id=1, replica_groups=mesh['ta'=4,'gx'=16,'gy'=8] {'gx','gy'}, dimensions={0} | all-to-all | bytes 131072 | tf_op jit(solution)/shard_map/all_to_all | solution.py:837
  161.6 0.5 slice_reduce_fusion
Async XLA Ops:
  45.0 27.4 %all-to-all-start.1 = ((f32[128,1,384]{2,1,0:T(1,128)}), f32[128,1,384]{2,1,0:T(1,128)S(1)}, u32[]{:S(2)}, u32[]{:S(2)}) async-start(f32[128,1,384]{2,1,0:T(1,128)} %bitcast.4), calls=%async_computation.1 | async-start | bytes 393216 | tf_op jit(solution)/shard_map/all_to_all | solution.py:837
  53.0 26.6 %collective-permute-start = (f32[12,16,128]{2,1,0:T(8,128)S(1)}, f32[12,16,128]{2,1,0:T(8,128)S(1)}, u32[]{:S(2)}, u32[]{:S(2)}) collective-permute-start(f32[12,16,128]{2,1,0:T(8,128)S(1)} %get-tuple-element.34), channel_id=1, source_target_pairs={{0,8},{8,16},{16,24},{24,32},{32,40},{40,48},{48,56},{56,64},{64,7... | collective-permute-start | bytes 294920 | tf_op jit(solution)/shard_map/ppermute | solution.py:832
  56.3 23.3 %collective-permute-start.1 = (f32[12,8,128]{2,1,0:T(8,128)S(1)}, f32[12,8,128]{2,1,0:T(8,128)S(1)}, u32[]{:S(2)}, u32[]{:S(2)}) collective-permute-start(f32[12,8,128]{2,1,0:T(8,128)S(1)} %get-tuple-element.35), channel_id=1, source_target_pairs={{0,1},{1,2},{2,3},{3,4},{4,5},{5,6},{6,7},{7,0},{8,9},{9,10},{10,1... | collective-permute-start | bytes 147464 | tf_op jit(solution)/shard_map/ppermute | solution.py:832

commit v6 on v5

--- a/solution.py
+++ b/solution.py
@@ -527,7 +527,9 @@
         behind = part[144:160] + mass * jnp.where(row == 0, 0.0, value[0:16])
         below = part[168:176] + mass * jnp.where(row[:8] == 0, value[0:8], value[32:40])
         parts.append(jnp.concatenate([part[:144], behind, part[160:168], below], axis=0))
-    comps_in[...] = right_dot(jnp.concatenate(parts, axis=0), table, Z_OUT, True)
+    for k in range(0, 8, 2):
+        group = jnp.concatenate(parts[k : k + 2], axis=0)
+        comps_in[pl.ds(176 * k, 352), :] = right_dot(group, table, Z_OUT, True)
 
 
 def make(c, before=None):

time: 162 us -> 162 us (level)
  no operation moved by 1% of the time
where the time goes in v6:
time: 162 us; the launch traced here: 161 us
  blocking collectives  111 us (69%)
  Pallas kernels  21.5 us (13%)
  waiting for transfers between devices  14.4 us (9%)
  starting transfers between devices  13 us (8%)
    all_to_all x4, blocking collectives, exchange(): lax.all_to_all(rows, ('gx', 'gy'), split_axis=0, concat_axis=0, tiled=True)  111 us
    all_to_all x1, waiting for transfers between devices, exchange(): lax.all_to_all(rows, ('gx', 'gy'), split_axis=0, concat_axis=0, tiled=True)  14.4 us
    pallas_call x2, Pallas kernels, update_call(): pl.pallas_call(kernel, in_specs=[pl.BlockSpec(memory_space=pl.ANY) if k =...  13.4 us
    all_to_all x1, starting transfers between devices, exchange(): lax.all_to_all(rows, ('gx', 'gy'), split_axis=0, concat_axis=0, tiled=True)  7.96 us
    ppermute x2, starting transfers between devices, shifted(): return lax.ppermute(value, axis, pairs)  5.02 us
    pallas_call x2, Pallas kernels, plane_call(): pl.pallas_call(plane_kernel, in_specs=[pl.BlockSpec(memory_space=pltpu.SM...  4.6 us
    pallas_call x1, Pallas kernels, first_call(): pl.pallas_call(first_kernel, in_specs=[pl.BlockSpec(memory_space=pl.ANY)]...  3.52 us
  transfers between devices with their start and end apart: 3, of which 1 were waited for; matrix products, arithmetic and copies ran while one was open for 0% of the time, Pallas kernels for 4%

profile of v6, /device:TPU:1, one launch (start us, length us, event | category | flops | bytes accessed | tf_op | source)
XLA Modules:
  0.0 161.3 jit_solution(4738231682980032129)
XLA Ops:
  0.6 3.5 %first_divergence.1 = (f32[384,128]{1,0:T(8,128)S(1)}, f32[8,128,128]{2,1,0:T(8,128)S(1)}, f32[8,16,128]{2,1,0:T(8,128)S(1)}, f32[8,8,128]{2,1,0:T(8,128)S(1)}, ...) custom-call(f32[54,8,16,128]{3,2,1,0:T(8,128)} %bitcast.22, ...), custom_call_target="tpu_custom_call" | custom-call | tf_op jit(solution)/shard_map/first_divergence/pallas_call | solution.py:783
  4.2 38.2 %all_to_all.25 = f32[128,1,384]{2,1,0:T(1,128)S(1)} all-to-all(f32[128,1,384]{2,1,0:T(1,128)S(1)} %bitcast.20), channel_id=1, replica_groups=mesh['ta'=4,'gx'=16,'gy'=8] {'gx','gy'}, dimensions={0} | all-to-all | bytes 393216 | tf_op jit(solution)/shard_map/all_to_all | solution.py:839
  42.4 2.6 %plane_solve.2 = f32[384,128]{1,0:T(8,128)} custom-call(s32[1]{0:T(128)} %bitcast.1.own, f32[384,128]{1,0:T(8,128)S(1)} %bitcast.17, bf16[992,768]{1,0:T(8,128)(2,1)S(1)} %get-tuple-element.31.table.refs_3_), custom_call_target="tpu_custom_call" | custom-call | tf_op jit(solution)/shard_map/plane_solve/pallas_call | solution.py:801
  45.0 8.0 %all-to-all-start.1 = ((f32[128,1,384]{2,1,0:T(1,128)}), f32[128,1,384]{2,1,0:T(1,128)S(1)}, u32[]{:S(2)}, u32[]{:S(2)}) async-start(f32[128,1,384]{2,1,0:T(1,128)} %bitcast.4), calls=%async_computation.1 | async-start | bytes 393216 | tf_op jit(solution)/shard_map/all_to_all | solution.py:839
  53.0 3.3 %collective-permute-start = (f32[12,16,128]{2,1,0:T(8,128)S(1)}, f32[12,16,128]{2,1,0:T(8,128)S(1)}, u32[]{:S(2)}, u32[]{:S(2)}) collective-permute-start(f32[12,16,128]{2,1,0:T(8,128)S(1)} %get-tuple-element.34), channel_id=1, source_target_pairs={{0,8},{8,16},{16,24},{24,32},{32,40},{40,48},{48,56},{56,64},{64,7... | collective-permute-start | bytes 294920 | tf_op jit(solution)/shard_map/ppermute | solution.py:834
  56.3 1.7 %collective-permute-start.1 = (f32[12,8,128]{2,1,0:T(8,128)S(1)}, f32[12,8,128]{2,1,0:T(8,128)S(1)}, u32[]{:S(2)}, u32[]{:S(2)}) collective-permute-start(f32[12,8,128]{2,1,0:T(8,128)S(1)} %get-tuple-element.35), channel_id=1, source_target_pairs={{0,1},{1,2},{2,3},{3,4},{4,5},{5,6},{6,7},{7,0},{8,9},{9,10},{10,1... | collective-permute-start | bytes 147464 | tf_op jit(solution)/shard_map/ppermute | solution.py:834
  58.0 14.4 %all-to-all-done.1 = f32[128,1,384]{2,1,0:T(1,128)S(1)} async-done(((f32[128,1,384]{2,1,0:T(1,128)}), f32[128,1,384]{2,1,0:T(1,128)S(1)}, u32[]{:S(2)}, u32[]{:S(2)}) %all-to-all-start.1) | async-done | bytes 196640 | tf_op jit(solution)/shard_map/all_to_all | solution.py:839
  72.4 6.5 %update.1 = (f32[384,128]{1,0:T(8,128)S(1)}, f32[8,128,128]{2,1,0:T(8,128)S(1)}, f32[8,16,128]{2,1,0:T(8,128)S(1)}, f32[8,8,128]{2,1,0:T(8,128)S(1)}, f32[8,128]...) custom-call(f32[384,128]{1,0:T(8,128)S(1)} %bitcast.14, ...), custom_call_target="tpu_custom_call" | custom-call | tf_op jit(solution)/shard_map/update/pallas_call | solution.py:820
  78.9 0.0 collective-permute-done.1.refs_11_
  78.9 0.0 collective-permute-done.refs_10_
  78.9 24.5 %all_to_all.26 = f32[128,1,384]{2,1,0:T(1,128)S(1)} all-to-all(f32[128,1,384]{2,1,0:T(1,128)S(1)} %bitcast.19), channel_id=1, replica_groups=mesh['ta'=4,'gx'=16,'gy'=8] {'gx','gy'}, dimensions={0} | all-to-all | bytes 393216 | tf_op jit(solution)/shard_map/all_to_all | solution.py:839
  103.4 2.0 %plane_solve.3 = f32[384,128]{1,0:T(8,128)S(1)} custom-call(s32[1]{0:T(128)} %bitcast.1.own, f32[384,128]{1,0:T(8,128)S(1)} %bitcast.15, bf16[992,768]{1,0:T(8,128)(2,1)S(1)} %get-tuple-element.31.table.refs_3_), custom_call_target="tpu_custom_call" | custom-call | tf_op jit(solution)/shard_map/plane_solve/pallas_call | solution.py:801
  105.4 25.8 %all_to_all.27 = f32[128,1,384]{2,1,0:T(1,128)S(1)} all-to-all(f32[128,1,384]{2,1,0:T(1,128)S(1)} %bitcast.16), channel_id=1, replica_groups=mesh['ta'=4,'gx'=16,'gy'=8] {'gx','gy'}, dimensions={0} | all-to-all | bytes 393216 | tf_op jit(solution)/shard_map/all_to_all | solution.py:839
  131.2 6.9 %last_update.1 = (f32[8,8,16,128]{3,2,1,0:T(8,128)}, f32[2,2,3,8,16,128]{5,4,3,2,1,0:T(8,128)}, f32[128,128]{1,0:T(8,128)S(1)}) custom-call(f32[384,128]{1,0:T(8,128)S(1)} %bitcast.18, f32[8,128,128]{2,1,0:T(8,128)S(1)} %get-tuple-element.37.refs_1_, f32[54,8,16,128]{3,2,1,0:T(8,128)} %bitcast.24, bf16[992,768]{1,0:T(8,128)(2,1)S(1)} %get-tuple-element.31.table.refs_3_, ...), custom_call_target="tpu_custom_call" | custom-call | tf_op jit(solution)/shard_map/last_update/pallas_call | solution.py:820
  138.1 22.7 %all_to_all.28 = f32[128,1,128]{2,1,0:T(1,128)S(1)} all-to-all(f32[128,1,128]{2,1,0:T(1,128)S(1)} %bitcast.21), channel_id=1, replica_groups=mesh['ta'=4,'gx'=16,'gy'=8] {'gx','gy'}, dimensions={0} | all-to-all | bytes 131072 | tf_op jit(solution)/shard_map/all_to_all | solution.py:839
  160.8 0.5 slice_reduce_fusion
Async XLA Ops:
  45.0 27.4 %all-to-all-start.1 = ((f32[128,1,384]{2,1,0:T(1,128)}), f32[128,1,384]{2,1,0:T(1,128)S(1)}, u32[]{:S(2)}, u32[]{:S(2)}) async-start(f32[128,1,384]{2,1,0:T(1,128)} %bitcast.4), calls=%async_computation.1 | async-start | bytes 393216 | tf_op jit(solution)/shard_map/all_to_all | solution.py:839
  53.0 25.9 %collective-permute-start = (f32[12,16,128]{2,1,0:T(8,128)S(1)}, f32[12,16,128]{2,1,0:T(8,128)S(1)}, u32[]{:S(2)}, u32[]{:S(2)}) collective-permute-start(f32[12,16,128]{2,1,0:T(8,128)S(1)} %get-tuple-element.34), channel_id=1, source_target_pairs={{0,8},{8,16},{16,24},{24,32},{32,40},{40,48},{48,56},{56,64},{64,7... | collective-permute-start | bytes 294920 | tf_op jit(solution)/shard_map/ppermute | solution.py:834
  56.3 22.6 %collective-permute-start.1 = (f32[12,8,128]{2,1,0:T(8,128)S(1)}, f32[12,8,128]{2,1,0:T(8,128)S(1)}, u32[]{:S(2)}, u32[]{:S(2)}) collective-permute-start(f32[12,8,128]{2,1,0:T(8,128)S(1)} %get-tuple-element.35), channel_id=1, source_target_pairs={{0,1},{1,2},{2,3},{3,4},{4,5},{5,6},{6,7},{7,0},{8,9},{9,10},{10,1... | collective-permute-start | bytes 147464 | tf_op jit(solution)/shard_map/ppermute | solution.py:834

commit v7 on v6

--- a/solution.py
+++ b/solution.py
@@ -604,7 +604,7 @@
         plane(x + 1, lambda c: 176 * c + 16 * x)
         return carry
 
-    lax.fori_loop(0, 8, inner, 0)
+    lax.fori_loop(0, 8, inner, 0, unroll=2)
     plane(9, lambda c: 176 * c + 128)
     g = make([comps_in[pl.ds(176 * c + 160, 8), :] for c in range(8)])
     for k in range(18):
@@ -701,7 +701,7 @@
         plane(x + 1, lambda c: 176 * c + 16 * x, before_at(x + 1))
         return carry
 
-    lax.fori_loop(0, 8, inner, 0)
+    lax.fori_loop(0, 8, inner, 0, unroll=2)
     gauge_copy = pltpu.make_async_copy(gauge, gauge_hbm, out_sems.at[8])
     gauge_copy.start()
 

time: 162 us -> 162 us (level)
  no operation moved by 1% of the time
where the time goes in v7:
time: 162 us; the launch traced here: 161 us
  blocking collectives  111 us (69%)
  Pallas kernels  21.4 us (13%)
  waiting for transfers between devices  14.4 us (9%)
  starting transfers between devices  13 us (8%)
    all_to_all x4, blocking collectives, exchange(): lax.all_to_all(rows, ('gx', 'gy'), split_axis=0, concat_axis=0, tiled=True)  111 us
    all_to_all x1, waiting for transfers between devices, exchange(): lax.all_to_all(rows, ('gx', 'gy'), split_axis=0, concat_axis=0, tiled=True)  14.4 us
    pallas_call x2, Pallas kernels, update_call(): pl.pallas_call(kernel, in_specs=[pl.BlockSpec(memory_space=pl.ANY) if k =...  13.3 us
    all_to_all x1, starting transfers between devices, exchange(): lax.all_to_all(rows, ('gx', 'gy'), split_axis=0, concat_axis=0, tiled=True)  7.96 us
    ppermute x2, starting transfers between devices, shifted(): return lax.ppermute(value, axis, pairs)  5.02 us
    pallas_call x2, Pallas kernels, plane_call(): pl.pallas_call(plane_kernel, in_specs=[pl.BlockSpec(memory_space=pltpu.SM...  4.6 us
    pallas_call x1, Pallas kernels, first_call(): pl.pallas_call(first_kernel, in_specs=[pl.BlockSpec(memory_space=pl.ANY)]...  3.52 us
  transfers between devices with their start and end apart: 3, of which 1 were waited for; matrix products, arithmetic and copies ran while one was open for 0% of the time, Pallas kernels for 4%

profile of v7, /device:TPU:1, one launch (start us, length us, event | category | flops | bytes accessed | tf_op | source)
XLA Modules:
  0.0 161.2 jit_solution(5307108935047577458)
XLA Ops:
  0.6 3.5 %first_divergence.1 = (f32[384,128]{1,0:T(8,128)S(1)}, f32[8,128,128]{2,1,0:T(8,128)S(1)}, f32[8,16,128]{2,1,0:T(8,128)S(1)}, f32[8,8,128]{2,1,0:T(8,128)S(1)}, ...) custom-call(f32[54,8,16,128]{3,2,1,0:T(8,128)} %bitcast.22, ...), custom_call_target="tpu_custom_call" | custom-call | tf_op jit(solution)/shard_map/first_divergence/pallas_call | solution.py:783
  4.2 38.2 %all_to_all.25 = f32[128,1,384]{2,1,0:T(1,128)S(1)} all-to-all(f32[128,1,384]{2,1,0:T(1,128)S(1)} %bitcast.20), channel_id=1, replica_groups=mesh['ta'=4,'gx'=16,'gy'=8] {'gx','gy'}, dimensions={0} | all-to-all | bytes 393216 | tf_op jit(solution)/shard_map/all_to_all | solution.py:839
  42.4 2.6 %plane_solve.2 = f32[384,128]{1,0:T(8,128)} custom-call(s32[1]{0:T(128)} %bitcast.1.own, f32[384,128]{1,0:T(8,128)S(1)} %bitcast.17, bf16[992,768]{1,0:T(8,128)(2,1)S(1)} %get-tuple-element.31.table.refs_3_), custom_call_target="tpu_custom_call" | custom-call | tf_op jit(solution)/shard_map/plane_solve/pallas_call | solution.py:801
  45.0 8.0 %all-to-all-start.1 = ((f32[128,1,384]{2,1,0:T(1,128)}), f32[128,1,384]{2,1,0:T(1,128)S(1)}, u32[]{:S(2)}, u32[]{:S(2)}) async-start(f32[128,1,384]{2,1,0:T(1,128)} %bitcast.4), calls=%async_computation.1 | async-start | bytes 393216 | tf_op jit(solution)/shard_map/all_to_all | solution.py:839
  53.0 3.3 %collective-permute-start = (f32[12,16,128]{2,1,0:T(8,128)S(1)}, f32[12,16,128]{2,1,0:T(8,128)S(1)}, u32[]{:S(2)}, u32[]{:S(2)}) collective-permute-start(f32[12,16,128]{2,1,0:T(8,128)S(1)} %get-tuple-element.34), channel_id=1, source_target_pairs={{0,8},{8,16},{16,24},{24,32},{32,40},{40,48},{48,56},{56,64},{64,7... | collective-permute-start | bytes 294920 | tf_op jit(solution)/shard_map/ppermute | solution.py:834
  56.3 1.7 %collective-permute-start.1 = (f32[12,8,128]{2,1,0:T(8,128)S(1)}, f32[12,8,128]{2,1,0:T(8,128)S(1)}, u32[]{:S(2)}, u32[]{:S(2)}) collective-permute-start(f32[12,8,128]{2,1,0:T(8,128)S(1)} %get-tuple-element.35), channel_id=1, source_target_pairs={{0,1},{1,2},{2,3},{3,4},{4,5},{5,6},{6,7},{7,0},{8,9},{9,10},{10,1... | collective-permute-start | bytes 147464 | tf_op jit(solution)/shard_map/ppermute | solution.py:834
  58.0 14.4 %all-to-all-done.1 = f32[128,1,384]{2,1,0:T(1,128)S(1)} async-done(((f32[128,1,384]{2,1,0:T(1,128)}), f32[128,1,384]{2,1,0:T(1,128)S(1)}, u32[]{:S(2)}, u32[]{:S(2)}) %all-to-all-start.1) | async-done | bytes 196640 | tf_op jit(solution)/shard_map/all_to_all | solution.py:839
  72.4 6.4 %update.1 = (f32[384,128]{1,0:T(8,128)S(1)}, f32[8,128,128]{2,1,0:T(8,128)S(1)}, f32[8,16,128]{2,1,0:T(8,128)S(1)}, f32[8,8,128]{2,1,0:T(8,128)S(1)}, f32[8,128]...) custom-call(f32[384,128]{1,0:T(8,128)S(1)} %bitcast.14, ...), custom_call_target="tpu_custom_call" | custom-call | tf_op jit(solution)/shard_map/update/pallas_call | solution.py:820
  78.8 0.0 collective-permute-done.1.refs_11_
  78.8 0.0 collective-permute-done.refs_10_
  78.8 24.5 %all_to_all.26 = f32[128,1,384]{2,1,0:T(1,128)S(1)} all-to-all(f32[128,1,384]{2,1,0:T(1,128)S(1)} %bitcast.19), channel_id=1, replica_groups=mesh['ta'=4,'gx'=16,'gy'=8] {'gx','gy'}, dimensions={0} | all-to-all | bytes 393216 | tf_op jit(solution)/shard_map/all_to_all | solution.py:839
  103.3 2.0 %plane_solve.3 = f32[384,128]{1,0:T(8,128)S(1)} custom-call(s32[1]{0:T(128)} %bitcast.1.own, f32[384,128]{1,0:T(8,128)S(1)} %bitcast.15, bf16[992,768]{1,0:T(8,128)(2,1)S(1)} %get-tuple-element.31.table.refs_3_), custom_call_target="tpu_custom_call" | custom-call | tf_op jit(solution)/shard_map/plane_solve/pallas_call | solution.py:801
  105.3 25.8 %all_to_all.27 = f32[128,1,384]{2,1,0:T(1,128)S(1)} all-to-all(f32[128,1,384]{2,1,0:T(1,128)S(1)} %bitcast.16), channel_id=1, replica_groups=mesh['ta'=4,'gx'=16,'gy'=8] {'gx','gy'}, dimensions={0} | all-to-all | bytes 393216 | tf_op jit(solution)/shard_map/all_to_all | solution.py:839
  131.1 6.9 %last_update.1 = (f32[8,8,16,128]{3,2,1,0:T(8,128)}, f32[2,2,3,8,16,128]{5,4,3,2,1,0:T(8,128)}, f32[128,128]{1,0:T(8,128)S(1)}) custom-call(f32[384,128]{1,0:T(8,128)S(1)} %bitcast.18, f32[8,128,128]{2,1,0:T(8,128)S(1)} %get-tuple-element.37.refs_1_, f32[54,8,16,128]{3,2,1,0:T(8,128)} %bitcast.24, bf16[992,768]{1,0:T(8,128)(2,1)S(1)} %get-tuple-element.31.table.refs_3_, ...), custom_call_target="tpu_custom_call" | custom-call | tf_op jit(solution)/shard_map/last_update/pallas_call | solution.py:820
  138.0 22.7 %all_to_all.28 = f32[128,1,128]{2,1,0:T(1,128)S(1)} all-to-all(f32[128,1,128]{2,1,0:T(1,128)S(1)} %bitcast.21), channel_id=1, replica_groups=mesh['ta'=4,'gx'=16,'gy'=8] {'gx','gy'}, dimensions={0} | all-to-all | bytes 131072 | tf_op jit(solution)/shard_map/all_to_all | solution.py:839
  160.7 0.5 slice_reduce_fusion
Async XLA Ops:
  45.0 27.4 %all-to-all-start.1 = ((f32[128,1,384]{2,1,0:T(1,128)}), f32[128,1,384]{2,1,0:T(1,128)S(1)}, u32[]{:S(2)}, u32[]{:S(2)}) async-start(f32[128,1,384]{2,1,0:T(1,128)} %bitcast.4), calls=%async_computation.1 | async-start | bytes 393216 | tf_op jit(solution)/shard_map/all_to_all | solution.py:839
  53.0 25.8 %collective-permute-start = (f32[12,16,128]{2,1,0:T(8,128)S(1)}, f32[12,16,128]{2,1,0:T(8,128)S(1)}, u32[]{:S(2)}, u32[]{:S(2)}) collective-permute-start(f32[12,16,128]{2,1,0:T(8,128)S(1)} %get-tuple-element.34), channel_id=1, source_target_pairs={{0,8},{8,16},{16,24},{24,32},{32,40},{40,48},{48,56},{56,64},{64,7... | collective-permute-start | bytes 294920 | tf_op jit(solution)/shard_map/ppermute | solution.py:834
  56.3 22.5 %collective-permute-start.1 = (f32[12,8,128]{2,1,0:T(8,128)S(1)}, f32[12,8,128]{2,1,0:T(8,128)S(1)}, u32[]{:S(2)}, u32[]{:S(2)}) collective-permute-start(f32[12,8,128]{2,1,0:T(8,128)S(1)} %get-tuple-element.35), channel_id=1, source_target_pairs={{0,1},{1,2},{2,3},{3,4},{4,5},{5,6},{6,7},{7,0},{8,9},{9,10},{10,1... | collective-permute-start | bytes 147464 | tf_op jit(solution)/shard_map/ppermute | solution.py:834
